TPU v7x, 32 devices: a whole 2x2x4 slice. The times are simulated.
32 devices in a mesh: dp: 8 (over y, x, core), mp: 4 (over z).
Axes of the slice: x: 2, y: 2, z: 4, core: 2. Of those that a mesh axis runs over, the one named last changes fastest.
Arguments:
- clips: bfloat16 [1024, 768], P('dp', 'mp')
- captions: bfloat16 [1024, 768], P('dp', 'mp')
- video_id: int32 [1024], replicated, may hold values from 0 to 63, never falling along the last dimension, each value on 1 to 128 neighbouring positions
- logit_scale: float32 [], replicated, may hold values from 110 to 160
Outputs:
- d_clips: float32 [1024, 768], P(('dp', 'mp'))
- d_captions: float32 [1024, 768], P(('dp', 'mp'))
Inputs may be any that keep to these rules, and one draw needn't show every extreme that they name: `video_id`: video ids never fall along the rows; each video covers 1 to 128 consecutive rows.
All inputs are finite; a program needn't handle non-finite values.
Results may differ from a plain program's by a relative error of at most 0.0095.
Values may be sent and summed in bfloat16 or wider, within the bound.
No kernel may reach another device: no remote copies, remote signals or barrier semaphores. Data moves between devices by JAX's collectives and lax.ppermute only.
A program may use at most 64 MiB of HBM per device.

v0:
```python
import jax
import jax.numpy as jnp
from jax import lax
from jax.sharding import PartitionSpec as P

epsilon = 1e-06
negative_fill = -1e30


def extended(value, sides, width):
    for axis, dim in sides:
        size, length = (lax.axis_size(axis), value.shape[dim])
        up = [(i, (i + 1) % size) for i in range(size - 1)]
        down = [(j, i) for i, j in up]
        last = lax.slice_in_dim(value, length - width, length, axis=dim)
        leading = lax.slice_in_dim(value, 0, width, axis=dim)
        before = lax.ppermute(last, axis, up)
        after = lax.ppermute(leading, axis, down)
        value = jnp.concatenate([before, value, after], axis=dim)
    return value


def shifted(block, axis, distance):
    devices = range(lax.axis_size(axis))
    route = [((i - distance) % len(devices), i) for i in devices]
    return lax.ppermute(block, axis, route)


def combined_all(value, axis, combine):
    everything = jax.tree.map(lambda part: lax.all_gather(part, axis), value)
    leading = jax.tree.map(lambda part: part[0], everything)

    def lap(k, so_far):
        return combine(so_far, jax.tree.map(lambda part: part[k], everything))

    return lax.fori_loop(1, lax.axis_size(axis), lap, leading)


def unit_rows(values):
    widened = values.astype(jnp.float32)
    length = jnp.sqrt(jnp.sum(widened * widened, axis=-1) + epsilon)
    return (widened / length[:, None], length)


def tile_scores(caption_panel, clip_unit, logit_scale):
    return logit_scale * lax.dot_general(
        caption_panel, clip_unit, (((1,), (1,)), ((), ())), preferred_element_type=jnp.float32
    )


def forward_update(running, scores, allowed):
    row_max, row_sum, col_max, col_sum = running
    masked = jnp.where(allowed, scores, negative_fill)
    new_row = jnp.maximum(row_max, jnp.max(masked, axis=0))
    new_col = jnp.maximum(col_max, jnp.max(masked, axis=1))
    row_terms = jnp.exp(scores - new_row[None, :])
    col_terms = jnp.exp(scores - new_col[:, None])
    row_terms = jnp.where(allowed, row_terms, 0.0)
    col_terms = jnp.where(allowed, col_terms, 0.0)
    row_sum = row_sum * jnp.exp(row_max - new_row) + jnp.sum(row_terms, axis=0)
    col_sum = col_sum * jnp.exp(col_max - new_col) + jnp.sum(col_terms, axis=1)
    return (new_row, row_sum, new_col, col_sum)


def backward_update(
    accumulated, scores, allowed, same_video, caption_panel, clip_unit, row_lse, col_lse
):
    clip_acc, pool_acc, cap_acc = accumulated
    weights = 0.5 * (jnp.exp(scores - row_lse[None, :]) + jnp.exp(scores - col_lse[:, None]))
    weights = jnp.where(allowed, weights, 0.0)
    weights = weights.astype(jnp.bfloat16)
    clip_acc = clip_acc + lax.dot_general(
        weights, caption_panel, (((0,), (0,)), ((), ())), preferred_element_type=jnp.float32
    )
    cap_acc = cap_acc + jnp.dot(weights, clip_unit, preferred_element_type=jnp.float32)
    pool_acc = pool_acc + lax.dot_general(
        same_video.astype(jnp.bfloat16),
        caption_panel,
        (((0,), (0,)), ((), ())),
        preferred_element_type=jnp.float32,
    )
    return (clip_acc, pool_acc, cap_acc)


def join_stats(left_pair, right_pair):
    top_value = jnp.maximum(left_pair[0], right_pair[0])
    return (
        top_value,
        left_pair[1] * jnp.exp(left_pair[0] - top_value)
        + right_pair[1] * jnp.exp(right_pair[0] - top_value),
    )


def body(clips, captions, video_id, logit_scale):
    dp_count = lax.axis_size("dp")
    mp_count = lax.axis_size("mp")
    row_count = clips.shape[0]
    sub_rows = row_count // mp_count
    feature_width = clips.shape[1] * mp_count
    dp_index = lax.axis_index("dp")
    mp_index = lax.axis_index("mp")
    full_clips = lax.all_gather(clips, "mp", axis=1, tiled=True)
    home_captions = lax.all_to_all(captions, "mp", split_axis=0, concat_axis=1, tiled=True)
    clip_float, clip_length = unit_rows(full_clips)
    clip_unit = clip_float.astype(jnp.bfloat16)
    cap_float, cap_length = unit_rows(home_captions)
    cap_unit = cap_float.astype(jnp.bfloat16)
    all_rows = video_id.shape[0]
    first_clip = dp_index * row_count
    clip_positions = first_clip + jnp.arange(row_count, dtype=jnp.int32)
    clip_videos = lax.dynamic_slice_in_dim(video_id, first_clip, row_count, 0)
    same_block = (clip_videos[:, None] == clip_videos[None, :]).astype(jnp.bfloat16)
    local_pool = jnp.dot(same_block, clip_unit, preferred_element_type=jnp.float32)
    edge_sums = jnp.stack([local_pool[0], local_pool[row_count - 1]])
    beside = extended(edge_sums, (("dp", 0),), 1)
    left_video = lax.dynamic_index_in_dim(
        video_id, jnp.maximum(first_clip - 1, 0), 0, keepdims=False
    )
    right_video = lax.dynamic_index_in_dim(
        video_id, jnp.minimum(first_clip + row_count, all_rows - 1), 0, keepdims=False
    )
    from_left = ((clip_videos == left_video) & (dp_index > 0)).astype(jnp.float32)
    from_right = ((clip_videos == right_video) & (dp_index < dp_count - 1)).astype(jnp.float32)
    pooled = (
        local_pool
        + from_left[:, None] * beside[0][None, :]
        + from_right[:, None] * beside[3][None, :]
    )
    pool_length = jnp.sqrt(jnp.sum(pooled * pooled, axis=-1) + epsilon)
    pool_unit = pooled / pool_length[:, None]

    def tile_masks(first_row):
        panel_videos = lax.dynamic_slice_in_dim(video_id, first_row, sub_rows, 0)
        panel_positions = first_row + jnp.arange(sub_rows, dtype=jnp.int32)
        same_video = panel_videos[:, None] == clip_videos[None, :]
        allowed = jnp.logical_not(same_video) | (
            panel_positions[:, None] == clip_positions[None, :]
        )
        return (allowed, same_video)

    def source_first(turn_index):
        source_index = (dp_index - turn_index) % dp_count
        return (source_index, source_index * row_count + mp_index * sub_rows)

    def forward_step(turn_index, caption_panel, running):
        source_index, first_row = source_first(turn_index)
        scores = tile_scores(caption_panel, clip_unit, logit_scale)
        allowed, same_video = tile_masks(first_row)
        return forward_update(running, scores, allowed)

    def send_panel(caption_panel):
        return shifted(caption_panel, "dp", 1)

    def send_stats(stat_pair):
        return shifted(stat_pair, "dp", 1)

    def store_panel(panel_store, caption_panel, turn_index):
        return lax.dynamic_update_index_in_dim(panel_store, caption_panel, turn_index, 0)

    panel_store = jnp.zeros((dp_count, sub_rows, feature_width), jnp.bfloat16)
    running = (
        jnp.full((row_count,), negative_fill, jnp.float32),
        jnp.zeros((row_count,), jnp.float32),
        jnp.full((sub_rows,), negative_fill, jnp.float32),
        jnp.zeros((sub_rows,), jnp.float32),
    )

    def forward_turn(turn_index, state_tuple):
        caption_panel, current, stored = state_tuple
        current = forward_step(turn_index, caption_panel, current)
        stored = store_panel(stored, caption_panel, turn_index)
        col_pair = send_stats((current[2], current[3]))
        return (
            send_panel(caption_panel),
            (current[0], current[1], col_pair[0], col_pair[1]),
            stored,
        )

    caption_panel, running, panel_store = lax.fori_loop(
        0, dp_count - 1, forward_turn, (cap_unit, running, panel_store)
    )
    running = forward_step(dp_count - 1, caption_panel, running)
    panel_store = store_panel(panel_store, caption_panel, dp_count - 1)
    col_max, col_sum = send_stats((running[2], running[3]))
    row_max, row_sum = combined_all((running[0], running[1]), "mp", join_stats)
    row_lse = row_max + jnp.log(row_sum)
    col_lse = col_max + jnp.log(col_sum)

    def backward_step(turn_index, caption_panel, col_lse_now, accumulated):
        source_index, first_row = source_first(turn_index)
        scores = tile_scores(caption_panel, clip_unit, logit_scale)
        allowed, same_video = tile_masks(first_row)
        return backward_update(
            accumulated, scores, allowed, same_video, caption_panel, clip_unit, row_lse, col_lse_now
        )

    def send_sums(sum_pair):
        return shifted(sum_pair, "dp", 1)

    def panel_at(turn_index):
        return lax.dynamic_index_in_dim(panel_store, turn_index, 0, keepdims=False)

    def backward_turn(turn_index, state_tuple):
        caption_panel, sum_pair, clip_acc, pool_acc = state_tuple
        current_panel = panel_at(turn_index)
        clip_acc, pool_acc, cap_acc = backward_step(
            turn_index, current_panel, sum_pair[0], (clip_acc, pool_acc, sum_pair[1])
        )
        sum_pair = send_sums((sum_pair[0], cap_acc))
        return (caption_panel, sum_pair, clip_acc, pool_acc)

    zero_clips = jnp.zeros((row_count, feature_width), jnp.float32)
    start_state = (
        cap_unit,
        (col_lse, jnp.zeros((sub_rows, feature_width), jnp.float32)),
        zero_clips,
        zero_clips,
    )
    caption_panel, sum_pair, clip_acc, pool_acc = lax.fori_loop(
        0, dp_count - 1, backward_turn, start_state
    )
    current_panel = panel_at(dp_count - 1)
    clip_acc, pool_acc, cap_acc = backward_step(
        dp_count - 1, current_panel, sum_pair[0], (clip_acc, pool_acc, sum_pair[1])
    )
    sum_pair = send_sums((sum_pair[0], cap_acc))
    cap_acc = sum_pair[1]
    projected = pool_acc - pool_unit * jnp.sum(pool_unit * pool_acc, axis=-1, keepdims=True)
    partial_grad = logit_scale * clip_acc - 0.5 * logit_scale * projected / pool_length[:, None]
    own_first = mp_index * sub_rows
    own_rows = lax.dynamic_slice_in_dim(
        partial_grad, own_first, sub_rows, 0
    ) - 0.5 * logit_scale * cap_unit.astype(jnp.float32)
    partial_grad = lax.dynamic_update_slice_in_dim(partial_grad, own_rows, own_first, 0)
    clip_grad_unit = lax.psum_scatter(
        partial_grad.astype(jnp.bfloat16), "mp", scatter_dimension=0, tiled=True
    ).astype(jnp.float32)
    sub_float = lax.dynamic_slice_in_dim(clip_float, own_first, sub_rows, 0)
    sub_length = lax.dynamic_slice_in_dim(clip_length, own_first, sub_rows, 0)
    sub_clip_unit = lax.dynamic_slice_in_dim(clip_unit, own_first, sub_rows, 0).astype(jnp.float32)
    sub_pool_unit = lax.dynamic_slice_in_dim(pool_unit, own_first, sub_rows, 0)
    d_clips = (
        clip_grad_unit - sub_float * jnp.sum(sub_float * clip_grad_unit, axis=-1, keepdims=True)
    ) / sub_length[:, None]
    cap_grad_unit = (
        logit_scale * cap_acc
        - 0.5 * logit_scale * sub_clip_unit
        - 0.5 * logit_scale * sub_pool_unit
    )
    d_captions = (
        cap_grad_unit - cap_float * jnp.sum(cap_float * cap_grad_unit, axis=-1, keepdims=True)
    ) / cap_length[:, None]
    return (d_clips, d_captions)


def solution(mesh):
    in_specs = (P("dp", "mp"), P("dp", "mp"), P(), P())
    out_specs = (P(("dp", "mp"), None), P(("dp", "mp"), None))
    return jax.shard_map(body, mesh=mesh, in_specs=in_specs, out_specs=out_specs, check_vma=False)
```

profile of v0, /device:TPU:0, one launch (start us, length us, event | category | flops | bytes accessed | tf_op | source)
XLA Modules:
  0.0 180.4 jit_solution(5815430619514614368)
XLA Ops:
  7.2 1.5 copy.11
  8.7 6.4 %all-to-all-start = ((bf16[4,32,192]{2,1,0:T(8,128)(2,1)}), bf16[4,32,192]{2,1,0:T(8,128)(2,1)S(1)}, u32[]{:S(2)}, u32[]{:S(2)}) async-start(bf16[4,32,192]{2,1,0:T(8,128)(2,1)} %bitcast.2), calls=%async_computation | async-start | bytes 131072 | tf_op jit(solution)/shard_map/all_to_all | solution.py:103
  15.2 14.3 %all_gather.15 = bf16[128,768]{0,1:T(8,128)(2,1)S(1)} all-gather(bf16[128,192]{0,1:T(8,128)(2,1)S(1)} %copy-done.1), channel_id=1, replica_groups=mesh['dp'=8,'mp'=4] {'mp'}, dimensions={1}, use_global_device_ids=true | all-gather | bytes 245760 | tf_op jit(solution)/shard_map/all_gather | solution.py:102
  31.9 1.3 collective-permute-start.7
  33.2 1.3 collective-permute-start.8
  36.0 2.0 %collective-permute-done.8 = f32[1,768]{1,0:T(1,128)S(1)} collective-permute-done((f32[1,768]{1,0:T(1,128)S(1)}, f32[1,768]{1,0:T(1,128)S(1)}, u32[]{:S(2)}, u32[]{:S(2)}) %collective-permute-start.8) | collective-permute-done | bytes 3104 | tf_op jit(solution)/shard_map/ppermute | solution.py:18
  38.8 45.5 %while.66 = (s32[]{:T(128)}, bf16[32,768]{1,0:T(8,128)(2,1)S(1)}, f32[128]{0:T(128)S(1)}, f32[128]{0:T(128)S(1)}, f32[32]{0:T(128)S(1)}, /*index=5*/f32[32]{0:T(...) while((s32[]{:T(128)}, bf16[32,768]{1,0:T(8,128)(2,1)S(1)}, ...), condition=%wide.region_7.8_spmd.clone, body=%wide.region_2.7_spmd.clone.sunk | while | flops 6366068 | bytes 685055 | solution.py:179
  38.8 2.4 %collective-permute-start = (bf16[32,768]{1,0:T(8,128)(2,1)S(1)}, bf16[32,768]{1,0:T(8,128)(2,1)S(1)}, u32[]{:S(2)}, u32[]{:S(2)}) collective-permute-start(bf16[32,768]{1,0:T(8,128)(2,1)S(1)} %copy.23), channel_id=1, source_target_pairs={{28,0},{0,4},{4,8},{8,12},{12,16},{16,20},{20,24},{24,28},{29,1},{... | collective-permute-start | bytes 147464 | tf_op jit(solution)/shard_map/while/body/eval_jaxpr/ppermute | solution.py:26
  41.3 0.9 select_reduce_fusion.10
  42.8 2.3 %collective-permute-start.2 = (f32[32]{0:T(128)S(1)}, f32[32]{0:T(128)S(1)}, u32[]{:S(2)}, u32[]{:S(2)}) collective-permute-start(f32[32]{0:T(128)S(1)} %multiply_add_fusion.4), channel_id=1, source_target_pairs={{28,0},{0,4},{4,8},{8,12},{12,16},{16,20},{20,24},{24,28},{29,1},{... | collective-permute-start | bytes 392 | tf_op jit(solution)/shard_map/while/body/eval_jaxpr/ppermute | solution.py:26
  45.1 1.1 collective-permute-done.1
  46.9 0.9 select_reduce_fusion.10
  47.9 1.6 collective-permute-start.1
  49.8 2.0 %collective-permute-done.1 = f32[32]{0:T(128)S(1)} collective-permute-done((f32[32]{0:T(128)S(1)}, f32[32]{0:T(128)S(1)}, u32[]{:S(2)}, u32[]{:S(2)}) %collective-permute-start.1) | collective-permute-done | bytes 160 | tf_op jit(solution)/shard_map/while/body/eval_jaxpr/ppermute | solution.py:26
  51.8 1.8 collective-permute-done.2
  53.8 0.9 select_reduce_fusion.10
  54.7 0.7 collective-permute-start.1
  55.8 2.9 %collective-permute-done.1 = f32[32]{0:T(128)S(1)} collective-permute-done((f32[32]{0:T(128)S(1)}, f32[32]{0:T(128)S(1)}, u32[]{:S(2)}, u32[]{:S(2)}) %collective-permute-start.1) | collective-permute-done | bytes 160 | tf_op jit(solution)/shard_map/while/body/eval_jaxpr/ppermute | solution.py:26
  58.7 0.9 collective-permute-done.2
  59.8 0.9 select_reduce_fusion.10
  61.1 3.5 %collective-permute-done.1 = f32[32]{0:T(128)S(1)} collective-permute-done((f32[32]{0:T(128)S(1)}, f32[32]{0:T(128)S(1)}, u32[]{:S(2)}, u32[]{:S(2)}) %collective-permute-start.1) | collective-permute-done | bytes 160 | tf_op jit(solution)/shard_map/while/body/eval_jaxpr/ppermute | solution.py:26
  65.1 0.9 select_reduce_fusion.10
  66.1 1.2 collective-permute-start.1
  67.6 2.4 %collective-permute-done.1 = f32[32]{0:T(128)S(1)} collective-permute-done((f32[32]{0:T(128)S(1)}, f32[32]{0:T(128)S(1)}, u32[]{:S(2)}, u32[]{:S(2)}) %collective-permute-start.1) | collective-permute-done | bytes 160 | tf_op jit(solution)/shard_map/while/body/eval_jaxpr/ppermute | solution.py:26
  70.0 1.4 collective-permute-done.2
  71.6 0.9 select_reduce_fusion.10
  72.6 1.6 collective-permute-start.1
  74.5 2.0 %collective-permute-done.1 = f32[32]{0:T(128)S(1)} collective-permute-done((f32[32]{0:T(128)S(1)}, f32[32]{0:T(128)S(1)}, u32[]{:S(2)}, u32[]{:S(2)}) %collective-permute-start.1) | collective-permute-done | bytes 160 | tf_op jit(solution)/shard_map/while/body/eval_jaxpr/ppermute | solution.py:26
  76.5 1.8 %collective-permute-done.2 = f32[32]{0:T(128)S(1)} collective-permute-done((f32[32]{0:T(128)S(1)}, f32[32]{0:T(128)S(1)}, u32[]{:S(2)}, u32[]{:S(2)}) %collective-permute-start.2) | collective-permute-done | bytes 160 | tf_op jit(solution)/shard_map/while/body/eval_jaxpr/ppermute | solution.py:26
  78.5 0.9 select_reduce_fusion.10
  79.4 0.7 collective-permute-start.1
  80.5 2.9 %collective-permute-done.1 = f32[32]{0:T(128)S(1)} collective-permute-done((f32[32]{0:T(128)S(1)}, f32[32]{0:T(128)S(1)}, u32[]{:S(2)}, u32[]{:S(2)}) %collective-permute-start.1) | collective-permute-done | bytes 160 | tf_op jit(solution)/shard_map/while/body/eval_jaxpr/ppermute | solution.py:26
  83.4 0.9 collective-permute-done.2
  85.2 10.9 %all-gather.3 = f32[4,1,128]{2,1,0:T(1,128)S(1)} all-gather(f32[1,1,128]{2,1,0:T(1,128)S(1)} %add_bitcast_fusion), channel_id=3, replica_groups=mesh['dp'=8,'mp'=4] {'mp'}, dimensions={0}, use_global_device_ids=true | all-gather | bytes 2560 | tf_op jit(solution)/shard_map/all_gather | solution.py:30
  96.1 7.5 %all-gather.2 = f32[4,1,128]{2,1,0:T(1,128)S(1)} all-gather(f32[1,1,128]{2,1,0:T(1,128)S(1)} %bitcast.75), channel_id=2, replica_groups=mesh['dp'=8,'mp'=4] {'mp'}, dimensions={0}, use_global_device_ids=true | all-gather | bytes 2560 | tf_op jit(solution)/shard_map/all_gather | solution.py:30
  103.9 3.8 %collective-permute-done.6 = f32[32]{0:T(128)S(1)} collective-permute-done((f32[32]{0:T(128)S(1)}, f32[32]{0:T(128)S(1)}, u32[]{:S(2)}, u32[]{:S(2)}) %collective-permute-start.6) | collective-permute-done | bytes 160 | tf_op jit(solution)/shard_map/ppermute | solution.py:26
  107.7 42.8 %while.67 = (s32[]{:T(128)}, f32[32]{0:T(128)S(1)}, f32[32,768]{1,0:T(8,128)S(1)}, f32[128,768]{1,0:T(8,128)S(1)}, f32[128,768]{1,0:T(8,128)S(1)}, /*index=5*/s3...) while((s32[]{:T(128)}, f32[32]{0:T(128)S(1)}, ...), condition=%wide.region_15.16_spmd.clone, body=%wide.region_14.15_spmd.clone.sunk | while | flops 25632948 | bytes 2734175 | solution.py:219
  107.9 0.8 select_convert_fusion.5
  109.7 2.0 %collective-permute-done.3 = f32[32]{0:T(128)S(1)} collective-permute-done((f32[32]{0:T(128)S(1)}, f32[32]{0:T(128)S(1)}, u32[]{:S(2)}, u32[]{:S(2)}) %collective-permute-start.3) | collective-permute-done | bytes 160 | tf_op jit(solution)/shard_map/while/body/eval_jaxpr/ppermute | solution.py:26
  111.7 2.3 %collective-permute-done.4 = f32[32,768]{1,0:T(8,128)S(1)} collective-permute-done((f32[32,768]{1,0:T(8,128)S(1)}, f32[32,768]{1,0:T(8,128)S(1)}, u32[]{:S(2)}, u32[]{:S(2)}) %collective-permute-start.4) | collective-permute-done | bytes 98336 | tf_op jit(solution)/shard_map/while/body/eval_jaxpr/ppermute | solution.py:26
  114.0 0.8 select_convert_fusion.5
  115.8 2.0 %collective-permute-done.3 = f32[32]{0:T(128)S(1)} collective-permute-done((f32[32]{0:T(128)S(1)}, f32[32]{0:T(128)S(1)}, u32[]{:S(2)}, u32[]{:S(2)}) %collective-permute-start.3) | collective-permute-done | bytes 160 | tf_op jit(solution)/shard_map/while/body/eval_jaxpr/ppermute | solution.py:26
  117.8 2.2 %collective-permute-done.4 = f32[32,768]{1,0:T(8,128)S(1)} collective-permute-done((f32[32,768]{1,0:T(8,128)S(1)}, f32[32,768]{1,0:T(8,128)S(1)}, u32[]{:S(2)}, u32[]{:S(2)}) %collective-permute-start.4) | collective-permute-done | bytes 98336 | tf_op jit(solution)/shard_map/while/body/eval_jaxpr/ppermute | solution.py:26
  120.1 0.8 select_convert_fusion.5
  121.9 2.0 %collective-permute-done.3 = f32[32]{0:T(128)S(1)} collective-permute-done((f32[32]{0:T(128)S(1)}, f32[32]{0:T(128)S(1)}, u32[]{:S(2)}, u32[]{:S(2)}) %collective-permute-start.3) | collective-permute-done | bytes 160 | tf_op jit(solution)/shard_map/while/body/eval_jaxpr/ppermute | solution.py:26
  123.9 2.2 %collective-permute-done.4 = f32[32,768]{1,0:T(8,128)S(1)} collective-permute-done((f32[32,768]{1,0:T(8,128)S(1)}, f32[32,768]{1,0:T(8,128)S(1)}, u32[]{:S(2)}, u32[]{:S(2)}) %collective-permute-start.4) | collective-permute-done | bytes 98336 | tf_op jit(solution)/shard_map/while/body/eval_jaxpr/ppermute | solution.py:26
  126.2 0.8 select_convert_fusion.5
  128.0 2.0 %collective-permute-done.3 = f32[32]{0:T(128)S(1)} collective-permute-done((f32[32]{0:T(128)S(1)}, f32[32]{0:T(128)S(1)}, u32[]{:S(2)}, u32[]{:S(2)}) %collective-permute-start.3) | collective-permute-done | bytes 160 | tf_op jit(solution)/shard_map/while/body/eval_jaxpr/ppermute | solution.py:26
  130.0 2.2 %collective-permute-done.4 = f32[32,768]{1,0:T(8,128)S(1)} collective-permute-done((f32[32,768]{1,0:T(8,128)S(1)}, f32[32,768]{1,0:T(8,128)S(1)}, u32[]{:S(2)}, u32[]{:S(2)}) %collective-permute-start.4) | collective-permute-done | bytes 98336 | tf_op jit(solution)/shard_map/while/body/eval_jaxpr/ppermute | solution.py:26
  132.4 0.8 select_convert_fusion.5
  134.1 2.0 %collective-permute-done.3 = f32[32]{0:T(128)S(1)} collective-permute-done((f32[32]{0:T(128)S(1)}, f32[32]{0:T(128)S(1)}, u32[]{:S(2)}, u32[]{:S(2)}) %collective-permute-start.3) | collective-permute-done | bytes 160 | tf_op jit(solution)/shard_map/while/body/eval_jaxpr/ppermute | solution.py:26
  136.1 2.2 %collective-permute-done.4 = f32[32,768]{1,0:T(8,128)S(1)} collective-permute-done((f32[32,768]{1,0:T(8,128)S(1)}, f32[32,768]{1,0:T(8,128)S(1)}, u32[]{:S(2)}, u32[]{:S(2)}) %collective-permute-start.4) | collective-permute-done | bytes 98336 | tf_op jit(solution)/shard_map/while/body/eval_jaxpr/ppermute | solution.py:26
  138.5 0.8 select_convert_fusion.5
  140.2 2.0 %collective-permute-done.3 = f32[32]{0:T(128)S(1)} collective-permute-done((f32[32]{0:T(128)S(1)}, f32[32]{0:T(128)S(1)}, u32[]{:S(2)}, u32[]{:S(2)}) %collective-permute-start.3) | collective-permute-done | bytes 160 | tf_op jit(solution)/shard_map/while/body/eval_jaxpr/ppermute | solution.py:26
  142.2 2.2 %collective-permute-done.4 = f32[32,768]{1,0:T(8,128)S(1)} collective-permute-done((f32[32,768]{1,0:T(8,128)S(1)}, f32[32,768]{1,0:T(8,128)S(1)}, u32[]{:S(2)}, u32[]{:S(2)}) %collective-permute-start.4) | collective-permute-done | bytes 98336 | tf_op jit(solution)/shard_map/while/body/eval_jaxpr/ppermute | solution.py:26
  144.6 0.8 select_convert_fusion.5
  146.3 2.0 %collective-permute-done.3 = f32[32]{0:T(128)S(1)} collective-permute-done((f32[32]{0:T(128)S(1)}, f32[32]{0:T(128)S(1)}, u32[]{:S(2)}, u32[]{:S(2)}) %collective-permute-start.3) | collective-permute-done | bytes 160 | tf_op jit(solution)/shard_map/while/body/eval_jaxpr/ppermute | solution.py:26
  148.3 2.2 %collective-permute-done.4 = f32[32,768]{1,0:T(8,128)S(1)} collective-permute-done((f32[32,768]{1,0:T(8,128)S(1)}, f32[32,768]{1,0:T(8,128)S(1)}, u32[]{:S(2)}, u32[]{:S(2)}) %collective-permute-start.4) | collective-permute-done | bytes 98336 | tf_op jit(solution)/shard_map/while/body/eval_jaxpr/ppermute | solution.py:26
  151.7 0.7 convert_element_type.69
  152.5 3.6 %collective-permute-done.9 = f32[32,768]{1,0:T(8,128)S(1)} collective-permute-done((f32[32,768]{1,0:T(8,128)S(1)}, f32[32,768]{1,0:T(8,128)S(1)}, u32[]{:S(2)}, u32[]{:S(2)}) %collective-permute-start.9) | collective-permute-done | bytes 98336 | tf_op jit(solution)/shard_map/ppermute | solution.py:26
  156.3 0.7 subtract_divide_fusion
  157.0 14.8 %reduce-scatter.2.cloned.1.call-done = bf16[32,768]{1,0:T(8,128)(2,1)} async-done(((bf16[128,768]{1,0:T(8,128)(2,1)}), bf16[32,768]{1,0:T(8,128)(2,1)}) %reduce-scatter.2.cloned.1.call-update) | async-done | bytes 49168 | tf_op jit(solution)/shard_map/reduce_scatter | solution.py:235
  171.8 1.0 fusion.27
  172.8 0.7 fusion.28
  (238 shorter events, 17.6 us)
Async XLA Ops:
  8.7 6.5 %copy-start.1 = (bf16[128,192]{0,1:T(8,128)(2,1)S(1)}, bf16[128,192]{0,1:T(8,128)(2,1)}, u32[]{:S(2)}) copy-start(bf16[128,192]{0,1:T(8,128)(2,1)} %param.10) | copy-start | bytes 147460
  8.7 29.5 %all-to-all-start = ((bf16[4,32,192]{2,1,0:T(8,128)(2,1)}), bf16[4,32,192]{2,1,0:T(8,128)(2,1)S(1)}, u32[]{:S(2)}, u32[]{:S(2)}) async-start(bf16[4,32,192]{2,1,0:T(8,128)(2,1)} %bitcast.2), calls=%async_computation | async-start | bytes 131072 | tf_op jit(solution)/shard_map/all_to_all | solution.py:103
  15.1 156.7 %reduce-scatter.2.cloned.1.call-start = ((), (), s32[]{:S(2)}) async-start(), calls=%async_computation.2 | async-start | bytes 245760 | tf_op jit(solution)/shard_map/reduce_scatter | solution.py:235
  29.7 0.7 copy-start.2
  31.9 4.1 %collective-permute-start.7 = (f32[1,768]{1,0:T(1,128)S(1)}, f32[1,768]{1,0:T(1,128)S(1)}, u32[]{:S(2)}, u32[]{:S(2)}) collective-permute-start(f32[1,768]{1,0:T(1,128)S(1)} %get-tuple-element.999), channel_id=1, source_target_pairs={{0,4},{4,8},{8,12},{12,16},{16,20},{20,24},{24,28},{1,5},{5,9},{9,... | collective-permute-start | bytes 9224 | tf_op jit(solution)/shard_map/ppermute | solution.py:17
  33.2 4.8 %collective-permute-start.8 = (f32[1,768]{1,0:T(1,128)S(1)}, f32[1,768]{1,0:T(1,128)S(1)}, u32[]{:S(2)}, u32[]{:S(2)}) collective-permute-start(f32[1,768]{1,0:T(1,128)S(1)} %get-tuple-element.1000), channel_id=1, source_target_pairs={{4,0},{8,4},{12,8},{16,12},{20,16},{24,20},{28,24},{5,1},{9,5},{13... | collective-permute-start | bytes 9224 | tf_op jit(solution)/shard_map/ppermute | solution.py:18
  38.8 7.9 %collective-permute-start = (bf16[32,768]{1,0:T(8,128)(2,1)S(1)}, bf16[32,768]{1,0:T(8,128)(2,1)S(1)}, u32[]{:S(2)}, u32[]{:S(2)}) collective-permute-start(bf16[32,768]{1,0:T(8,128)(2,1)S(1)} %copy.23), channel_id=1, source_target_pairs={{28,0},{0,4},{4,8},{8,12},{12,16},{16,20},{20,24},{24,28},{29,1},{... | collective-permute-start | bytes 147464 | tf_op jit(solution)/shard_map/while/body/eval_jaxpr/ppermute | solution.py:26
  42.2 3.9 %collective-permute-start.1 = (f32[32]{0:T(128)S(1)}, f32[32]{0:T(128)S(1)}, u32[]{:S(2)}, u32[]{:S(2)}) collective-permute-start(f32[32]{0:T(128)S(1)} %max.50), channel_id=1, source_target_pairs={{28,0},{0,4},{4,8},{8,12},{12,16},{16,20},{20,24},{24,28},{29,1},{... | collective-permute-start | bytes 392 | tf_op jit(solution)/shard_map/while/body/eval_jaxpr/ppermute | solution.py:26
  42.8 3.9 %collective-permute-start.2 = (f32[32]{0:T(128)S(1)}, f32[32]{0:T(128)S(1)}, u32[]{:S(2)}, u32[]{:S(2)}) collective-permute-start(f32[32]{0:T(128)S(1)} %multiply_add_fusion.4), channel_id=1, source_target_pairs={{28,0},{0,4},{4,8},{8,12},{12,16},{16,20},{20,24},{24,28},{29,1},{... | collective-permute-start | bytes 392 | tf_op jit(solution)/shard_map/while/body/eval_jaxpr/ppermute | solution.py:26
  46.7 6.9 %collective-permute-start = (bf16[32,768]{1,0:T(8,128)(2,1)S(1)}, bf16[32,768]{1,0:T(8,128)(2,1)S(1)}, u32[]{:S(2)}, u32[]{:S(2)}) collective-permute-start(bf16[32,768]{1,0:T(8,128)(2,1)S(1)} %copy.23), channel_id=1, source_target_pairs={{28,0},{0,4},{4,8},{8,12},{12,16},{16,20},{20,24},{24,28},{29,1},{... | collective-permute-start | bytes 147464 | tf_op jit(solution)/shard_map/while/body/eval_jaxpr/ppermute | solution.py:26
  47.9 3.9 %collective-permute-start.1 = (f32[32]{0:T(128)S(1)}, f32[32]{0:T(128)S(1)}, u32[]{:S(2)}, u32[]{:S(2)}) collective-permute-start(f32[32]{0:T(128)S(1)} %max.50), channel_id=1, source_target_pairs={{28,0},{0,4},{4,8},{8,12},{12,16},{16,20},{20,24},{24,28},{29,1},{... | collective-permute-start | bytes 392 | tf_op jit(solution)/shard_map/while/body/eval_jaxpr/ppermute | solution.py:26
  49.7 3.9 %collective-permute-start.2 = (f32[32]{0:T(128)S(1)}, f32[32]{0:T(128)S(1)}, u32[]{:S(2)}, u32[]{:S(2)}) collective-permute-start(f32[32]{0:T(128)S(1)} %multiply_add_fusion.4), channel_id=1, source_target_pairs={{28,0},{0,4},{4,8},{8,12},{12,16},{16,20},{20,24},{24,28},{29,1},{... | collective-permute-start | bytes 392 | tf_op jit(solution)/shard_map/while/body/eval_jaxpr/ppermute | solution.py:26
  53.6 6.0 %collective-permute-start = (bf16[32,768]{1,0:T(8,128)(2,1)S(1)}, bf16[32,768]{1,0:T(8,128)(2,1)S(1)}, u32[]{:S(2)}, u32[]{:S(2)}) collective-permute-start(bf16[32,768]{1,0:T(8,128)(2,1)S(1)} %copy.23), channel_id=1, source_target_pairs={{28,0},{0,4},{4,8},{8,12},{12,16},{16,20},{20,24},{24,28},{29,1},{... | collective-permute-start | bytes 147464 | tf_op jit(solution)/shard_map/while/body/eval_jaxpr/ppermute | solution.py:26
  54.7 3.9 %collective-permute-start.1 = (f32[32]{0:T(128)S(1)}, f32[32]{0:T(128)S(1)}, u32[]{:S(2)}, u32[]{:S(2)}) collective-permute-start(f32[32]{0:T(128)S(1)} %max.50), channel_id=1, source_target_pairs={{28,0},{0,4},{4,8},{8,12},{12,16},{16,20},{20,24},{24,28},{29,1},{... | collective-permute-start | bytes 392 | tf_op jit(solution)/shard_map/while/body/eval_jaxpr/ppermute | solution.py:26
  55.6 3.9 %collective-permute-start.2 = (f32[32]{0:T(128)S(1)}, f32[32]{0:T(128)S(1)}, u32[]{:S(2)}, u32[]{:S(2)}) collective-permute-start(f32[32]{0:T(128)S(1)} %multiply_add_fusion.4), channel_id=1, source_target_pairs={{28,0},{0,4},{4,8},{8,12},{12,16},{16,20},{20,24},{24,28},{29,1},{... | collective-permute-start | bytes 392 | tf_op jit(solution)/shard_map/while/body/eval_jaxpr/ppermute | solution.py:26
  59.6 5.4 %collective-permute-start = (bf16[32,768]{1,0:T(8,128)(2,1)S(1)}, bf16[32,768]{1,0:T(8,128)(2,1)S(1)}, u32[]{:S(2)}, u32[]{:S(2)}) collective-permute-start(bf16[32,768]{1,0:T(8,128)(2,1)S(1)} %copy.23), channel_id=1, source_target_pairs={{28,0},{0,4},{4,8},{8,12},{12,16},{16,20},{20,24},{24,28},{29,1},{... | collective-permute-start | bytes 147464 | tf_op jit(solution)/shard_map/while/body/eval_jaxpr/ppermute | solution.py:26
  60.7 3.9 %collective-permute-start.1 = (f32[32]{0:T(128)S(1)}, f32[32]{0:T(128)S(1)}, u32[]{:S(2)}, u32[]{:S(2)}) collective-permute-start(f32[32]{0:T(128)S(1)} %max.50), channel_id=1, source_target_pairs={{28,0},{0,4},{4,8},{8,12},{12,16},{16,20},{20,24},{24,28},{29,1},{... | collective-permute-start | bytes 392 | tf_op jit(solution)/shard_map/while/body/eval_jaxpr/ppermute | solution.py:26
  61.0 3.9 %collective-permute-start.2 = (f32[32]{0:T(128)S(1)}, f32[32]{0:T(128)S(1)}, u32[]{:S(2)}, u32[]{:S(2)}) collective-permute-start(f32[32]{0:T(128)S(1)} %multiply_add_fusion.4), channel_id=1, source_target_pairs={{28,0},{0,4},{4,8},{8,12},{12,16},{16,20},{20,24},{24,28},{29,1},{... | collective-permute-start | bytes 392 | tf_op jit(solution)/shard_map/while/body/eval_jaxpr/ppermute | solution.py:26
  64.9 6.5 %collective-permute-start = (bf16[32,768]{1,0:T(8,128)(2,1)S(1)}, bf16[32,768]{1,0:T(8,128)(2,1)S(1)}, u32[]{:S(2)}, u32[]{:S(2)}) collective-permute-start(bf16[32,768]{1,0:T(8,128)(2,1)S(1)} %copy.23), channel_id=1, source_target_pairs={{28,0},{0,4},{4,8},{8,12},{12,16},{16,20},{20,24},{24,28},{29,1},{... | collective-permute-start | bytes 147464 | tf_op jit(solution)/shard_map/while/body/eval_jaxpr/ppermute | solution.py:26
  66.1 3.9 %collective-permute-start.1 = (f32[32]{0:T(128)S(1)}, f32[32]{0:T(128)S(1)}, u32[]{:S(2)}, u32[]{:S(2)}) collective-permute-start(f32[32]{0:T(128)S(1)} %max.50), channel_id=1, source_target_pairs={{28,0},{0,4},{4,8},{8,12},{12,16},{16,20},{20,24},{24,28},{29,1},{... | collective-permute-start | bytes 392 | tf_op jit(solution)/shard_map/while/body/eval_jaxpr/ppermute | solution.py:26
  67.5 3.9 %collective-permute-start.2 = (f32[32]{0:T(128)S(1)}, f32[32]{0:T(128)S(1)}, u32[]{:S(2)}, u32[]{:S(2)}) collective-permute-start(f32[32]{0:T(128)S(1)} %multiply_add_fusion.4), channel_id=1, source_target_pairs={{28,0},{0,4},{4,8},{8,12},{12,16},{16,20},{20,24},{24,28},{29,1},{... | collective-permute-start | bytes 392 | tf_op jit(solution)/shard_map/while/body/eval_jaxpr/ppermute | solution.py:26
  71.4 6.9 %collective-permute-start = (bf16[32,768]{1,0:T(8,128)(2,1)S(1)}, bf16[32,768]{1,0:T(8,128)(2,1)S(1)}, u32[]{:S(2)}, u32[]{:S(2)}) collective-permute-start(bf16[32,768]{1,0:T(8,128)(2,1)S(1)} %copy.23), channel_id=1, source_target_pairs={{28,0},{0,4},{4,8},{8,12},{12,16},{16,20},{20,24},{24,28},{29,1},{... | collective-permute-start | bytes 147464 | tf_op jit(solution)/shard_map/while/body/eval_jaxpr/ppermute | solution.py:26
  72.6 3.9 %collective-permute-start.1 = (f32[32]{0:T(128)S(1)}, f32[32]{0:T(128)S(1)}, u32[]{:S(2)}, u32[]{:S(2)}) collective-permute-start(f32[32]{0:T(128)S(1)} %max.50), channel_id=1, source_target_pairs={{28,0},{0,4},{4,8},{8,12},{12,16},{16,20},{20,24},{24,28},{29,1},{... | collective-permute-start | bytes 392 | tf_op jit(solution)/shard_map/while/body/eval_jaxpr/ppermute | solution.py:26
  74.4 3.9 %collective-permute-start.2 = (f32[32]{0:T(128)S(1)}, f32[32]{0:T(128)S(1)}, u32[]{:S(2)}, u32[]{:S(2)}) collective-permute-start(f32[32]{0:T(128)S(1)} %multiply_add_fusion.4), channel_id=1, source_target_pairs={{28,0},{0,4},{4,8},{8,12},{12,16},{16,20},{20,24},{24,28},{29,1},{... | collective-permute-start | bytes 392 | tf_op jit(solution)/shard_map/while/body/eval_jaxpr/ppermute | solution.py:26
  78.3 6.0 %collective-permute-start = (bf16[32,768]{1,0:T(8,128)(2,1)S(1)}, bf16[32,768]{1,0:T(8,128)(2,1)S(1)}, u32[]{:S(2)}, u32[]{:S(2)}) collective-permute-start(bf16[32,768]{1,0:T(8,128)(2,1)S(1)} %copy.23), channel_id=1, source_target_pairs={{28,0},{0,4},{4,8},{8,12},{12,16},{16,20},{20,24},{24,28},{29,1},{... | collective-permute-start | bytes 147464 | tf_op jit(solution)/shard_map/while/body/eval_jaxpr/ppermute | solution.py:26
  79.4 3.9 %collective-permute-start.1 = (f32[32]{0:T(128)S(1)}, f32[32]{0:T(128)S(1)}, u32[]{:S(2)}, u32[]{:S(2)}) collective-permute-start(f32[32]{0:T(128)S(1)} %max.50), channel_id=1, source_target_pairs={{28,0},{0,4},{4,8},{8,12},{12,16},{16,20},{20,24},{24,28},{29,1},{... | collective-permute-start | bytes 392 | tf_op jit(solution)/shard_map/while/body/eval_jaxpr/ppermute | solution.py:26
  80.3 3.9 %collective-permute-start.2 = (f32[32]{0:T(128)S(1)}, f32[32]{0:T(128)S(1)}, u32[]{:S(2)}, u32[]{:S(2)}) collective-permute-start(f32[32]{0:T(128)S(1)} %multiply_add_fusion.4), channel_id=1, source_target_pairs={{28,0},{0,4},{4,8},{8,12},{12,16},{16,20},{20,24},{24,28},{29,1},{... | collective-permute-start | bytes 392 | tf_op jit(solution)/shard_map/while/body/eval_jaxpr/ppermute | solution.py:26
  84.9 22.8 %collective-permute-start.5 = (f32[32]{0:T(128)S(1)}, f32[32]{0:T(128)S(1)}, u32[]{:S(2)}, u32[]{:S(2)}) collective-permute-start(f32[32]{0:T(128)S(1)} %max.39), channel_id=1, source_target_pairs={{28,0},{0,4},{4,8},{8,12},{12,16},{16,20},{20,24},{24,28},{29,1},{... | collective-permute-start | bytes 392 | tf_op jit(solution)/shard_map/ppermute | solution.py:26
  103.8 3.9 %collective-permute-start.6 = (f32[32]{0:T(128)S(1)}, f32[32]{0:T(128)S(1)}, u32[]{:S(2)}, u32[]{:S(2)}) collective-permute-start(f32[32]{0:T(128)S(1)} %multiply_add_fusion.2), channel_id=1, source_target_pairs={{28,0},{0,4},{4,8},{8,12},{12,16},{16,20},{20,24},{24,28},{29,1},{... | collective-permute-start | bytes 392 | tf_op jit(solution)/shard_map/ppermute | solution.py:26
  107.7 3.9 %collective-permute-start.3 = (f32[32]{0:T(128)S(1)}, f32[32]{0:T(128)S(1)}, u32[]{:S(2)}, u32[]{:S(2)}) collective-permute-start(f32[32]{0:T(128)S(1)} %copy.52), channel_id=1, source_target_pairs={{28,0},{0,4},{4,8},{8,12},{12,16},{16,20},{20,24},{24,28},{29,1},{... | collective-permute-start | bytes 392 | tf_op jit(solution)/shard_map/while/body/eval_jaxpr/ppermute | solution.py:26
  108.9 5.0 %collective-permute-start.4 = (f32[32,768]{1,0:T(8,128)S(1)}, f32[32,768]{1,0:T(8,128)S(1)}, u32[]{:S(2)}, u32[]{:S(2)}) collective-permute-start(f32[32,768]{1,0:T(8,128)S(1)} %convolution_add_fusion.6), channel_id=1, source_target_pairs={{28,0},{0,4},{4,8},{8,12},{12,16},{16,20},{20,24},{24,28},{29,1},{... | collective-permute-start | bytes 294920 | tf_op jit(solution)/shard_map/while/body/eval_jaxpr/ppermute | solution.py:26
  113.9 3.9 %collective-permute-start.3 = (f32[32]{0:T(128)S(1)}, f32[32]{0:T(128)S(1)}, u32[]{:S(2)}, u32[]{:S(2)}) collective-permute-start(f32[32]{0:T(128)S(1)} %copy.52), channel_id=1, source_target_pairs={{28,0},{0,4},{4,8},{8,12},{12,16},{16,20},{20,24},{24,28},{29,1},{... | collective-permute-start | bytes 392 | tf_op jit(solution)/shard_map/while/body/eval_jaxpr/ppermute | solution.py:26
  115.0 5.0 %collective-permute-start.4 = (f32[32,768]{1,0:T(8,128)S(1)}, f32[32,768]{1,0:T(8,128)S(1)}, u32[]{:S(2)}, u32[]{:S(2)}) collective-permute-start(f32[32,768]{1,0:T(8,128)S(1)} %convolution_add_fusion.6), channel_id=1, source_target_pairs={{28,0},{0,4},{4,8},{8,12},{12,16},{16,20},{20,24},{24,28},{29,1},{... | collective-permute-start | bytes 294920 | tf_op jit(solution)/shard_map/while/body/eval_jaxpr/ppermute | solution.py:26
  120.0 3.9 %collective-permute-start.3 = (f32[32]{0:T(128)S(1)}, f32[32]{0:T(128)S(1)}, u32[]{:S(2)}, u32[]{:S(2)}) collective-permute-start(f32[32]{0:T(128)S(1)} %copy.52), channel_id=1, source_target_pairs={{28,0},{0,4},{4,8},{8,12},{12,16},{16,20},{20,24},{24,28},{29,1},{... | collective-permute-start | bytes 392 | tf_op jit(solution)/shard_map/while/body/eval_jaxpr/ppermute | solution.py:26
  121.2 5.0 %collective-permute-start.4 = (f32[32,768]{1,0:T(8,128)S(1)}, f32[32,768]{1,0:T(8,128)S(1)}, u32[]{:S(2)}, u32[]{:S(2)}) collective-permute-start(f32[32,768]{1,0:T(8,128)S(1)} %convolution_add_fusion.6), channel_id=1, source_target_pairs={{28,0},{0,4},{4,8},{8,12},{12,16},{16,20},{20,24},{24,28},{29,1},{... | collective-permute-start | bytes 294920 | tf_op jit(solution)/shard_map/while/body/eval_jaxpr/ppermute | solution.py:26
  126.1 3.9 %collective-permute-start.3 = (f32[32]{0:T(128)S(1)}, f32[32]{0:T(128)S(1)}, u32[]{:S(2)}, u32[]{:S(2)}) collective-permute-start(f32[32]{0:T(128)S(1)} %copy.52), channel_id=1, source_target_pairs={{28,0},{0,4},{4,8},{8,12},{12,16},{16,20},{20,24},{24,28},{29,1},{... | collective-permute-start | bytes 392 | tf_op jit(solution)/shard_map/while/body/eval_jaxpr/ppermute | solution.py:26
  127.3 5.0 %collective-permute-start.4 = (f32[32,768]{1,0:T(8,128)S(1)}, f32[32,768]{1,0:T(8,128)S(1)}, u32[]{:S(2)}, u32[]{:S(2)}) collective-permute-start(f32[32,768]{1,0:T(8,128)S(1)} %convolution_add_fusion.6), channel_id=1, source_target_pairs={{28,0},{0,4},{4,8},{8,12},{12,16},{16,20},{20,24},{24,28},{29,1},{... | collective-permute-start | bytes 294920 | tf_op jit(solution)/shard_map/while/body/eval_jaxpr/ppermute | solution.py:26
  132.2 3.9 %collective-permute-start.3 = (f32[32]{0:T(128)S(1)}, f32[32]{0:T(128)S(1)}, u32[]{:S(2)}, u32[]{:S(2)}) collective-permute-start(f32[32]{0:T(128)S(1)} %copy.52), channel_id=1, source_target_pairs={{28,0},{0,4},{4,8},{8,12},{12,16},{16,20},{20,24},{24,28},{29,1},{... | collective-permute-start | bytes 392 | tf_op jit(solution)/shard_map/while/body/eval_jaxpr/ppermute | solution.py:26
  133.4 5.0 %collective-permute-start.4 = (f32[32,768]{1,0:T(8,128)S(1)}, f32[32,768]{1,0:T(8,128)S(1)}, u32[]{:S(2)}, u32[]{:S(2)}) collective-permute-start(f32[32,768]{1,0:T(8,128)S(1)} %convolution_add_fusion.6), channel_id=1, source_target_pairs={{28,0},{0,4},{4,8},{8,12},{12,16},{16,20},{20,24},{24,28},{29,1},{... | collective-permute-start | bytes 294920 | tf_op jit(solution)/shard_map/while/body/eval_jaxpr/ppermute | solution.py:26
  138.4 3.9 %collective-permute-start.3 = (f32[32]{0:T(128)S(1)}, f32[32]{0:T(128)S(1)}, u32[]{:S(2)}, u32[]{:S(2)}) collective-permute-start(f32[32]{0:T(128)S(1)} %copy.52), channel_id=1, source_target_pairs={{28,0},{0,4},{4,8},{8,12},{12,16},{16,20},{20,24},{24,28},{29,1},{... | collective-permute-start | bytes 392 | tf_op jit(solution)/shard_map/while/body/eval_jaxpr/ppermute | solution.py:26
  139.5 5.0 %collective-permute-start.4 = (f32[32,768]{1,0:T(8,128)S(1)}, f32[32,768]{1,0:T(8,128)S(1)}, u32[]{:S(2)}, u32[]{:S(2)}) collective-permute-start(f32[32,768]{1,0:T(8,128)S(1)} %convolution_add_fusion.6), channel_id=1, source_target_pairs={{28,0},{0,4},{4,8},{8,12},{12,16},{16,20},{20,24},{24,28},{29,1},{... | collective-permute-start | bytes 294920 | tf_op jit(solution)/shard_map/while/body/eval_jaxpr/ppermute | solution.py:26
  144.5 3.9 %collective-permute-start.3 = (f32[32]{0:T(128)S(1)}, f32[32]{0:T(128)S(1)}, u32[]{:S(2)}, u32[]{:S(2)}) collective-permute-start(f32[32]{0:T(128)S(1)} %copy.52), channel_id=1, source_target_pairs={{28,0},{0,4},{4,8},{8,12},{12,16},{16,20},{20,24},{24,28},{29,1},{... | collective-permute-start | bytes 392 | tf_op jit(solution)/shard_map/while/body/eval_jaxpr/ppermute | solution.py:26
  145.6 5.0 %collective-permute-start.4 = (f32[32,768]{1,0:T(8,128)S(1)}, f32[32,768]{1,0:T(8,128)S(1)}, u32[]{:S(2)}, u32[]{:S(2)}) collective-permute-start(f32[32,768]{1,0:T(8,128)S(1)} %convolution_add_fusion.6), channel_id=1, source_target_pairs={{28,0},{0,4},{4,8},{8,12},{12,16},{16,20},{20,24},{24,28},{29,1},{... | collective-permute-start | bytes 294920 | tf_op jit(solution)/shard_map/while/body/eval_jaxpr/ppermute | solution.py:26
  151.1 5.0 %collective-permute-start.9 = (f32[32,768]{1,0:T(8,128)S(1)}, f32[32,768]{1,0:T(8,128)S(1)}, u32[]{:S(2)}, u32[]{:S(2)}) collective-permute-start(f32[32,768]{1,0:T(8,128)S(1)} %add.398), channel_id=1, source_target_pairs={{28,0},{0,4},{4,8},{8,12},{12,16},{16,20},{20,24},{24,28},{29,1},{... | collective-permute-start | bytes 294920 | tf_op jit(solution)/shard_map/ppermute | solution.py:26
  171.8 1.0 copy-start
Sparse Core Ops, SparseCore 0:
  152.5 19.2 reduce-scatter.1
where the time goes:
time: 181 us; the launch traced here: 180 us
  waiting for transfers between devices  78.3 us (43%)
  blocking collectives  32.7 us (18%)
  starting transfers between devices  21.6 us (12%)
  matrix products  19.5 us (11%)
  between operations  15 us (8%)
  other arithmetic  7.82 us (4%)
  local copies, waits for them, and re-layouts  4.46 us (2%)
    ppermute x38, waiting for transfers between devices, shifted(): return lax.ppermute(block, axis, route)  61.5 us
    all_gather x2, blocking collectives, combined_all(): everything = jax.tree.map(lambda part: lax.all_gather(part, axis), value)  18.4 us
    reduce_scatter x1, waiting for transfers between devices, body(): lax.psum_scatter(partial_grad.astype(jnp.bfloat16), 'mp', scatter_dimensi...  14.8 us
    all_gather x1, blocking collectives, body(): full_clips = lax.all_gather(clips, 'mp', axis=1, tiled=True)  14.3 us
    dot_general x15, matrix products, tile_scores(): lax.dot_general(caption_panel, clip_unit, (((1,), (1,)), ((), ())), prefe...  12.8 us
    ppermute x38, starting transfers between devices, shifted(): return lax.ppermute(block, axis, route)  12.6 us
    all_to_all x1, starting transfers between devices, body(): lax.all_to_all(captions, 'mp', split_axis=0, concat_axis=1, tiled=True)  6.45 us
  transfers between devices with their start and end apart: 42, of which 32 were waited for; matrix products, arithmetic and copies ran while one was open for 15% of the time, Pallas kernels for 0%

commit v1 on v0

v1 whole, which is shorter than its diff:
```python
import functools
import math

import jax
import jax.numpy as jnp
from jax import lax
from jax.experimental import pallas as pl
from jax.experimental.pallas import tpu as pltpu
from jax.sharding import PartitionSpec as P

epsilon = 1e-06
negative_fill = -1e30
log2_e = math.log2(math.e)


def unit_rows(values):
    widened = values.astype(jnp.float32)
    length = jnp.sqrt(jnp.sum(widened * widened, axis=-1, keepdims=True) + epsilon)
    return widened / length, length


def gather_columns(block):
    count = lax.axis_size("mp")
    chunks = [block]
    for k in range(1, count):
        chunks.append(lax.ppermute(block, "mp", [(i, i ^ k) for i in range(count)]))
    return jnp.concatenate(chunks, axis=-1)


def gather_orders(dp_count):
    bits = [1 << k for k in range(1, dp_count.bit_length() - 1)]
    return bits, bits[1:] + bits[:1]


def gather_blocks(block):
    dp_count = lax.axis_size("dp")
    even, odd = gather_orders(dp_count)
    held = block[None]
    for bit_even, bit_odd in zip(even, odd):
        route = [(i, i ^ (bit_odd if i & 1 else bit_even)) for i in range(dp_count)]
        held = jnp.concatenate([held, lax.ppermute(held, "dp", route)], axis=0)
    other = lax.ppermute(held, "dp", [(i, i ^ 1) for i in range(dp_count)])
    return jnp.concatenate([held, other], axis=0)


def block_offsets(dp_count):
    even, odd = gather_orders(dp_count)
    own = []
    for order in (even, odd):
        held = [0]
        for bit in order:
            held = held + [h ^ bit for h in held]
        own.append(held)
    return [own[0] + [h ^ 1 for h in own[1]], own[1] + [h ^ 1 for h in own[0]]]


def kernel(
    mp_ref,
    scale_ref,
    clips_ref,
    caps_ref,
    own_clips_ref,
    own_caps_ref,
    row_videos_ref,
    column_videos_ref,
    d_clips_ref,
    d_caps_ref,
    row_lse_ref,
    col_max_ref,
    col_sum_ref,
    *,
    mp_count,
):
    total = clips_ref.shape[0]
    own = own_clips_ref.shape[0]
    width = clips_ref.shape[1]
    row_tile = min(256, total)
    col_tile = min(1024, total)
    mp_index = mp_ref[0]
    scale = scale_ref[0]
    scale2 = scale * log2_e
    contract_last = (((1,), (1,)), ((), ()))

    col_max_ref[...] = jnp.full(col_max_ref.shape, negative_fill, jnp.float32)
    col_sum_ref[...] = jnp.zeros(col_sum_ref.shape, jnp.float32)

    def one_tile(row_first, col_first, carry):
        row_max, row_sum = carry
        rows = pl.ds(row_first, row_tile)
        cols = pl.ds(col_first, col_tile)
        scores = scale2 * lax.dot_general(
            clips_ref[rows, :], caps_ref[cols, :], contract_last, preferred_element_type=jnp.float32
        )
        same = column_videos_ref[rows, :] == row_videos_ref[:, cols]
        distance = lax.broadcasted_iota(jnp.int32, scores.shape, 0) - lax.broadcasted_iota(
            jnp.int32, scores.shape, 1
        )
        off_diagonal = distance != col_first - row_first
        scores = jnp.where(same & off_diagonal, negative_fill, scores)
        new_row = jnp.maximum(row_max, jnp.max(scores, axis=1, keepdims=True))
        row_sum = row_sum * jnp.exp2(row_max - new_row) + jnp.sum(
            jnp.exp2(scores - new_row), axis=1, keepdims=True
        )
        old_col = col_max_ref[:, cols]
        new_col = jnp.maximum(old_col, jnp.max(scores, axis=0, keepdims=True))
        col_sum_ref[:, cols] = col_sum_ref[:, cols] * jnp.exp2(old_col - new_col) + jnp.sum(
            jnp.exp2(scores - new_col), axis=0, keepdims=True
        )
        col_max_ref[:, cols] = new_col
        return new_row, row_sum

    def one_row_block(block):
        row_first = block * row_tile
        if not isinstance(block, int):
            row_first = pl.multiple_of(row_first, row_tile)
        carry = (
            jnp.full((row_tile, 1), negative_fill, jnp.float32),
            jnp.zeros((row_tile, 1), jnp.float32),
        )
        if total == col_tile:
            row_max, row_sum = one_tile(row_first, 0, carry)
        else:
            row_max, row_sum = lax.fori_loop(
                0,
                total // col_tile,
                lambda c, so_far: one_tile(row_first, pl.multiple_of(c * col_tile, col_tile), so_far),
                carry,
            )
        lse = row_max + jnp.log2(row_sum)
        row_lse_ref[:, pl.ds(row_first, row_tile)] = jnp.transpose(
            jnp.broadcast_to(lse, (row_tile, 128))
        )[:8, :]

    if total // row_tile <= 8:
        for block in range(total // row_tile):
            one_row_block(block)
    else:
        pl.loop(0, total // row_tile)(one_row_block)

    col_lse = col_max_ref[...] + jnp.log2(col_sum_ref[...])
    row_lse = row_lse_ref[0:1, :]

    own_first = pl.multiple_of(mp_index * own, own)
    own_rows = pl.ds(own_first, own)
    clip_unit = clips_ref[own_rows, :]
    cap_unit = caps_ref[own_rows, :]
    same = column_videos_ref[own_rows, :] == row_videos_ref[...]
    distance = lax.broadcasted_iota(jnp.int32, (own, total), 1) - lax.broadcasted_iota(
        jnp.int32, (own, total), 0
    )
    blocked = same & (distance != own_first)
    same = same.astype(jnp.bfloat16)

    def strip(unit, others_ref, own_lse_all, other_lse):
        scores = scale2 * lax.dot_general(
            unit, others_ref[...], contract_last, preferred_element_type=jnp.float32
        )
        scores = jnp.where(blocked, negative_fill, scores)
        top = jnp.max(scores, axis=1, keepdims=True)
        own_lse = top + jnp.log2(jnp.sum(jnp.exp2(scores - top), axis=1, keepdims=True))
        weights = 0.5 * (jnp.exp2(scores - own_lse) + jnp.exp2(scores - other_lse))
        weights = weights.astype(jnp.bfloat16)
        both = jnp.concatenate([weights, same], axis=0)
        sums = jnp.dot(both, others_ref[...], preferred_element_type=jnp.float32)
        return sums[:own], sums[own:]

    clip_acc, caption_pool = strip(clip_unit, caps_ref, None, col_lse)
    cap_acc, pooled = strip(cap_unit, clips_ref, None, row_lse)
    clip_unit = clip_unit.astype(jnp.float32)
    cap_unit = cap_unit.astype(jnp.float32)
    pool_length = jnp.sqrt(jnp.sum(pooled * pooled, axis=1, keepdims=True) + epsilon)
    pool_unit = pooled / pool_length
    projected = caption_pool - pool_unit * jnp.sum(pool_unit * caption_pool, axis=1, keepdims=True)
    clip_grad = scale * clip_acc - 0.5 * scale * cap_unit - 0.5 * scale * projected / pool_length
    cap_grad = scale * cap_acc - 0.5 * scale * clip_unit - 0.5 * scale * pool_unit

    def finish(values_ref, grad, out_ref):
        unit, length = unit_rows(values_ref[...])
        result = (grad - unit * jnp.sum(unit * grad, axis=1, keepdims=True)) / length
        chunk = width // mp_count
        for index in range(mp_count):

            @pl.when(mp_index == index)
            def _():
                out_ref[...] = jnp.concatenate(
                    [result[:, (q ^ index) * chunk : ((q ^ index) + 1) * chunk] for q in range(mp_count)],
                    axis=1,
                )

    finish(own_clips_ref, clip_grad, d_clips_ref)
    finish(own_caps_ref, cap_grad, d_caps_ref)


def body(clips, captions, video_id, logit_scale):
    dp_count = lax.axis_size("dp")
    mp_count = lax.axis_size("mp")
    row_count = clips.shape[0]
    own = row_count // mp_count
    width = clips.shape[1] * mp_count
    total = row_count * dp_count
    dp_index = lax.axis_index("dp")
    mp_index = lax.axis_index("mp")

    full = gather_columns(jnp.stack([clips, captions]))
    unit = unit_rows(full)[0].astype(jnp.bfloat16)
    own_raw = lax.dynamic_slice_in_dim(full, mp_index * own, own, 1)
    every = gather_blocks(unit)
    all_clips = every[:, 0].reshape(total, width)
    all_caps = every[:, 1].reshape(total, width)

    offsets = block_offsets(dp_count)
    videos = []
    for even, odd in zip(*offsets):
        block = dp_index ^ jnp.where(dp_index & 1, odd, even)
        videos.append(lax.dynamic_slice_in_dim(video_id, block * row_count, row_count, 0))
    videos = jnp.concatenate(videos)

    vmem = pl.BlockSpec(memory_space=pltpu.VMEM)
    smem = pl.BlockSpec(memory_space=pltpu.SMEM)
    out = jax.ShapeDtypeStruct((own, width), jnp.float32)
    return pl.pallas_call(
        functools.partial(kernel, mp_count=mp_count),
        out_shape=(out, out),
        in_specs=[smem, smem] + [vmem] * 6,
        out_specs=(vmem, vmem),
        scratch_shapes=[
            pltpu.VMEM((8, total), jnp.float32),
            pltpu.VMEM((1, total), jnp.float32),
            pltpu.VMEM((1, total), jnp.float32),
        ],
        compiler_params=pltpu.CompilerParams(vmem_limit_bytes=48 * 1024 * 1024),
    )(
        jnp.reshape(mp_index, (1,)).astype(jnp.int32),
        jnp.reshape(logit_scale, (1,)),
        all_clips,
        all_caps,
        own_raw[0],
        own_raw[1],
        videos[None, :],
        videos[:, None],
    )


def solution(mesh):
    in_specs = (P("dp", "mp"), P("dp", "mp"), P(), P())
    out_specs = (P(("dp", "mp"), None), P(("dp", "mp"), None))
    return jax.shard_map(body, mesh=mesh, in_specs=in_specs, out_specs=out_specs, check_vma=False)
```

time: 181 us -> 53 us (0.29)
  waiting for transfers between devices: 78.3 us -> 29.9 us
  blocking collectives: 32.7 us -> 0 us
  matrix products: 19.5 us -> 0 us
  between operations: 15 us -> 1.38 us
  starting transfers between devices: 21.6 us -> 8.82 us
  Pallas kernels: 0 us -> 6.15 us
  other arithmetic: 7.82 us -> 3.45 us
    ppermute x40 -> x6, waiting for transfers between devices: 63.5 us -> 29.9 us  [the longest x2 17.4 us: gather_blocks(): held = jnp.concatenate([held, lax.ppermute(held, 'dp', route)], axis=0)]
    all_gather x3 -> x0, blocking collectives: 32.7 us -> none  [the longest x2 18.4 us: combined_all(): everything = jax.tree.map(lambda part: lax.all_gather(part, axis), value)]
    dot_general x40 -> x0, matrix products: 19.5 us -> none  [the longest x15 12.8 us: tile_scores(): lax.dot_general(caption_panel, clip_unit, (((1,), (1,)), ((), ())), prefe...]
    reduce_scatter x1 -> x0, waiting for transfers between devices: 14.8 us -> none  [body(): lax.psum_scatter(partial_grad.astype(jnp.bfloat16), 'mp', scatter_dimensi...]
    all_to_all x1 -> x0, starting transfers between devices: 6.45 us -> none  [body(): lax.all_to_all(captions, 'mp', split_axis=0, concat_axis=1, tiled=True)]
    ppermute x40 -> x6, starting transfers between devices: 15.1 us -> 8.82 us  [the longest x3 5.68 us: gather_columns(): chunks.append(lax.ppermute(block, 'mp', [(i, i ^ k) for i in range(count)]))]
    pallas_call x0 -> x1, Pallas kernels: none -> 6.15 us  [body(): pl.pallas_call(functools.partial(kernel, mp_count=mp_count), out_shape=(o...]
    reduce_sum x14 -> x1, other arithmetic: 3.38 us -> 0.27 us  [unit_rows(): jnp.sum(widened * widened, axis=-1, keepdims=True) + epsilon]
  transfers between devices with their start and end apart: 42 -> 6, of which waited for: 32 -> 5; matrix products, arithmetic and copies ran while one was open for 15% -> 2% of each run, Pallas kernels for 0% -> 0%
where the time goes in v1:
time: 53 us; the launch traced here: 52.7 us
  waiting for transfers between devices  29.9 us (56%)
  starting transfers between devices  8.82 us (17%)
  Pallas kernels  6.15 us (12%)
  other arithmetic  3.45 us (7%)
  local copies, waits for them, and re-layouts  2.96 us (6%)
  between operations  1.38 us (3%)
    ppermute x2, waiting for transfers between devices, gather_blocks(): held = jnp.concatenate([held, lax.ppermute(held, 'dp', route)], axis=0)  17.4 us
    ppermute x3, waiting for transfers between devices, gather_columns(): chunks.append(lax.ppermute(block, 'mp', [(i, i ^ k) for i in range(count)]))  10.3 us
    pallas_call x1, Pallas kernels, body(): pl.pallas_call(functools.partial(kernel, mp_count=mp_count), out_shape=(o...  6.15 us
    ppermute x3, starting transfers between devices, gather_columns(): chunks.append(lax.ppermute(block, 'mp', [(i, i ^ k) for i in range(count)]))  5.68 us
    ppermute x2, starting transfers between devices, gather_blocks(): held = jnp.concatenate([held, lax.ppermute(held, 'dp', route)], axis=0)  3.14 us
    unnamed x11, local copies, waits for them, and re-layouts  2.35 us
    ppermute x1, waiting for transfers between devices, gather_blocks(): other = lax.ppermute(held, 'dp', [(i, i ^ 1) for i in range(dp_count)])  2.2 us
    concatenate x1, other arithmetic, gather_blocks(): return jnp.concatenate([held, other], axis=0)  1.55 us
  transfers between devices with their start and end apart: 6, of which 5 were waited for; matrix products, arithmetic and copies ran while one was open for 2% of the time, Pallas kernels for 0%

profile of v1, /device:TPU:0, one launch (start us, length us, event | category | flops | bytes accessed | tf_op | source)
XLA Modules:
  0.0 52.7 jit_solution(17015778252954836591)
XLA Ops:
  0.6 0.9 %copy.8 = bf16[128,192]{1,0:T(8,128)(2,1)S(1)} copy(bf16[128,192]{0,1:T(8,128)(2,1)} %param.4) | data formatting | bytes 98304 | tf_op args[0]
  1.5 0.9 %copy.9 = bf16[128,192]{1,0:T(8,128)(2,1)S(1)} copy(bf16[128,192]{0,1:T(8,128)(2,1)} %param.5) | data formatting | bytes 98304 | tf_op args[1]
  2.5 3.1 %collective-permute-start = (bf16[2,128,192]{2,1,0:T(8,128)(2,1)S(1)}, bf16[2,128,192]{2,1,0:T(8,128)(2,1)S(1)}, u32[]{:S(2)}, u32[]{:S(2)}) collective-permute-start(bf16[2,128,192]{2,1,0:T(8,128)(2,1)S(1)} %get-tuple-element.9), channel_id=1, source_target_pairs={{0,1},{1,0},{2,3},{3,2},{4,5},{5,4},{6,7},{7,6},{8,9},{9,8},{10,11... | collective-permute-start | bytes 294920 | tf_op jit(solution)/shard_map/ppermute | solution.py:26
  5.6 2.6 %collective-permute-start.1 = (bf16[2,128,192]{2,1,0:T(8,128)(2,1)S(1)}, bf16[2,128,192]{2,1,0:T(8,128)(2,1)S(1)}, u32[]{:S(2)}, u32[]{:S(2)}) collective-permute-start(bf16[2,128,192]{2,1,0:T(8,128)(2,1)S(1)} %get-tuple-element.9), channel_id=1, source_target_pairs={{0,2},{1,3},{2,0},{3,1},{4,6},{5,7},{6,4},{7,5},{8,10},{9,11},{10,... | collective-permute-start | bytes 294920 | tf_op jit(solution)/shard_map/ppermute | solution.py:26
  8.2 0.0 collective-permute-start.2
  8.2 2.4 %collective-permute-done = bf16[2,128,192]{2,1,0:T(8,128)(2,1)S(1)} collective-permute-done((bf16[2,128,192]{2,1,0:T(8,128)(2,1)S(1)}, bf16[2,128,192]{2,1,0:T(8,128)(2,1)S(1)}, u32[]{:S(2)}, u32[]{:S(2)}) %collective-permute-start) | collective-permute-done | bytes 98336 | tf_op jit(solution)/shard_map/ppermute | solution.py:26
  10.6 7.9 %collective-permute-done.1 = bf16[2,128,192]{2,1,0:T(8,128)(2,1)S(1)} collective-permute-done((bf16[2,128,192]{2,1,0:T(8,128)(2,1)S(1)}, bf16[2,128,192]{2,1,0:T(8,128)(2,1)S(1)}, u32[]{:S(2)}, u32[]{:S(2)}) %collective-permute-start.1) | collective-permute-done | bytes 98336 | tf_op jit(solution)/shard_map/ppermute | solution.py:26
  18.5 0.0 collective-permute-done.2
  18.5 0.3 multiply_reduce_fusion
  18.8 0.2 divide_convert_fusion
  19.0 1.6 %collective-permute-start.3 = (bf16[1,2,128,768]{3,2,1,0:T(8,128)(2,1)S(1)}, bf16[1,2,128,768]{3,2,1,0:T(8,128)(2,1)S(1)}, u32[]{:S(2)}, u32[]{:S(2)}) collective-permute-start(bf16[1,2,128,768]{3,2,1,0:T(8,128)(2,1)S(1)} %divide_convert_fusion), channel_id=1, source_target_pairs={{0,8},{4,20},{8,0},{12,28},{16,24},{20,4},{24,16},{28,12},{1,9},{5... | collective-permute-start | bytes 1179656 | tf_op jit(solution)/shard_map/ppermute | solution.py:41
  20.6 6.9 %collective-permute-done.3 = bf16[1,2,128,768]{3,2,1,0:T(8,128)(2,1)S(1)} collective-permute-done((bf16[1,2,128,768]{3,2,1,0:T(8,128)(2,1)S(1)}, bf16[1,2,128,768]{3,2,1,0:T(8,128)(2,1)S(1)}, u32[]{:S(2)}, u32[]{:S(2)}) %collective-permute-start.3) | collective-permute-done | bytes 393248 | tf_op jit(solution)/shard_map/ppermute | solution.py:41
  27.5 0.1 pad_maximum_fusion.2
  27.6 0.0 copy-start
  27.6 1.6 %collective-permute-start.4 = (bf16[2,2,128,768]{3,2,1,0:T(8,128)(2,1)S(1)}, bf16[2,2,128,768]{3,2,1,0:T(8,128)(2,1)S(1)}, u32[]{:S(2)}, u32[]{:S(2)}) collective-permute-start(bf16[2,2,128,768]{3,2,1,0:T(8,128)(2,1)S(1)} %pad_maximum_fusion.2), channel_id=1, source_target_pairs={{0,16},{4,12},{8,24},{12,4},{16,0},{20,28},{24,8},{28,20},{1,17},{... | collective-permute-start | bytes 2359304 | tf_op jit(solution)/shard_map/ppermute | solution.py:41
  29.2 10.5 %collective-permute-done.4 = bf16[2,2,128,768]{3,2,1,0:T(8,128)(2,1)S(1)} collective-permute-done((bf16[2,2,128,768]{3,2,1,0:T(8,128)(2,1)S(1)}, bf16[2,2,128,768]{3,2,1,0:T(8,128)(2,1)S(1)}, u32[]{:S(2)}, u32[]{:S(2)}) %collective-permute-start.4) | collective-permute-done | bytes 786464 | tf_op jit(solution)/shard_map/ppermute | solution.py:41
  39.6 1.3 %pad_maximum_fusion.1 = bf16[4,2,128,768]{3,2,1,0:T(8,128)(2,1)} fusion(bf16[2,2,128,768]{3,2,1,0:T(8,128)(2,1)S(1)} %collective-permute-done.4, bf16[1,2,128,768]{3,2,1,0:T(8,128)(2,1)S(1)} %collective-permute-done.3, bf16[1,2,128,768]{3,2,1,0:T(8,128)(2,1)S(1)} %divide_convert_fusion), kind=kLoop, calls=%fused_computation.1 | loop fusion | flops 1572864 | bytes 3145728 | tf_op jit(solution)/shard_map/concatenate | solution.py:41
  41.0 0.0 collective-permute-start.5
  41.0 0.0 copy-done
  41.0 0.1 constant_dynamic-update-slice_fusion.7
  41.0 0.1 constant_dynamic-update-slice_fusion.6
  41.1 0.1 constant_dynamic-update-slice_fusion.5
  41.2 0.1 constant_dynamic-update-slice_fusion.4
  41.3 0.1 constant_dynamic-update-slice_fusion.3
  41.4 0.1 constant_dynamic-update-slice_fusion.2
  41.4 0.1 constant_dynamic-update-slice_fusion.1
  41.5 0.1 constant_dynamic-update-slice_fusion
  41.6 0.2 copy.10.column_videos_ref
  42.5 2.2 %collective-permute-done.5 = bf16[4,2,128,768]{3,2,1,0:T(8,128)(2,1)} collective-permute-done((bf16[4,2,128,768]{3,2,1,0:T(8,128)(2,1)}, bf16[4,2,128,768]{3,2,1,0:T(8,128)(2,1)}, u32[]{:S(2)}, u32[]{:S(2)}) %collective-permute-start.5) | collective-permute-done | bytes 1572896 | tf_op jit(solution)/shard_map/ppermute | solution.py:42
  44.7 1.5 %pad_maximum_fusion = bf16[8,2,128,768]{3,2,1,0:T(8,128)(2,1)S(1)} fusion(bf16[4,2,128,768]{3,2,1,0:T(8,128)(2,1)} %collective-permute-done.5, bf16[2,2,128,768]{3,2,1,0:T(8,128)(2,1)S(1)} %collective-permute-done.4, bf16[1,2,128,768]{3,2,1,0:T(8,128)(2,1)S(1)} %collective-permute-done.3, bf16[1,2,128,768]{3,2,1,0:T(8,128)(2,1)S(1)} %divide_convert_fusion), kind=kLoop, calls=%fused_computation | loop fusion | flops 4718592 | bytes 6291456 | tf_op jit(solution)/shard_map/concatenate | solution.py:43
  46.3 0.3 fusion.1
  46.5 6.2 %shard_map.59 = (f32[32,768]{1,0:T(8,128)}, f32[32,768]{1,0:T(8,128)}) custom-call(s32[1]{0:T(128)} %bitcast.mp_ref, f32[1]{0:T(128)} %bitcast.17.scale_ref, bf16[1024,768]{1,0:T(8,128)(2,1)S(1)} %bitcast.19, bf16[1024,768]{1,0:T(8,128)(2,1)S(1)} %bitcast.18, bf16[32,768]{1,0:T(8,128)(2,1)S(1)} %get-tuple-element.7.own_clips_ref, ...), custom_call_target="tpu_custom_call" | custom-call | tf_op jit(solution)/shard_map/pallas_call | solution.py:221
  (4 shorter events, 0.1 us)
Async XLA Ops:
  2.5 8.1 %collective-permute-start = (bf16[2,128,192]{2,1,0:T(8,128)(2,1)S(1)}, bf16[2,128,192]{2,1,0:T(8,128)(2,1)S(1)}, u32[]{:S(2)}, u32[]{:S(2)}) collective-permute-start(bf16[2,128,192]{2,1,0:T(8,128)(2,1)S(1)} %get-tuple-element.9), channel_id=1, source_target_pairs={{0,1},{1,0},{2,3},{3,2},{4,5},{5,4},{6,7},{7,6},{8,9},{9,8},{10,11... | collective-permute-start | bytes 294920 | tf_op jit(solution)/shard_map/ppermute | solution.py:26
  5.6 12.9 %collective-permute-start.1 = (bf16[2,128,192]{2,1,0:T(8,128)(2,1)S(1)}, bf16[2,128,192]{2,1,0:T(8,128)(2,1)S(1)}, u32[]{:S(2)}, u32[]{:S(2)}) collective-permute-start(bf16[2,128,192]{2,1,0:T(8,128)(2,1)S(1)} %get-tuple-element.9), channel_id=1, source_target_pairs={{0,2},{1,3},{2,0},{3,1},{4,6},{5,7},{6,4},{7,5},{8,10},{9,11},{10,... | collective-permute-start | bytes 294920 | tf_op jit(solution)/shard_map/ppermute | solution.py:26
  8.2 10.3 %collective-permute-start.2 = (bf16[2,128,192]{2,1,0:T(8,128)(2,1)S(1)}, bf16[2,128,192]{2,1,0:T(8,128)(2,1)S(1)}, u32[]{:S(2)}, u32[]{:S(2)}) collective-permute-start(bf16[2,128,192]{2,1,0:T(8,128)(2,1)S(1)} %get-tuple-element.9), channel_id=1, source_target_pairs={{0,3},{1,2},{2,1},{3,0},{4,7},{5,6},{6,5},{7,4},{8,11},{9,10},{10,... | collective-permute-start | bytes 294920 | tf_op jit(solution)/shard_map/ppermute | solution.py:26
  19.0 8.5 %collective-permute-start.3 = (bf16[1,2,128,768]{3,2,1,0:T(8,128)(2,1)S(1)}, bf16[1,2,128,768]{3,2,1,0:T(8,128)(2,1)S(1)}, u32[]{:S(2)}, u32[]{:S(2)}) collective-permute-start(bf16[1,2,128,768]{3,2,1,0:T(8,128)(2,1)S(1)} %divide_convert_fusion), channel_id=1, source_target_pairs={{0,8},{4,20},{8,0},{12,28},{16,24},{20,4},{24,16},{28,12},{1,9},{5... | collective-permute-start | bytes 1179656 | tf_op jit(solution)/shard_map/ppermute | solution.py:41
  27.6 13.4 %copy-start = (s32[1024]{0:T(1024)S(1)}, s32[1024]{0:T(1024)}, u32[]{:S(2)}) copy-start(s32[1024]{0:T(1024)} %param.6) | copy-start | bytes 12292
  27.6 12.1 %collective-permute-start.4 = (bf16[2,2,128,768]{3,2,1,0:T(8,128)(2,1)S(1)}, bf16[2,2,128,768]{3,2,1,0:T(8,128)(2,1)S(1)}, u32[]{:S(2)}, u32[]{:S(2)}) collective-permute-start(bf16[2,2,128,768]{3,2,1,0:T(8,128)(2,1)S(1)} %pad_maximum_fusion.2), channel_id=1, source_target_pairs={{0,16},{4,12},{8,24},{12,4},{16,0},{20,28},{24,8},{28,20},{1,17},{... | collective-permute-start | bytes 2359304 | tf_op jit(solution)/shard_map/ppermute | solution.py:41
  41.0 3.8 %collective-permute-start.5 = (bf16[4,2,128,768]{3,2,1,0:T(8,128)(2,1)}, bf16[4,2,128,768]{3,2,1,0:T(8,128)(2,1)}, u32[]{:S(2)}, u32[]{:S(2)}) collective-permute-start(bf16[4,2,128,768]{3,2,1,0:T(8,128)(2,1)} %pad_maximum_fusion.1), channel_id=1, source_target_pairs={{0,4},{4,0},{8,12},{12,8},{16,20},{20,16},{24,28},{28,24},{1,5},{5... | collective-permute-start | bytes 4718600 | tf_op jit(solution)/shard_map/ppermute | solution.py:42

commit v2 on v1

--- a/solution.py
+++ b/solution.py
@@ -11,6 +11,7 @@
 epsilon = 1e-06
 negative_fill = -1e30
 log2_e = math.log2(math.e)
+resident_limit = 8 * 1024 * 1024
 
 
 def unit_rows(values):
@@ -54,7 +55,7 @@
     return [own[0] + [h ^ 1 for h in own[1]], own[1] + [h ^ 1 for h in own[0]]]
 
 
-def kernel(
+def streamed_kernel(
     mp_ref,
     scale_ref,
     clips_ref,
@@ -191,7 +192,7 @@
     finish(own_caps_ref, cap_grad, d_caps_ref)
 
 
-def body(clips, captions, video_id, logit_scale):
+def streamed_body(clips, captions, video_id, logit_scale):
     dp_count = lax.axis_size("dp")
     mp_count = lax.axis_size("mp")
     row_count = clips.shape[0]
@@ -219,7 +220,7 @@
     smem = pl.BlockSpec(memory_space=pltpu.SMEM)
     out = jax.ShapeDtypeStruct((own, width), jnp.float32)
     return pl.pallas_call(
-        functools.partial(kernel, mp_count=mp_count),
+        functools.partial(streamed_kernel, mp_count=mp_count),
         out_shape=(out, out),
         in_specs=[smem, smem] + [vmem] * 6,
         out_specs=(vmem, vmem),
@@ -241,6 +242,213 @@
     )
 
 
+def resident_kernel(
+    mp_ref,
+    scale_ref,
+    *refs,
+    piece_counts,
+    places,
+    mp_count,
+):
+    lead_refs = refs[: piece_counts[0]]
+    rest_refs = refs[piece_counts[0] : sum(piece_counts)]
+    refs = refs[sum(piece_counts) :]
+    row_videos_ref, column_videos_ref, d_clips_ref, d_caps_ref = refs[:4]
+    clips_ref, caps_ref, own_ref, row_lse_ref = refs[4:]
+    total, width = clips_ref.shape
+    rows = own_ref.shape[1]
+    own = d_clips_ref.shape[0]
+    mp_index = mp_ref[0]
+    scale = scale_ref[0]
+    scale2 = scale * log2_e
+
+    for position, (lead_place, rest_place) in enumerate(places):
+        span = pl.ds(position * rows, rows)
+        for kind in range(2):
+            lead_ref, lead_at = lead_refs[lead_place[0]], lead_place[1]
+            rest_ref, rest_at = rest_refs[rest_place[0]], rest_place[1]
+            chunk = width // mp_count
+            raw = jnp.concatenate(
+                [
+                    lead_ref[kind, lead_at * chunk : (lead_at + 1) * chunk, :],
+                    rest_ref[kind, rest_at * (width - chunk) : (rest_at + 1) * (width - chunk), :],
+                ],
+                axis=0,
+            )
+            if position == 0:
+                own_ref[kind] = jnp.transpose(raw)
+            wide = raw.astype(jnp.float32)
+            inverse = 1.0 / jnp.sqrt(jnp.sum(wide * wide, axis=0, keepdims=True) + epsilon)
+            unit = (wide * inverse).astype(jnp.bfloat16)
+            if kind == 0:
+                clips_ref[span, :] = jnp.transpose(unit)
+            else:
+                caps_ref[:, span] = unit
+
+    row_tile = min(256, total)
+    col_max = jnp.full((1, total), negative_fill, jnp.float32)
+    col_sum = jnp.zeros((1, total), jnp.float32)
+    for row_first in range(0, total, row_tile):
+        span = pl.ds(row_first, row_tile)
+        scores = scale2 * jnp.dot(clips_ref[span, :], caps_ref[...], preferred_element_type=jnp.float32)
+        same = column_videos_ref[span, :] == row_videos_ref[...]
+        distance = lax.broadcasted_iota(jnp.int32, scores.shape, 1) - lax.broadcasted_iota(
+            jnp.int32, scores.shape, 0
+        )
+        scores = jnp.where(same & (distance != row_first), negative_fill, scores)
+        row_max = jnp.max(scores, axis=1, keepdims=True)
+        row_sum = jnp.sum(jnp.exp2(scores - row_max), axis=1, keepdims=True)
+        new_col = jnp.maximum(col_max, jnp.max(scores, axis=0, keepdims=True))
+        col_sum = col_sum * jnp.exp2(col_max - new_col) + jnp.sum(
+            jnp.exp2(scores - new_col), axis=0, keepdims=True
+        )
+        col_max = new_col
+        row_lse_ref[:, span] = jnp.transpose(
+            jnp.broadcast_to(row_max + jnp.log2(row_sum), (row_tile, 128))
+        )[:8, :]
+    col_lse = col_max + jnp.log2(col_sum)
+    row_lse = row_lse_ref[0:1, :]
+
+    own_first = pl.multiple_of(mp_index * own, own)
+    own_rows = pl.ds(own_first, own)
+    clip_float, clip_length = unit_rows(own_ref[0, own_rows, :])
+    cap_float, cap_length = unit_rows(own_ref[1, own_rows, :])
+    clip_unit = clips_ref[own_rows, :]
+    cap_unit = cap_float.astype(jnp.bfloat16)
+    same = column_videos_ref[own_rows, :] == row_videos_ref[...]
+    distance = lax.broadcasted_iota(jnp.int32, (own, total), 1) - lax.broadcasted_iota(
+        jnp.int32, (own, total), 0
+    )
+    blocked = same & (distance != own_first)
+    same = same.astype(jnp.bfloat16)
+    last = (((1,), (1,)), ((), ()))
+
+    def strip(products, other_lse):
+        scores = jnp.where(blocked, negative_fill, scale2 * products)
+        top = jnp.max(scores, axis=1, keepdims=True)
+        own_lse = top + jnp.log2(jnp.sum(jnp.exp2(scores - top), axis=1, keepdims=True))
+        weights = 0.5 * (jnp.exp2(scores - own_lse) + jnp.exp2(scores - other_lse))
+        return jnp.concatenate([weights.astype(jnp.bfloat16), same], axis=0)
+
+    clip_products = jnp.dot(clip_unit, caps_ref[...], preferred_element_type=jnp.float32)
+    cap_products = lax.dot_general(cap_unit, clips_ref[...], last, preferred_element_type=jnp.float32)
+    clip_sums = lax.dot_general(
+        strip(clip_products, col_lse), caps_ref[...], last, preferred_element_type=jnp.float32
+    )
+    cap_sums = jnp.dot(strip(cap_products, row_lse), clips_ref[...], preferred_element_type=jnp.float32)
+    clip_acc, caption_pool = clip_sums[:own], clip_sums[own:]
+    cap_acc, pooled = cap_sums[:own], cap_sums[own:]
+    pool_length = jnp.sqrt(jnp.sum(pooled * pooled, axis=1, keepdims=True) + epsilon)
+    pool_unit = pooled / pool_length
+    projected = caption_pool - pool_unit * jnp.sum(pool_unit * caption_pool, axis=1, keepdims=True)
+    clip_grad = (
+        scale * clip_acc
+        - 0.5 * scale * cap_unit.astype(jnp.float32)
+        - 0.5 * scale * projected / pool_length
+    )
+    cap_grad = scale * cap_acc - 0.5 * scale * clip_unit.astype(jnp.float32) - 0.5 * scale * pool_unit
+
+    def finish(unit, length, grad, out_ref):
+        result = (grad - unit * jnp.sum(unit * grad, axis=1, keepdims=True)) / length
+        chunk = width // mp_count
+        for index in range(mp_count):
+
+            @pl.when(mp_index == index)
+            def _():
+                out_ref[...] = jnp.concatenate(
+                    [result[:, (q ^ index) * chunk : ((q ^ index) + 1) * chunk] for q in range(mp_count)],
+                    axis=1,
+                )
+
+    finish(clip_float, clip_length, clip_grad, d_clips_ref)
+    finish(cap_float, cap_length, cap_grad, d_caps_ref)
+
+
+def resident_body(clips, captions, video_id, logit_scale):
+    dp_count = lax.axis_size("dp")
+    mp_count = lax.axis_size("mp")
+    row_count = clips.shape[0]
+    own = row_count // mp_count
+    width = clips.shape[1] * mp_count
+    total = row_count * dp_count
+    dp_index = lax.axis_index("dp")
+    mp_index = lax.axis_index("mp")
+    even, odd = gather_orders(dp_count)
+
+    def along(step, block):
+        route = [(i, i ^ (odd[step] if i & 1 else even[step])) for i in range(dp_count)]
+        return lax.ppermute(block, "dp", route)
+
+    def across(block):
+        return lax.ppermute(block, "dp", [(i, i ^ 1) for i in range(dp_count)])
+
+    lead = jnp.stack([clips.T, captions.T])
+    lead_first = along(0, lead)
+    arrived = [
+        lax.ppermute(lead, "mp", [(i, i ^ k) for i in range(mp_count)]) for k in range(1, mp_count)
+    ]
+    lead_second = along(1, jnp.concatenate([lead, lead_first], axis=1))
+    rest = jnp.concatenate(arrived, axis=1)
+    rest, lead_second = lax.optimization_barrier((rest, lead_second))
+    rest_first = along(0, rest)
+    rest_second = along(1, rest)
+    rest_third = along(1, rest_first)
+    lead_other = across(jnp.concatenate([lead, lead_first, lead_second], axis=1))
+    rest_held = [rest, rest_first, rest_second, rest_third]
+    leads = [lead, lead_first, lead_second, lead_other]
+    rests = rest_held + [across(piece) for piece in rest_held]
+    places = [((0, 0), (0, 0)), ((1, 0), (1, 0)), ((2, 0), (2, 0)), ((2, 1), (3, 0))]
+    places += [((3, p), (4 + p, 0)) for p in range(4)]
+
+    offsets = [[0, even[0], even[1], even[0] ^ even[1]], [0, odd[0], odd[1], odd[0] ^ odd[1]]]
+    offsets = [
+        offsets[0] + [o ^ 1 for o in offsets[1]],
+        offsets[1] + [o ^ 1 for o in offsets[0]],
+    ]
+    videos = []
+    for even_offset, odd_offset in zip(*offsets):
+        block = dp_index ^ jnp.where(dp_index & 1, odd_offset, even_offset)
+        videos.append(lax.dynamic_slice_in_dim(video_id, block * row_count, row_count, 0))
+    videos = jnp.concatenate(videos)
+
+    vmem = pl.BlockSpec(memory_space=pltpu.VMEM)
+    smem = pl.BlockSpec(memory_space=pltpu.SMEM)
+    out = jax.ShapeDtypeStruct((own, width), jnp.float32)
+    return pl.pallas_call(
+        functools.partial(
+            resident_kernel,
+            piece_counts=(len(leads), len(rests)),
+            places=places,
+            mp_count=mp_count,
+        ),
+        out_shape=(out, out),
+        in_specs=[smem, smem] + [vmem] * (len(leads) + len(rests) + 2),
+        out_specs=(vmem, vmem),
+        scratch_shapes=[
+            pltpu.VMEM((total, width), jnp.bfloat16),
+            pltpu.VMEM((width, total), jnp.bfloat16),
+            pltpu.VMEM((2, row_count, width), jnp.bfloat16),
+            pltpu.VMEM((8, total), jnp.float32),
+        ],
+        compiler_params=pltpu.CompilerParams(vmem_limit_bytes=40 * 1024 * 1024),
+    )(
+        jnp.reshape(mp_index, (1,)).astype(jnp.int32),
+        jnp.reshape(logit_scale, (1,)),
+        *leads,
+        *rests,
+        videos[None, :],
+        videos[:, None],
+    )
+
+
+def body(clips, captions, video_id, logit_scale):
+    dp_count, mp_count = lax.axis_size("dp"), lax.axis_size("mp")
+    gathered_bytes = 2 * clips.size * clips.dtype.itemsize * dp_count * mp_count
+    if len(gather_orders(dp_count)[0]) == 2 and gathered_bytes <= resident_limit:
+        return resident_body(clips, captions, video_id, logit_scale)
+    return streamed_body(clips, captions, video_id, logit_scale)
+
+
 def solution(mesh):
     in_specs = (P("dp", "mp"), P("dp", "mp"), P(), P())
     out_specs = (P(("dp", "mp"), None), P(("dp", "mp"), None))

time: 53 us -> 40.6 us (0.77)
  waiting for transfers between devices: 29.9 us -> 15.6 us
  starting transfers between devices: 8.82 us -> 13.8 us
  local copies, waits for them, and re-layouts: 2.96 us -> 0.86 us
  other arithmetic: 3.45 us -> 1.68 us
  Pallas kernels: 6.15 us -> 6.99 us
    ppermute x6 -> x13, waiting for transfers between devices: 29.9 us -> 15.6 us  [the longest x5 9.45 us: along(): return lax.ppermute(block, 'dp', route)]
    ppermute x6 -> x13, starting transfers between devices: 8.82 us -> 13.8 us  [the longest x5 8.44 us: along(): return lax.ppermute(block, 'dp', route)]
    concatenate x4 -> x3, other arithmetic: 2.95 us -> 0.81 us  [the longest x1 0.77 us: resident_body(): jnp.concatenate([lead, lead_first, lead_second], axis=1)]
    unnamed x11 -> x13, local copies, waits for them, and re-layouts: 2.35 us -> 0.56 us
    another operation x0 -> x1, other arithmetic: none -> 0.87 us  [resident_body(): lead = jnp.stack([clips.T, captions.T])]
    pallas_call x1, Pallas kernels: 6.15 us -> 6.99 us  [resident_body(): pl.pallas_call(functools.partial(resident_kernel, piece_counts=(len(leads...]
  transfers between devices with their start and end apart: 6 -> 13, of which waited for: 5 -> 5; matrix products, arithmetic and copies ran while one was open for 2% -> 4% of each run, Pallas kernels for 0% -> 0%
where the time goes in v2:
time: 40.6 us; the launch traced here: 40.4 us
  waiting for transfers between devices  15.6 us (38%)
  starting transfers between devices  13.8 us (34%)
  Pallas kernels  6.99 us (17%)
  other arithmetic  1.68 us (4%)
  between operations  1.43 us (4%)
  local copies, waits for them, and re-layouts  0.86 us (2%)
    ppermute x5, waiting for transfers between devices, along(): return lax.ppermute(block, 'dp', route)  9.45 us
    ppermute x5, starting transfers between devices, along(): return lax.ppermute(block, 'dp', route)  8.44 us
    pallas_call x1, Pallas kernels, resident_body(): pl.pallas_call(functools.partial(resident_kernel, piece_counts=(len(leads...  6.99 us
    ppermute x3, waiting for transfers between devices, resident_body(): lax.ppermute(lead, 'mp', [(i, i ^ k) for i in range(mp_count)])  4.9 us
    ppermute x3, starting transfers between devices, resident_body(): lax.ppermute(lead, 'mp', [(i, i ^ k) for i in range(mp_count)])  4.39 us
    ppermute x5, waiting for transfers between devices, across(): return lax.ppermute(block, 'dp', [(i, i ^ 1) for i in range(dp_count)])  1.21 us
    ppermute x5, starting transfers between devices, across(): return lax.ppermute(block, 'dp', [(i, i ^ 1) for i in range(dp_count)])  1.02 us
    another operation x1, other arithmetic, resident_body(): lead = jnp.stack([clips.T, captions.T])  0.87 us
  transfers between devices with their start and end apart: 13, of which 5 were waited for; matrix products, arithmetic and copies ran while one was open for 4% of the time, Pallas kernels for 0%

profile of v2, /device:TPU:0, one launch (start us, length us, event | category | flops | bytes accessed | tf_op | source)
XLA Modules:
  0.0 40.4 jit_solution(6719521727374663472)
XLA Ops:
  0.6 0.0 copy-start
  0.6 0.0 copy-start.1
  0.6 0.9 %pad_maximum_fusion.3.refs_0_ = bf16[2,192,128]{2,1,0:T(8,128)(2,1)S(1)} fusion(bf16[1,192,128]{2,1,0:T(8,128)(2,1)} %bitcast.13, bf16[1,192,128]{2,1,0:T(8,128)(2,1)} %bitcast.16), kind=kLoop, calls=%fused_computation.3 | loop fusion | flops 49152 | bytes 196608 | tf_op jit(solution)/shard_map/stack | solution.py:385
  1.5 3.0 %collective-permute-start = (bf16[2,192,128]{2,1,0:T(8,128)(2,1)S(1)}, bf16[2,192,128]{2,1,0:T(8,128)(2,1)S(1)}, u32[]{:S(2)}, u32[]{:S(2)}) collective-permute-start(bf16[2,192,128]{2,1,0:T(8,128)(2,1)S(1)} %pad_maximum_fusion.3.refs_0_), channel_id=1, source_target_pairs={{0,8},{4,20},{8,0},{12,28},{16,24},{20,4},{24,16},{28,12},{1,9},{5... | collective-permute-start | bytes 294920 | tf_op jit(solution)/shard_map/ppermute | solution.py:380
  4.5 3.6 %collective-permute-start.3 = (bf16[2,192,128]{2,1,0:T(8,128)(2,1)S(1)}, bf16[2,192,128]{2,1,0:T(8,128)(2,1)S(1)}, u32[]{:S(2)}, u32[]{:S(2)}) collective-permute-start(bf16[2,192,128]{2,1,0:T(8,128)(2,1)S(1)} %pad_maximum_fusion.3.refs_0_), channel_id=1, source_target_pairs={{0,3},{1,2},{2,1},{3,0},{4,7},{5,6},{6,5},{7,4},{8,11},{9,10},{10,... | collective-permute-start | bytes 294920 | tf_op jit(solution)/shard_map/ppermute | solution.py:388
  8.1 0.0 collective-permute-start.2
  8.1 0.8 %collective-permute-start.1 = (bf16[2,192,128]{2,1,0:T(8,128)(2,1)S(1)}, bf16[2,192,128]{2,1,0:T(8,128)(2,1)S(1)}, u32[]{:S(2)}, u32[]{:S(2)}) collective-permute-start(bf16[2,192,128]{2,1,0:T(8,128)(2,1)S(1)} %pad_maximum_fusion.3.refs_0_), channel_id=1, source_target_pairs={{0,1},{1,0},{2,3},{3,2},{4,5},{5,4},{6,7},{7,6},{8,9},{9,8},{10,11... | collective-permute-start | bytes 294920 | tf_op jit(solution)/shard_map/ppermute | solution.py:388
  8.9 0.0 collective-permute-done.refs_1_
  8.9 0.0 copy-done
  8.9 0.0 copy-done.1
  9.0 1.6 %collective-permute-start.4 = (bf16[2,384,128]{2,1,0:T(8,128)(2,1)S(1)}, bf16[2,384,128]{2,1,0:T(8,128)(2,1)S(1)}, u32[]{:S(2)}, u32[]{:S(2)}) collective-permute-start(bf16[2,384,128]{2,1,0:T(8,128)(2,1)S(1)} %pad_maximum_fusion.2), channel_id=1, source_target_pairs={{0,16},{4,12},{8,24},{12,4},{16,0},{20,28},{24,8},{28,20},{1,17},{... | collective-permute-start | bytes 589832 | tf_op jit(solution)/shard_map/ppermute | solution.py:380
  11.2 0.0 copy-start.2
  11.2 0.8 %collective-permute-done.3 = bf16[2,192,128]{2,1,0:T(8,128)(2,1)S(1)} collective-permute-done((bf16[2,192,128]{2,1,0:T(8,128)(2,1)S(1)}, bf16[2,192,128]{2,1,0:T(8,128)(2,1)S(1)}, u32[]{:S(2)}, u32[]{:S(2)}) %collective-permute-start.3) | collective-permute-done | bytes 98336 | tf_op jit(solution)/shard_map/ppermute | solution.py:388
  12.0 4.1 %collective-permute-done.2 = bf16[2,192,128]{2,1,0:T(8,128)(2,1)S(1)} collective-permute-done((bf16[2,192,128]{2,1,0:T(8,128)(2,1)S(1)}, bf16[2,192,128]{2,1,0:T(8,128)(2,1)S(1)}, u32[]{:S(2)}, u32[]{:S(2)}) %collective-permute-start.2) | collective-permute-done | bytes 98336 | tf_op jit(solution)/shard_map/ppermute | solution.py:388
  16.1 0.0 collective-permute-done.1
  16.2 0.0 collective-permute-done.4.refs_2_
  16.2 1.6 %collective-permute-start.6 = (bf16[2,576,128]{2,1,0:T(8,128)(2,1)S(1)}, bf16[2,576,128]{2,1,0:T(8,128)(2,1)S(1)}, u32[]{:S(2)}, u32[]{:S(2)}) collective-permute-start(bf16[2,576,128]{2,1,0:T(8,128)(2,1)S(1)} %pad_maximum_fusion.1.refs_4_), channel_id=1, source_target_pairs={{0,8},{4,20},{8,0},{12,28},{16,24},{20,4},{24,16},{28,12},{1,9},{5... | collective-permute-start | bytes 884744 | tf_op jit(solution)/shard_map/ppermute | solution.py:380
  17.7 0.0 copy-done.2
  17.7 0.1 constant_dynamic-update-slice_fusion.7
  17.8 0.1 constant_dynamic-update-slice_fusion.6
  17.9 0.1 constant_dynamic-update-slice_fusion.5
  18.0 0.5 %collective-permute-start.7 = (bf16[2,576,128]{2,1,0:T(8,128)(2,1)S(1)}, bf16[2,576,128]{2,1,0:T(8,128)(2,1)S(1)}, u32[]{:S(2)}, u32[]{:S(2)}) collective-permute-start(bf16[2,576,128]{2,1,0:T(8,128)(2,1)S(1)} %pad_maximum_fusion.1.refs_4_), channel_id=1, source_target_pairs={{0,16},{4,12},{8,24},{12,4},{16,0},{20,28},{24,8},{28,20},{1,17},{... | collective-permute-start | bytes 884744 | tf_op jit(solution)/shard_map/ppermute | solution.py:380
  18.5 6.5 %collective-permute-done.6.refs_5_ = bf16[2,576,128]{2,1,0:T(8,128)(2,1)S(1)} collective-permute-done((bf16[2,576,128]{2,1,0:T(8,128)(2,1)S(1)}, bf16[2,576,128]{2,1,0:T(8,128)(2,1)S(1)}, u32[]{:S(2)}, u32[]{:S(2)}) %collective-permute-start.6) | collective-permute-done | bytes 294944 | tf_op jit(solution)/shard_map/ppermute | solution.py:380
  24.9 1.8 %collective-permute-start.8 = (bf16[2,576,128]{2,1,0:T(8,128)(2,1)S(1)}, bf16[2,576,128]{2,1,0:T(8,128)(2,1)S(1)}, u32[]{:S(2)}, u32[]{:S(2)}) collective-permute-start(bf16[2,576,128]{2,1,0:T(8,128)(2,1)S(1)} %collective-permute-done.6.refs_5_), channel_id=1, source_target_pairs={{0,16},{4,12},{8,24},{12,4},{16,0},{20,28},{24,8},{28,20},{1,17},{... | collective-permute-start | bytes 884744 | tf_op jit(solution)/shard_map/ppermute | solution.py:380
  26.7 0.1 constant_dynamic-update-slice_fusion.4
  26.8 0.8 %pad_maximum_fusion = bf16[2,768,128]{2,1,0:T(8,128)(2,1)} fusion(bf16[2,384,128]{2,1,0:T(8,128)(2,1)S(1)} %collective-permute-done.4.refs_2_, bf16[2,192,128]{2,1,0:T(8,128)(2,1)S(1)} %collective-permute-done.refs_1_, bf16[1,192,128]{2,1,0:T(8,128)(2,1)S(1)} %bitcast.15, bf16[1,192,128]{2,1,0:T(8,128)(2,1)S(1)} %bitcast.18), kind=kLoop, calls=%fused_computation | loop fusion | flops 1572864 | bytes 786432 | tf_op jit(solution)/shard_map/concatenate | solution.py:396
  27.6 0.0 collective-permute-start.5
  27.6 0.1 constant_dynamic-update-slice_fusion.3
  27.7 0.5 %collective-permute-start.9 = (bf16[2,576,128]{2,1,0:T(8,128)(2,1)S(1)}, bf16[2,576,128]{2,1,0:T(8,128)(2,1)S(1)}, u32[]{:S(2)}, u32[]{:S(2)}) collective-permute-start(bf16[2,576,128]{2,1,0:T(8,128)(2,1)S(1)} %pad_maximum_fusion.1.refs_4_), channel_id=1, source_target_pairs={{0,4},{4,0},{8,12},{12,8},{16,20},{20,16},{24,28},{28,24},{1,5},{5... | collective-permute-start | bytes 884744 | tf_op jit(solution)/shard_map/ppermute | solution.py:383
  28.2 0.1 collective-permute-start.10
  28.2 0.0 collective-permute-done.7.refs_6_
  28.2 0.4 %collective-permute-start.11 = (bf16[2,576,128]{2,1,0:T(8,128)(2,1)S(1)}, bf16[2,576,128]{2,1,0:T(8,128)(2,1)S(1)}, u32[]{:S(2)}, u32[]{:S(2)}) collective-permute-start(bf16[2,576,128]{2,1,0:T(8,128)(2,1)S(1)} %collective-permute-done.7.refs_6_), channel_id=1, source_target_pairs={{0,4},{4,0},{8,12},{12,8},{16,20},{20,16},{24,28},{28,24},{1,5},{5... | collective-permute-start | bytes 884744 | tf_op jit(solution)/shard_map/ppermute | solution.py:383
  28.7 3.0 %collective-permute-done.8.refs_7_ = bf16[2,576,128]{2,1,0:T(8,128)(2,1)S(1)} collective-permute-done((bf16[2,576,128]{2,1,0:T(8,128)(2,1)S(1)}, bf16[2,576,128]{2,1,0:T(8,128)(2,1)S(1)}, u32[]{:S(2)}, u32[]{:S(2)}) %collective-permute-start.8) | collective-permute-done | bytes 294944 | tf_op jit(solution)/shard_map/ppermute | solution.py:380
  31.7 0.0 collective-permute-start.12
  31.7 0.1 constant_dynamic-update-slice_fusion.2
  31.7 0.1 constant_dynamic-update-slice_fusion.1
  31.8 0.1 constant_dynamic-update-slice_fusion
  31.9 0.2 copy.6.refs_13_
  32.1 0.0 collective-permute-done.9.refs_8_
  32.1 0.0 collective-permute-done.5.refs_3_
  32.2 0.0 collective-permute-done.11.refs_10_
  32.2 0.0 collective-permute-done.10.refs_9_
  32.2 1.2 %collective-permute-done.12.refs_11_ = bf16[2,576,128]{2,1,0:T(8,128)(2,1)} collective-permute-done((bf16[2,576,128]{2,1,0:T(8,128)(2,1)S(1)}, bf16[2,576,128]{2,1,0:T(8,128)(2,1)}, u32[]{:S(2)}, u32[]{:S(2)}) %collective-permute-start.12) | collective-permute-done | bytes 294944 | tf_op jit(solution)/shard_map/ppermute | solution.py:383
  33.4 7.0 %shard_map.59 = (f32[32,768]{1,0:T(8,128)}, f32[32,768]{1,0:T(8,128)}) custom-call(s32[1]{0:T(128)} %bitcast.mp_ref, f32[1]{0:T(128)} %bitcast.10.scale_ref, bf16[2,192,128]{2,1,0:T(8,128)(2,1)S(1)} %pad_maximum_fusion.3.refs_0_, bf16[2,192,128]{2,1,0:T(8,128)(2,1)S(1)} %collective-permute-done.refs_1_, ...), custom_call_target="tpu_custom_call" | custom-call | tf_op jit(solution)/shard_map/pallas_call | solution.py:417
  (3 shorter events, 0.0 us)
Async XLA Ops:
  0.6 8.3 %copy-start = (bf16[128,192]{0,1:T(8,128)(2,1)S(1)}, bf16[128,192]{0,1:T(8,128)(2,1)}, u32[]{:S(2)}) copy-start(bf16[128,192]{0,1:T(8,128)(2,1)} %param.5) | copy-start | bytes 147460
  0.6 8.3 %copy-start.1 = (bf16[128,192]{0,1:T(8,128)(2,1)S(1)}, bf16[128,192]{0,1:T(8,128)(2,1)}, u32[]{:S(2)}) copy-start(bf16[128,192]{0,1:T(8,128)(2,1)} %param.4) | copy-start | bytes 147460
  1.5 7.4 %collective-permute-start = (bf16[2,192,128]{2,1,0:T(8,128)(2,1)S(1)}, bf16[2,192,128]{2,1,0:T(8,128)(2,1)S(1)}, u32[]{:S(2)}, u32[]{:S(2)}) collective-permute-start(bf16[2,192,128]{2,1,0:T(8,128)(2,1)S(1)} %pad_maximum_fusion.3.refs_0_), channel_id=1, source_target_pairs={{0,8},{4,20},{8,0},{12,28},{16,24},{20,4},{24,16},{28,12},{1,9},{5... | collective-permute-start | bytes 294920 | tf_op jit(solution)/shard_map/ppermute | solution.py:380
  4.5 7.5 %collective-permute-start.3 = (bf16[2,192,128]{2,1,0:T(8,128)(2,1)S(1)}, bf16[2,192,128]{2,1,0:T(8,128)(2,1)S(1)}, u32[]{:S(2)}, u32[]{:S(2)}) collective-permute-start(bf16[2,192,128]{2,1,0:T(8,128)(2,1)S(1)} %pad_maximum_fusion.3.refs_0_), channel_id=1, source_target_pairs={{0,3},{1,2},{2,1},{3,0},{4,7},{5,6},{6,5},{7,4},{8,11},{9,10},{10,... | collective-permute-start | bytes 294920 | tf_op jit(solution)/shard_map/ppermute | solution.py:388
  8.1 8.0 %collective-permute-start.2 = (bf16[2,192,128]{2,1,0:T(8,128)(2,1)S(1)}, bf16[2,192,128]{2,1,0:T(8,128)(2,1)S(1)}, u32[]{:S(2)}, u32[]{:S(2)}) collective-permute-start(bf16[2,192,128]{2,1,0:T(8,128)(2,1)S(1)} %pad_maximum_fusion.3.refs_0_), channel_id=1, source_target_pairs={{0,2},{1,3},{2,0},{3,1},{4,6},{5,7},{6,4},{7,5},{8,10},{9,11},{10,... | collective-permute-start | bytes 294920 | tf_op jit(solution)/shard_map/ppermute | solution.py:388
  8.1 8.0 %collective-permute-start.1 = (bf16[2,192,128]{2,1,0:T(8,128)(2,1)S(1)}, bf16[2,192,128]{2,1,0:T(8,128)(2,1)S(1)}, u32[]{:S(2)}, u32[]{:S(2)}) collective-permute-start(bf16[2,192,128]{2,1,0:T(8,128)(2,1)S(1)} %pad_maximum_fusion.3.refs_0_), channel_id=1, source_target_pairs={{0,1},{1,0},{2,3},{3,2},{4,5},{5,4},{6,7},{7,6},{8,9},{9,8},{10,11... | collective-permute-start | bytes 294920 | tf_op jit(solution)/shard_map/ppermute | solution.py:388
  9.0 7.2 %collective-permute-start.4 = (bf16[2,384,128]{2,1,0:T(8,128)(2,1)S(1)}, bf16[2,384,128]{2,1,0:T(8,128)(2,1)S(1)}, u32[]{:S(2)}, u32[]{:S(2)}) collective-permute-start(bf16[2,384,128]{2,1,0:T(8,128)(2,1)S(1)} %pad_maximum_fusion.2), channel_id=1, source_target_pairs={{0,16},{4,12},{8,24},{12,4},{16,0},{20,28},{24,8},{28,20},{1,17},{... | collective-permute-start | bytes 589832 | tf_op jit(solution)/shard_map/ppermute | solution.py:380
  11.2 6.5 %copy-start.2 = (s32[1024]{0:T(1024)S(1)}, s32[1024]{0:T(1024)}, u32[]{:S(2)}) copy-start(s32[1024]{0:T(1024)} %param.6) | copy-start | bytes 12292
  16.2 8.8 %collective-permute-start.6 = (bf16[2,576,128]{2,1,0:T(8,128)(2,1)S(1)}, bf16[2,576,128]{2,1,0:T(8,128)(2,1)S(1)}, u32[]{:S(2)}, u32[]{:S(2)}) collective-permute-start(bf16[2,576,128]{2,1,0:T(8,128)(2,1)S(1)} %pad_maximum_fusion.1.refs_4_), channel_id=1, source_target_pairs={{0,8},{4,20},{8,0},{12,28},{16,24},{20,4},{24,16},{28,12},{1,9},{5... | collective-permute-start | bytes 884744 | tf_op jit(solution)/shard_map/ppermute | solution.py:380
  18.0 10.3 %collective-permute-start.7 = (bf16[2,576,128]{2,1,0:T(8,128)(2,1)S(1)}, bf16[2,576,128]{2,1,0:T(8,128)(2,1)S(1)}, u32[]{:S(2)}, u32[]{:S(2)}) collective-permute-start(bf16[2,576,128]{2,1,0:T(8,128)(2,1)S(1)} %pad_maximum_fusion.1.refs_4_), channel_id=1, source_target_pairs={{0,16},{4,12},{8,24},{12,4},{16,0},{20,28},{24,8},{28,20},{1,17},{... | collective-permute-start | bytes 884744 | tf_op jit(solution)/shard_map/ppermute | solution.py:380
  24.9 6.7 %collective-permute-start.8 = (bf16[2,576,128]{2,1,0:T(8,128)(2,1)S(1)}, bf16[2,576,128]{2,1,0:T(8,128)(2,1)S(1)}, u32[]{:S(2)}, u32[]{:S(2)}) collective-permute-start(bf16[2,576,128]{2,1,0:T(8,128)(2,1)S(1)} %collective-permute-done.6.refs_5_), channel_id=1, source_target_pairs={{0,16},{4,12},{8,24},{12,4},{16,0},{20,28},{24,8},{28,20},{1,17},{... | collective-permute-start | bytes 884744 | tf_op jit(solution)/shard_map/ppermute | solution.py:380
  27.6 4.6 %collective-permute-start.5 = (bf16[2,768,128]{2,1,0:T(8,128)(2,1)}, bf16[2,768,128]{2,1,0:T(8,128)(2,1)S(1)}, u32[]{:S(2)}, u32[]{:S(2)}) collective-permute-start(bf16[2,768,128]{2,1,0:T(8,128)(2,1)} %pad_maximum_fusion), channel_id=1, source_target_pairs={{0,4},{4,0},{8,12},{12,8},{16,20},{20,16},{24,28},{28,24},{1,5},{5... | collective-permute-start | bytes 1179656 | tf_op jit(solution)/shard_map/ppermute | solution.py:383
  27.7 4.5 %collective-permute-start.9 = (bf16[2,576,128]{2,1,0:T(8,128)(2,1)S(1)}, bf16[2,576,128]{2,1,0:T(8,128)(2,1)S(1)}, u32[]{:S(2)}, u32[]{:S(2)}) collective-permute-start(bf16[2,576,128]{2,1,0:T(8,128)(2,1)S(1)} %pad_maximum_fusion.1.refs_4_), channel_id=1, source_target_pairs={{0,4},{4,0},{8,12},{12,8},{16,20},{20,16},{24,28},{28,24},{1,5},{5... | collective-permute-start | bytes 884744 | tf_op jit(solution)/shard_map/ppermute | solution.py:383
  28.2 4.0 %collective-permute-start.10 = (bf16[2,576,128]{2,1,0:T(8,128)(2,1)S(1)}, bf16[2,576,128]{2,1,0:T(8,128)(2,1)S(1)}, u32[]{:S(2)}, u32[]{:S(2)}) collective-permute-start(bf16[2,576,128]{2,1,0:T(8,128)(2,1)S(1)} %collective-permute-done.6.refs_5_), channel_id=1, source_target_pairs={{0,4},{4,0},{8,12},{12,8},{16,20},{20,16},{24,28},{28,24},{1,5},{5... | collective-permute-start | bytes 884744 | tf_op jit(solution)/shard_map/ppermute | solution.py:383
  28.2 3.9 %collective-permute-start.11 = (bf16[2,576,128]{2,1,0:T(8,128)(2,1)S(1)}, bf16[2,576,128]{2,1,0:T(8,128)(2,1)S(1)}, u32[]{:S(2)}, u32[]{:S(2)}) collective-permute-start(bf16[2,576,128]{2,1,0:T(8,128)(2,1)S(1)} %collective-permute-done.7.refs_6_), channel_id=1, source_target_pairs={{0,4},{4,0},{8,12},{12,8},{16,20},{20,16},{24,28},{28,24},{1,5},{5... | collective-permute-start | bytes 884744 | tf_op jit(solution)/shard_map/ppermute | solution.py:383
  31.7 1.7 %collective-permute-start.12 = (bf16[2,576,128]{2,1,0:T(8,128)(2,1)S(1)}, bf16[2,576,128]{2,1,0:T(8,128)(2,1)}, u32[]{:S(2)}, u32[]{:S(2)}) collective-permute-start(bf16[2,576,128]{2,1,0:T(8,128)(2,1)S(1)} %collective-permute-done.8.refs_7_), channel_id=1, source_target_pairs={{0,4},{4,0},{8,12},{12,8},{16,20},{20,16},{24,28},{28,24},{1,5},{5... | collective-permute-start | bytes 884744 | tf_op jit(solution)/shard_map/ppermute | solution.py:383

commit v3 on v2

--- a/solution.py
+++ b/solution.py
@@ -242,22 +242,46 @@
     )
 
 
-def resident_kernel(
-    mp_ref,
-    scale_ref,
-    *refs,
-    piece_counts,
-    places,
-    mp_count,
-):
-    lead_refs = refs[: piece_counts[0]]
-    rest_refs = refs[piece_counts[0] : sum(piece_counts)]
-    refs = refs[sum(piece_counts) :]
-    row_videos_ref, column_videos_ref, d_clips_ref, d_caps_ref = refs[:4]
-    clips_ref, caps_ref, own_ref, row_lse_ref = refs[4:]
-    total, width = clips_ref.shape
-    rows = own_ref.shape[1]
-    own = d_clips_ref.shape[0]
+def joined_lse(left, right):
+    top = jnp.maximum(left, right)
+    return top + jnp.log2(jnp.exp2(left - top) + jnp.exp2(right - top))
+
+
+def lane_vector(column):
+    return jnp.transpose(jnp.broadcast_to(column, (column.shape[0], 128)))[0:1, :]
+
+
+def add_terms(stat, scores, axis):
+    top = jnp.max(scores, axis=axis, keepdims=True)
+    if stat is not None:
+        top = jnp.maximum(stat[0], top)
+    terms = jnp.sum(jnp.exp2(scores - top), axis=axis, keepdims=True)
+    if stat is not None:
+        terms = terms + stat[1] * jnp.exp2(stat[0] - top)
+    return top, terms
+
+
+def stage_kernel(*refs, piece_counts, places, old_count, mp_count, final):
+    mp_ref, scale_ref, row_videos_ref, column_videos_ref = refs[:4]
+    refs = refs[4:]
+    lead_refs, refs = refs[: piece_counts[0]], refs[piece_counts[0] :]
+    rest_refs, refs = refs[: piece_counts[1]], refs[piece_counts[1] :]
+    old_refs, refs = refs[: 2 * old_count], refs[2 * old_count :]
+    old = [(old_refs[2 * k], old_refs[2 * k + 1]) for k in range(old_count)]
+    if old_count:
+        row_old_ref, col_old_ref, own_ref = refs[:3]
+        refs = refs[3:]
+    if final:
+        d_clips_ref, d_caps_ref, clips_ref, caps_ref = refs
+    elif old_count:
+        clips_ref, caps_ref, row_ref, col_ref = refs
+    else:
+        clips_ref, caps_ref, row_ref, col_ref, own_ref = refs
+    fresh, width = clips_ref.shape
+    rows = fresh // len(places)
+    chunk = width // mp_count
+    start = sum(clips.shape[0] for clips, _ in old)
+    total = start + fresh
     mp_index = mp_ref[0]
     scale = scale_ref[0]
     scale2 = scale * log2_e
@@ -267,7 +291,6 @@
         for kind in range(2):
             lead_ref, lead_at = lead_refs[lead_place[0]], lead_place[1]
             rest_ref, rest_at = rest_refs[rest_place[0]], rest_place[1]
-            chunk = width // mp_count
             raw = jnp.concatenate(
                 [
                     lead_ref[kind, lead_at * chunk : (lead_at + 1) * chunk, :],
@@ -275,7 +298,7 @@
                 ],
                 axis=0,
             )
-            if position == 0:
+            if position == 0 and not old_count:
                 own_ref[kind] = jnp.transpose(raw)
             wide = raw.astype(jnp.float32)
             inverse = 1.0 / jnp.sqrt(jnp.sum(wide * wide, axis=0, keepdims=True) + epsilon)
@@ -285,35 +308,65 @@
             else:
                 caps_ref[:, span] = unit
 
-    row_tile = min(256, total)
-    col_max = jnp.full((1, total), negative_fill, jnp.float32)
-    col_sum = jnp.zeros((1, total), jnp.float32)
-    for row_first in range(0, total, row_tile):
-        span = pl.ds(row_first, row_tile)
-        scores = scale2 * jnp.dot(clips_ref[span, :], caps_ref[...], preferred_element_type=jnp.float32)
-        same = column_videos_ref[span, :] == row_videos_ref[...]
-        distance = lax.broadcasted_iota(jnp.int32, scores.shape, 1) - lax.broadcasted_iota(
-            jnp.int32, scores.shape, 0
-        )
-        scores = jnp.where(same & (distance != row_first), negative_fill, scores)
-        row_max = jnp.max(scores, axis=1, keepdims=True)
-        row_sum = jnp.sum(jnp.exp2(scores - row_max), axis=1, keepdims=True)
-        new_col = jnp.maximum(col_max, jnp.max(scores, axis=0, keepdims=True))
-        col_sum = col_sum * jnp.exp2(col_max - new_col) + jnp.sum(
-            jnp.exp2(scores - new_col), axis=0, keepdims=True
-        )
-        col_max = new_col
-        row_lse_ref[:, span] = jnp.transpose(
-            jnp.broadcast_to(row_max + jnp.log2(row_sum), (row_tile, 128))
-        )[:8, :]
-    col_lse = col_max + jnp.log2(col_sum)
-    row_lse = row_lse_ref[0:1, :]
-
+    def tile(clip_tile, row_first, caps, col_first):
+        size = (clip_tile.shape[0], caps.shape[1])
+        scores = scale2 * jnp.dot(clip_tile, caps[...], preferred_element_type=jnp.float32)
+        banned = (
+            column_videos_ref[row_first : row_first + size[0], :]
+            == row_videos_ref[:, col_first : col_first + size[1]]
+        )
+        if col_first <= row_first < col_first + size[1]:
+            distance = lax.broadcasted_iota(jnp.int32, size, 1) - lax.broadcasted_iota(jnp.int32, size, 0)
+            banned = banned & (distance != row_first - col_first)
+        return jnp.where(banned, negative_fill, scores)
+
+    row_tile = min(2 * rows, fresh)
+    row_parts = []
+    col_new = None
+    at = 0
+    for clips, _ in old:
+        for first in range(0, clips.shape[0], row_tile):
+            scores = tile(clips[first : first + row_tile, :], at + first, caps_ref, start)
+            top, terms = add_terms(None, scores, 1)
+            col_new = add_terms(col_new, scores, 0)
+            row_parts.append(lane_vector(top + jnp.log2(terms)))
+        at += clips.shape[0]
+    col_olds = [None] * old_count
+    row_news = []
+    for first in range(0, fresh, row_tile):
+        stat = None
+        clip_tile = clips_ref[first : first + row_tile, :]
+        at = 0
+        for k, (clips, caps) in enumerate(old):
+            scores = tile(clip_tile, start + first, caps, at)
+            stat = add_terms(stat, scores, 1)
+            col_olds[k] = add_terms(col_olds[k], scores, 0)
+            at += clips.shape[0]
+        scores = tile(clip_tile, start + first, caps_ref, start)
+        top, terms = add_terms(stat, scores, 1)
+        col_new = add_terms(col_new, scores, 0)
+        row_news.append(lane_vector(top + jnp.log2(terms)))
+    row_lse = row_news
+    col_lse = [col_new[0] + jnp.log2(col_new[1])]
+    if old_count:
+        old_part = jnp.concatenate(row_parts, axis=1)
+        row_lse = [joined_lse(row_old_ref[...], old_part)] + row_lse
+        old_part = jnp.concatenate([top + jnp.log2(terms) for top, terms in col_olds], axis=1)
+        col_lse = [joined_lse(col_old_ref[...], old_part)] + col_lse
+    row_lse = jnp.concatenate(row_lse, axis=1)
+    col_lse = jnp.concatenate(col_lse, axis=1)
+    if not final:
+        row_ref[...] = row_lse
+        col_ref[...] = col_lse
+        return
+
+    own = d_clips_ref.shape[0]
+    every = old + [(clips_ref, caps_ref)]
     own_first = pl.multiple_of(mp_index * own, own)
     own_rows = pl.ds(own_first, own)
     clip_float, clip_length = unit_rows(own_ref[0, own_rows, :])
     cap_float, cap_length = unit_rows(own_ref[1, own_rows, :])
-    clip_unit = clips_ref[own_rows, :]
+    clip_unit = old[0][0][own_rows, :]
     cap_unit = cap_float.astype(jnp.bfloat16)
     same = column_videos_ref[own_rows, :] == row_videos_ref[...]
     distance = lax.broadcasted_iota(jnp.int32, (own, total), 1) - lax.broadcasted_iota(
@@ -324,20 +377,34 @@
     last = (((1,), (1,)), ((), ()))
 
     def strip(products, other_lse):
-        scores = jnp.where(blocked, negative_fill, scale2 * products)
-        top = jnp.max(scores, axis=1, keepdims=True)
-        own_lse = top + jnp.log2(jnp.sum(jnp.exp2(scores - top), axis=1, keepdims=True))
-        weights = 0.5 * (jnp.exp2(scores - own_lse) + jnp.exp2(scores - other_lse))
+        scores = jnp.where(blocked, negative_fill, scale2 * jnp.concatenate(products, axis=1))
+        top, terms = add_terms(None, scores, 1)
+        weights = 0.5 * (jnp.exp2(scores - (top + jnp.log2(terms))) + jnp.exp2(scores - other_lse))
         return jnp.concatenate([weights.astype(jnp.bfloat16), same], axis=0)
 
-    clip_products = jnp.dot(clip_unit, caps_ref[...], preferred_element_type=jnp.float32)
-    cap_products = lax.dot_general(cap_unit, clips_ref[...], last, preferred_element_type=jnp.float32)
-    clip_sums = lax.dot_general(
-        strip(clip_products, col_lse), caps_ref[...], last, preferred_element_type=jnp.float32
-    )
-    cap_sums = jnp.dot(strip(cap_products, row_lse), clips_ref[...], preferred_element_type=jnp.float32)
-    clip_acc, caption_pool = clip_sums[:own], clip_sums[own:]
-    cap_acc, pooled = cap_sums[:own], cap_sums[own:]
+    def summed(weights, multiply):
+        at, result = 0, None
+        for clips, caps in every:
+            part = multiply(weights[:, at : at + clips.shape[0]], clips, caps)
+            result = part if result is None else result + part
+            at += clips.shape[0]
+        return result[:own], result[own:]
+
+    clip_products = [
+        jnp.dot(clip_unit, caps[...], preferred_element_type=jnp.float32) for _, caps in every
+    ]
+    cap_products = [
+        lax.dot_general(cap_unit, clips[...], last, preferred_element_type=jnp.float32)
+        for clips, _ in every
+    ]
+    clip_acc, caption_pool = summed(
+        strip(clip_products, col_lse),
+        lambda w, clips, caps: lax.dot_general(w, caps[...], last, preferred_element_type=jnp.float32),
+    )
+    cap_acc, pooled = summed(
+        strip(cap_products, row_lse),
+        lambda w, clips, caps: jnp.dot(w, clips[...], preferred_element_type=jnp.float32),
+    )
     pool_length = jnp.sqrt(jnp.sum(pooled * pooled, axis=1, keepdims=True) + epsilon)
     pool_unit = pooled / pool_length
     projected = caption_pool - pool_unit * jnp.sum(pool_unit * caption_pool, axis=1, keepdims=True)
@@ -350,7 +417,6 @@
 
     def finish(unit, length, grad, out_ref):
         result = (grad - unit * jnp.sum(unit * grad, axis=1, keepdims=True)) / length
-        chunk = width // mp_count
         for index in range(mp_count):
 
             @pl.when(mp_index == index)
@@ -370,7 +436,6 @@
     row_count = clips.shape[0]
     own = row_count // mp_count
     width = clips.shape[1] * mp_count
-    total = row_count * dp_count
     dp_index = lax.axis_index("dp")
     mp_index = lax.axis_index("mp")
     even, odd = gather_orders(dp_count)
@@ -381,6 +446,56 @@
 
     def across(block):
         return lax.ppermute(block, "dp", [(i, i ^ 1) for i in range(dp_count)])
+
+    reached = [(0, 0), (even[0], odd[0]), (even[1], odd[1]), (even[0] ^ even[1], odd[0] ^ odd[1])]
+    crossed = [(b ^ 1, a ^ 1) for a, b in reached]
+    ordered = [reached[0], crossed[0], reached[1], reached[2], crossed[1], crossed[2], reached[3], crossed[3]]
+    videos = []
+    for even_offset, odd_offset in ordered:
+        block = dp_index ^ jnp.where(dp_index & 1, odd_offset, even_offset)
+        videos.append(lax.dynamic_slice_in_dim(video_id, block * row_count, row_count, 0))
+    videos = jnp.concatenate(videos)
+    common = (
+        jnp.reshape(mp_index, (1,)).astype(jnp.int32),
+        jnp.reshape(logit_scale, (1,)),
+        videos[None, :],
+        videos[:, None],
+    )
+    vmem = pl.BlockSpec(memory_space=pltpu.VMEM)
+    smem = pl.BlockSpec(memory_space=pltpu.SMEM)
+
+    def stage(leads, rests, places, old, carried, final=False):
+        fresh = len(places) * row_count
+        total = fresh + sum(clips.shape[0] for clips, _ in old)
+        units = [((fresh, width), jnp.bfloat16), ((width, fresh), jnp.bfloat16)]
+        scratch = []
+        if final:
+            outs = [((own, width), jnp.float32)] * 2
+            scratch = [pltpu.VMEM(*unit) for unit in units]
+        else:
+            outs = units + [((1, total), jnp.float32)] * 2
+            if not old:
+                outs = outs + [((2, row_count, width), jnp.bfloat16)]
+        operands = [*common, *leads, *rests, *[unit for pair in old for unit in pair], *carried]
+        score_count = (2 * total - fresh) * fresh
+        return pl.pallas_call(
+            functools.partial(
+                stage_kernel,
+                piece_counts=(len(leads), len(rests)),
+                places=places,
+                old_count=len(old),
+                mp_count=mp_count,
+                final=final,
+            ),
+            out_shape=[jax.ShapeDtypeStruct(*out) for out in outs],
+            in_specs=[smem, smem] + [vmem] * (len(operands) - 2),
+            out_specs=[vmem] * len(outs),
+            scratch_shapes=scratch,
+            cost_estimate=pl.CostEstimate(
+                flops=2 * score_count * width, bytes_accessed=8 * fresh * width, transcendentals=2 * score_count
+            ),
+            compiler_params=pltpu.CompilerParams(vmem_limit_bytes=32 * 1024 * 1024),
+        )(*operands)
 
     lead = jnp.stack([clips.T, captions.T])
     lead_first = along(0, lead)
@@ -391,53 +506,30 @@
     rest = jnp.concatenate(arrived, axis=1)
     rest, lead_second = lax.optimization_barrier((rest, lead_second))
     rest_first = along(0, rest)
+    lead_other = across(jnp.concatenate([lead, lead_first, lead_second], axis=1))
+    rest_other = across(rest)
+    clips_a, caps_a, row_a, col_a, own_raw = stage(
+        [lead, lead_other], [rest, rest_other], [((0, 0), (0, 0)), ((1, 0), (1, 0))], [], []
+    )
+    rest, row_a = lax.optimization_barrier((rest, row_a))
     rest_second = along(1, rest)
     rest_third = along(1, rest_first)
-    lead_other = across(jnp.concatenate([lead, lead_first, lead_second], axis=1))
-    rest_held = [rest, rest_first, rest_second, rest_third]
-    leads = [lead, lead_first, lead_second, lead_other]
-    rests = rest_held + [across(piece) for piece in rest_held]
-    places = [((0, 0), (0, 0)), ((1, 0), (1, 0)), ((2, 0), (2, 0)), ((2, 1), (3, 0))]
-    places += [((3, p), (4 + p, 0)) for p in range(4)]
-
-    offsets = [[0, even[0], even[1], even[0] ^ even[1]], [0, odd[0], odd[1], odd[0] ^ odd[1]]]
-    offsets = [
-        offsets[0] + [o ^ 1 for o in offsets[1]],
-        offsets[1] + [o ^ 1 for o in offsets[0]],
-    ]
-    videos = []
-    for even_offset, odd_offset in zip(*offsets):
-        block = dp_index ^ jnp.where(dp_index & 1, odd_offset, even_offset)
-        videos.append(lax.dynamic_slice_in_dim(video_id, block * row_count, row_count, 0))
-    videos = jnp.concatenate(videos)
-
-    vmem = pl.BlockSpec(memory_space=pltpu.VMEM)
-    smem = pl.BlockSpec(memory_space=pltpu.SMEM)
-    out = jax.ShapeDtypeStruct((own, width), jnp.float32)
-    return pl.pallas_call(
-        functools.partial(
-            resident_kernel,
-            piece_counts=(len(leads), len(rests)),
-            places=places,
-            mp_count=mp_count,
-        ),
-        out_shape=(out, out),
-        in_specs=[smem, smem] + [vmem] * (len(leads) + len(rests) + 2),
-        out_specs=(vmem, vmem),
-        scratch_shapes=[
-            pltpu.VMEM((total, width), jnp.bfloat16),
-            pltpu.VMEM((width, total), jnp.bfloat16),
-            pltpu.VMEM((2, row_count, width), jnp.bfloat16),
-            pltpu.VMEM((8, total), jnp.float32),
-        ],
-        compiler_params=pltpu.CompilerParams(vmem_limit_bytes=40 * 1024 * 1024),
-    )(
-        jnp.reshape(mp_index, (1,)).astype(jnp.int32),
-        jnp.reshape(logit_scale, (1,)),
-        *leads,
-        *rests,
-        videos[None, :],
-        videos[:, None],
+    clips_b, caps_b, row_b, col_b = stage(
+        [lead_first, lead_second, lead_other],
+        [rest_first, rest_second, across(rest_first), across(rest_second)],
+        [((0, 0), (0, 0)), ((1, 0), (1, 0)), ((2, 1), (2, 0)), ((2, 2), (3, 0))],
+        [(clips_a, caps_a)],
+        [row_a, col_a, own_raw],
+    )
+    return tuple(
+        stage(
+            [lead_second, lead_other],
+            [rest_third, across(rest_third)],
+            [((0, 1), (0, 0)), ((1, 3), (1, 0))],
+            [(clips_a, caps_a), (clips_b, caps_b)],
+            [row_b, col_b, own_raw],
+            final=True,
+        )
     )
 
 

time: 40.6 us -> 39.3 us (0.968)
  waiting for transfers between devices: 15.6 us -> 13.2 us
  starting transfers between devices: 13.8 us -> 16 us
  other arithmetic: 1.68 us -> 0.9 us
    ppermute x3, waiting for transfers between devices: 4.9 us -> 1.31 us  [resident_body(): lax.ppermute(lead, 'mp', [(i, i ^ k) for i in range(mp_count)])]
    ppermute x5, waiting for transfers between devices: 9.45 us -> 11.9 us  [along(): return lax.ppermute(block, 'dp', route)]
    ppermute x3, starting transfers between devices: 4.39 us -> 5.68 us  [resident_body(): lax.ppermute(lead, 'mp', [(i, i ^ k) for i in range(mp_count)])]
    ppermute x5, waiting for transfers between devices: 1.21 us -> 0.01 us  [across(): return lax.ppermute(block, 'dp', [(i, i ^ 1) for i in range(dp_count)])]
    ppermute x5, starting transfers between devices: 8.44 us -> 9.47 us  [along(): return lax.ppermute(block, 'dp', route)]
    concatenate x1, other arithmetic: 0.77 us -> 0.03 us  [resident_body(): jnp.concatenate([lead, lead_first, lead_second], axis=1)]
    pallas_call x1 -> x3, Pallas kernels: 6.99 us -> 6.75 us  [stage(): pl.pallas_call(functools.partial(stage_kernel, piece_counts=(len(leads),...]
  transfers between devices with their start and end apart: 13 -> 13, of which waited for: 5 -> 6; matrix products, arithmetic and copies ran while one was open for 4% -> 2% of each run, Pallas kernels for 0% -> 7%
where the time goes in v3:
time: 39.3 us; the launch traced here: 39.1 us
  starting transfers between devices  16 us (41%)
  waiting for transfers between devices  13.2 us (34%)
  Pallas kernels  6.75 us (17%)
  between operations  1.37 us (3%)
  other arithmetic  0.9 us (2%)
  local copies, waits for them, and re-layouts  0.86 us (2%)
    ppermute x5, waiting for transfers between devices, along(): return lax.ppermute(block, 'dp', route)  11.9 us
    ppermute x5, starting transfers between devices, along(): return lax.ppermute(block, 'dp', route)  9.47 us
    pallas_call x3, Pallas kernels, stage(): pl.pallas_call(functools.partial(stage_kernel, piece_counts=(len(leads),...  6.75 us
    ppermute x3, starting transfers between devices, resident_body(): lax.ppermute(lead, 'mp', [(i, i ^ k) for i in range(mp_count)])  5.68 us
    ppermute x3, waiting for transfers between devices, resident_body(): lax.ppermute(lead, 'mp', [(i, i ^ k) for i in range(mp_count)])  1.31 us
    ppermute x5, starting transfers between devices, across(): return lax.ppermute(block, 'dp', [(i, i ^ 1) for i in range(dp_count)])  0.85 us
    another operation x1, other arithmetic, resident_body(): lead = jnp.stack([clips.T, captions.T])  0.84 us
  transfers between devices with their start and end apart: 13, of which 6 were waited for; matrix products, arithmetic and copies ran while one was open for 2% of the time, Pallas kernels for 7%

profile of v3, /device:TPU:0, one launch (start us, length us, event | category | flops | bytes accessed | tf_op | source)
XLA Modules:
  0.0 39.1 jit_solution(15041816698791580699)
XLA Ops:
  0.6 0.0 copy-start.2
  0.6 0.8 %pad_maximum_fusion.3.refs_4_ = bf16[2,192,128]{2,1,0:T(8,128)(2,1)S(1)} fusion(bf16[1,192,128]{2,1,0:T(8,128)(2,1)} %bitcast.17, bf16[1,192,128]{2,1,0:T(8,128)(2,1)} %bitcast.20), kind=kLoop, calls=%fused_computation.3 | loop fusion | flops 49152 | bytes 196608 | tf_op jit(solution)/shard_map/stack | solution.py:500
  1.5 3.1 %collective-permute-start = (bf16[2,192,128]{2,1,0:T(8,128)(2,1)S(1)}, bf16[2,192,128]{2,1,0:T(8,128)(2,1)S(1)}, u32[]{:S(2)}, u32[]{:S(2)}) collective-permute-start(bf16[2,192,128]{2,1,0:T(8,128)(2,1)S(1)} %pad_maximum_fusion.3.refs_4_), channel_id=1, source_target_pairs={{0,1},{1,0},{2,3},{3,2},{4,5},{5,4},{6,7},{7,6},{8,9},{9,8},{10,11... | collective-permute-start | bytes 294920 | tf_op jit(solution)/shard_map/ppermute | solution.py:503
  4.6 2.6 %collective-permute-start.1 = (bf16[2,192,128]{2,1,0:T(8,128)(2,1)S(1)}, bf16[2,192,128]{2,1,0:T(8,128)(2,1)S(1)}, u32[]{:S(2)}, u32[]{:S(2)}) collective-permute-start(bf16[2,192,128]{2,1,0:T(8,128)(2,1)S(1)} %pad_maximum_fusion.3.refs_4_), channel_id=1, source_target_pairs={{0,2},{1,3},{2,0},{3,1},{4,6},{5,7},{6,4},{7,5},{8,10},{9,11},{10,... | collective-permute-start | bytes 294920 | tf_op jit(solution)/shard_map/ppermute | solution.py:503
  7.2 0.0 collective-permute-start.2
  7.2 1.7 %collective-permute-start.3 = (bf16[2,192,128]{2,1,0:T(8,128)(2,1)S(1)}, bf16[2,192,128]{2,1,0:T(8,128)(2,1)S(1)}, u32[]{:S(2)}, u32[]{:S(2)}) collective-permute-start(bf16[2,192,128]{2,1,0:T(8,128)(2,1)S(1)} %pad_maximum_fusion.3.refs_4_), channel_id=1, source_target_pairs={{0,8},{4,20},{8,0},{12,28},{16,24},{20,4},{24,16},{28,12},{1,9},{5... | collective-permute-start | bytes 294920 | tf_op jit(solution)/shard_map/ppermute | solution.py:445
  8.9 0.0 copy-start.1
  8.9 0.0 copy-start
  8.9 0.0 copy-done.2
  8.9 0.1 constant_dynamic-update-slice_fusion.7
  9.0 0.1 constant_dynamic-update-slice_fusion.6
  9.0 0.1 constant_dynamic-update-slice_fusion.5
  9.1 2.7 %collective-permute-done.3.refs_4_ = bf16[2,192,128]{2,1,0:T(8,128)(2,1)S(1)} collective-permute-done((bf16[2,192,128]{2,1,0:T(8,128)(2,1)S(1)}, bf16[2,192,128]{2,1,0:T(8,128)(2,1)S(1)}, u32[]{:S(2)}, u32[]{:S(2)}) %collective-permute-start.3) | collective-permute-done | bytes 98336 | tf_op jit(solution)/shard_map/ppermute | solution.py:445
  11.8 0.0 copy-done.1
  11.8 0.0 copy-done
  11.8 1.8 %collective-permute-start.4 = (bf16[2,384,128]{2,1,0:T(8,128)(2,1)S(1)}, bf16[2,384,128]{2,1,0:T(8,128)(2,1)S(1)}, u32[]{:S(2)}, u32[]{:S(2)}) collective-permute-start(bf16[2,384,128]{2,1,0:T(8,128)(2,1)S(1)} %pad_maximum_fusion.2), channel_id=1, source_target_pairs={{0,16},{4,12},{8,24},{12,4},{16,0},{20,28},{24,8},{28,20},{1,17},{... | collective-permute-start | bytes 589832 | tf_op jit(solution)/shard_map/ppermute | solution.py:445
  13.6 0.1 constant_dynamic-update-slice_fusion.4
  13.7 0.0 collective-permute-done
  13.7 1.3 %collective-permute-done.1 = bf16[2,192,128]{2,1,0:T(8,128)(2,1)S(1)} collective-permute-done((bf16[2,192,128]{2,1,0:T(8,128)(2,1)S(1)}, bf16[2,192,128]{2,1,0:T(8,128)(2,1)S(1)}, u32[]{:S(2)}, u32[]{:S(2)}) %collective-permute-start.1) | collective-permute-done | bytes 98336 | tf_op jit(solution)/shard_map/ppermute | solution.py:503
  15.0 0.0 collective-permute-done.2
  15.0 2.5 %collective-permute-done.4.refs_5_.refs_4_ = bf16[2,384,128]{2,1,0:T(8,128)(2,1)S(1)} collective-permute-done((bf16[2,384,128]{2,1,0:T(8,128)(2,1)S(1)}, bf16[2,384,128]{2,1,0:T(8,128)(2,1)S(1)}, u32[]{:S(2)}, u32[]{:S(2)}) %collective-permute-start.4) | collective-permute-done | bytes 196640 | tf_op jit(solution)/shard_map/ppermute | solution.py:445
  17.6 0.1 collective-permute-start.5
  17.6 0.1 constant_dynamic-update-slice_fusion.3
  17.7 0.5 %collective-permute-start.9 = (bf16[2,576,128]{2,1,0:T(8,128)(2,1)S(1)}, bf16[2,576,128]{2,1,0:T(8,128)(2,1)S(1)}, u32[]{:S(2)}, u32[]{:S(2)}) collective-permute-start(bf16[2,576,128]{2,1,0:T(8,128)(2,1)S(1)} %pad_maximum_fusion.1.refs_6_), channel_id=1, source_target_pairs={{0,4},{4,0},{8,12},{12,8},{16,20},{20,16},{24,28},{28,24},{1,5},{5... | collective-permute-start | bytes 884744 | tf_op jit(solution)/shard_map/ppermute | solution.py:448
  18.2 0.1 constant_dynamic-update-slice_fusion.2
  18.3 1.7 %collective-permute-start.6 = (bf16[2,576,128]{2,1,0:T(8,128)(2,1)S(1)}, bf16[2,576,128]{2,1,0:T(8,128)(2,1)S(1)}, u32[]{:S(2)}, u32[]{:S(2)}) collective-permute-start(bf16[2,576,128]{2,1,0:T(8,128)(2,1)S(1)} %pad_maximum_fusion.1.refs_6_), channel_id=1, source_target_pairs={{0,8},{4,20},{8,0},{12,28},{16,24},{20,4},{24,16},{28,12},{1,9},{5... | collective-permute-start | bytes 884744 | tf_op jit(solution)/shard_map/ppermute | solution.py:445
  20.0 0.1 constant_dynamic-update-slice_fusion.1
  20.1 0.1 constant_dynamic-update-slice_fusion
  20.2 0.2 copy.8.refs_3_
  21.1 0.0 collective-permute-done.9.refs_7_
  21.1 0.0 collective-permute-done.5.refs_5_.refs_6_
  21.1 0.8 %shard_map.59 = (bf16[256,768]{1,0:T(8,128)(2,1)S(1)}, bf16[768,256]{1,0:T(8,128)(2,1)S(1)}, f32[1,256]{1,0:T(1,128)S(1)}, f32[1,256]{1,0:T(1,128)S(1)}, bf16[2,128,768]{2,1,0:T(8,128)(2,1)S(1)}) custom-call(s32[1]{0:T(128)} %bitcast.refs_0_, f32[1]{0:T(128)} %bitcast.10.refs_1_, s32[1,1024]{1,0:T(1,128)S(1)} %bitcast.14, s32[1024,1]{1,0:T(8,128)S(1)} %copy.8.refs_3_, ...), custom_call_target="tpu_custom_call" | custom-call | flops 100663296 | bytes 1572864 | tf_op jit(solution)/shard_map/pallas_call | solution.py:481
  21.9 1.6 %collective-permute-start.10 = (bf16[2,576,128]{2,1,0:T(8,128)(2,1)S(1)}, bf16[2,576,128]{2,1,0:T(8,128)(2,1)S(1)}, u32[]{:S(2)}, u32[]{:S(2)}) collective-permute-start(bf16[2,576,128]{2,1,0:T(8,128)(2,1)S(1)} %pad_maximum_fusion.1.refs_6_), channel_id=1, source_target_pairs={{0,16},{4,12},{8,24},{12,4},{16,0},{20,28},{24,8},{28,20},{1,17},{... | collective-permute-start | bytes 884744 | tf_op jit(solution)/shard_map/ppermute | solution.py:445
  23.4 2.3 %collective-permute-done.6.refs_7_ = bf16[2,576,128]{2,1,0:T(8,128)(2,1)S(1)} collective-permute-done((bf16[2,576,128]{2,1,0:T(8,128)(2,1)S(1)}, bf16[2,576,128]{2,1,0:T(8,128)(2,1)S(1)}, u32[]{:S(2)}, u32[]{:S(2)}) %collective-permute-start.6) | collective-permute-done | bytes 294944 | tf_op jit(solution)/shard_map/ppermute | solution.py:445
  25.7 2.7 %collective-permute-start.7 = (bf16[2,576,128]{2,1,0:T(8,128)(2,1)S(1)}, bf16[2,576,128]{2,1,0:T(8,128)(2,1)S(1)}, u32[]{:S(2)}, u32[]{:S(2)}) collective-permute-start(bf16[2,576,128]{2,1,0:T(8,128)(2,1)S(1)} %collective-permute-done.6.refs_7_), channel_id=1, source_target_pairs={{0,16},{4,12},{8,24},{12,4},{16,0},{20,28},{24,8},{28,20},{1,17},{... | collective-permute-start | bytes 884744 | tf_op jit(solution)/shard_map/ppermute | solution.py:445
  28.4 0.0 collective-permute-start.11
  28.4 0.2 collective-permute-done.10.refs_8_
  28.6 0.3 collective-permute-start.12
  28.9 4.2 %collective-permute-done.7.refs_6_ = bf16[2,576,128]{2,1,0:T(8,128)(2,1)S(1)} collective-permute-done((bf16[2,576,128]{2,1,0:T(8,128)(2,1)S(1)}, bf16[2,576,128]{2,1,0:T(8,128)(2,1)S(1)}, u32[]{:S(2)}, u32[]{:S(2)}) %collective-permute-start.7) | collective-permute-done | bytes 294944 | tf_op jit(solution)/shard_map/ppermute | solution.py:445
  33.1 0.0 collective-permute-start.8
  33.1 0.0 collective-permute-done.11.refs_9_
  33.1 0.0 collective-permute-done.12.refs_10_
  33.1 2.1 %shard_map.60 = (bf16[512,768]{1,0:T(8,128)(2,1)S(1)}, bf16[768,512]{1,0:T(8,128)(2,1)S(1)}, f32[1,768]{1,0:T(1,128)S(1)}, f32[1,768]{1,0:T(1,128)S(1)}) custom-call(s32[1]{0:T(128)} %bitcast.refs_0_, f32[1]{0:T(128)} %bitcast.11.refs_1_, s32[1,1024]{1,0:T(1,128)S(1)} %bitcast.15, s32[1024,1]{1,0:T(8,128)S(1)} %copy.8.refs_3_, ...), custom_call_target="tpu_custom_call" | custom-call | flops 805306368 | bytes 3145728 | tf_op jit(solution)/shard_map/pallas_call | solution.py:481
  35.2 0.0 collective-permute-done.8.refs_7_
  35.2 3.9 %shard_map.61 = (f32[32,768]{1,0:T(8,128)}, f32[32,768]{1,0:T(8,128)}) custom-call(s32[1]{0:T(128)} %bitcast.refs_0_, f32[1]{0:T(128)} %bitcast.12.refs_1_, s32[1,1024]{1,0:T(1,128)S(1)} %bitcast.16, s32[1024,1]{1,0:T(8,128)S(1)} %copy.8.refs_3_, bf16[2,384,128]{2,1,0:T(8,128)(2,1)S(1)} %collective-permute-done.4.refs_5_.refs_4_, ...), custom_call_target="tpu_custom_call" | custom-call | flops 704643072 | bytes 1572864 | tf_op jit(solution)/shard_map/pallas_call | solution.py:481
  (4 shorter events, 0.1 us)
Async XLA Ops:
  0.6 8.3 %copy-start.2 = (s32[1024]{0:T(1024)S(1)}, s32[1024]{0:T(1024)}, u32[]{:S(2)}) copy-start(s32[1024]{0:T(1024)} %param.6) | copy-start | bytes 12292
  1.5 12.2 %collective-permute-start = (bf16[2,192,128]{2,1,0:T(8,128)(2,1)S(1)}, bf16[2,192,128]{2,1,0:T(8,128)(2,1)S(1)}, u32[]{:S(2)}, u32[]{:S(2)}) collective-permute-start(bf16[2,192,128]{2,1,0:T(8,128)(2,1)S(1)} %pad_maximum_fusion.3.refs_4_), channel_id=1, source_target_pairs={{0,1},{1,0},{2,3},{3,2},{4,5},{5,4},{6,7},{7,6},{8,9},{9,8},{10,11... | collective-permute-start | bytes 294920 | tf_op jit(solution)/shard_map/ppermute | solution.py:503
  4.6 10.4 %collective-permute-start.1 = (bf16[2,192,128]{2,1,0:T(8,128)(2,1)S(1)}, bf16[2,192,128]{2,1,0:T(8,128)(2,1)S(1)}, u32[]{:S(2)}, u32[]{:S(2)}) collective-permute-start(bf16[2,192,128]{2,1,0:T(8,128)(2,1)S(1)} %pad_maximum_fusion.3.refs_4_), channel_id=1, source_target_pairs={{0,2},{1,3},{2,0},{3,1},{4,6},{5,7},{6,4},{7,5},{8,10},{9,11},{10,... | collective-permute-start | bytes 294920 | tf_op jit(solution)/shard_map/ppermute | solution.py:503
  7.2 7.8 %collective-permute-start.2 = (bf16[2,192,128]{2,1,0:T(8,128)(2,1)S(1)}, bf16[2,192,128]{2,1,0:T(8,128)(2,1)S(1)}, u32[]{:S(2)}, u32[]{:S(2)}) collective-permute-start(bf16[2,192,128]{2,1,0:T(8,128)(2,1)S(1)} %pad_maximum_fusion.3.refs_4_), channel_id=1, source_target_pairs={{0,3},{1,2},{2,1},{3,0},{4,7},{5,6},{6,5},{7,4},{8,11},{9,10},{10,... | collective-permute-start | bytes 294920 | tf_op jit(solution)/shard_map/ppermute | solution.py:503
  7.2 4.6 %collective-permute-start.3 = (bf16[2,192,128]{2,1,0:T(8,128)(2,1)S(1)}, bf16[2,192,128]{2,1,0:T(8,128)(2,1)S(1)}, u32[]{:S(2)}, u32[]{:S(2)}) collective-permute-start(bf16[2,192,128]{2,1,0:T(8,128)(2,1)S(1)} %pad_maximum_fusion.3.refs_4_), channel_id=1, source_target_pairs={{0,8},{4,20},{8,0},{12,28},{16,24},{20,4},{24,16},{28,12},{1,9},{5... | collective-permute-start | bytes 294920 | tf_op jit(solution)/shard_map/ppermute | solution.py:445
  8.9 2.9 %copy-start.1 = (bf16[128,192]{0,1:T(8,128)(2,1)S(1)}, bf16[128,192]{0,1:T(8,128)(2,1)}, u32[]{:S(2)}) copy-start(bf16[128,192]{0,1:T(8,128)(2,1)} %param.4) | copy-start | bytes 147460
  8.9 2.9 %copy-start = (bf16[128,192]{0,1:T(8,128)(2,1)S(1)}, bf16[128,192]{0,1:T(8,128)(2,1)}, u32[]{:S(2)}) copy-start(bf16[128,192]{0,1:T(8,128)(2,1)} %param.5) | copy-start | bytes 147460
  11.8 5.7 %collective-permute-start.4 = (bf16[2,384,128]{2,1,0:T(8,128)(2,1)S(1)}, bf16[2,384,128]{2,1,0:T(8,128)(2,1)S(1)}, u32[]{:S(2)}, u32[]{:S(2)}) collective-permute-start(bf16[2,384,128]{2,1,0:T(8,128)(2,1)S(1)} %pad_maximum_fusion.2), channel_id=1, source_target_pairs={{0,16},{4,12},{8,24},{12,4},{16,0},{20,28},{24,8},{28,20},{1,17},{... | collective-permute-start | bytes 589832 | tf_op jit(solution)/shard_map/ppermute | solution.py:445
  17.6 3.5 %collective-permute-start.5 = (bf16[2,768,128]{2,1,0:T(8,128)(2,1)S(1)}, bf16[2,768,128]{2,1,0:T(8,128)(2,1)S(1)}, u32[]{:S(2)}, u32[]{:S(2)}) collective-permute-start(bf16[2,768,128]{2,1,0:T(8,128)(2,1)S(1)} %pad_maximum_fusion), channel_id=1, source_target_pairs={{0,4},{4,0},{8,12},{12,8},{16,20},{20,16},{24,28},{28,24},{1,5},{5... | collective-permute-start | bytes 1179656 | tf_op jit(solution)/shard_map/ppermute | solution.py:448
  17.7 3.3 %collective-permute-start.9 = (bf16[2,576,128]{2,1,0:T(8,128)(2,1)S(1)}, bf16[2,576,128]{2,1,0:T(8,128)(2,1)S(1)}, u32[]{:S(2)}, u32[]{:S(2)}) collective-permute-start(bf16[2,576,128]{2,1,0:T(8,128)(2,1)S(1)} %pad_maximum_fusion.1.refs_6_), channel_id=1, source_target_pairs={{0,4},{4,0},{8,12},{12,8},{16,20},{20,16},{24,28},{28,24},{1,5},{5... | collective-permute-start | bytes 884744 | tf_op jit(solution)/shard_map/ppermute | solution.py:448
  18.3 7.4 %collective-permute-start.6 = (bf16[2,576,128]{2,1,0:T(8,128)(2,1)S(1)}, bf16[2,576,128]{2,1,0:T(8,128)(2,1)S(1)}, u32[]{:S(2)}, u32[]{:S(2)}) collective-permute-start(bf16[2,576,128]{2,1,0:T(8,128)(2,1)S(1)} %pad_maximum_fusion.1.refs_6_), channel_id=1, source_target_pairs={{0,8},{4,20},{8,0},{12,28},{16,24},{20,4},{24,16},{28,12},{1,9},{5... | collective-permute-start | bytes 884744 | tf_op jit(solution)/shard_map/ppermute | solution.py:445
  21.9 6.8 %collective-permute-start.10 = (bf16[2,576,128]{2,1,0:T(8,128)(2,1)S(1)}, bf16[2,576,128]{2,1,0:T(8,128)(2,1)S(1)}, u32[]{:S(2)}, u32[]{:S(2)}) collective-permute-start(bf16[2,576,128]{2,1,0:T(8,128)(2,1)S(1)} %pad_maximum_fusion.1.refs_6_), channel_id=1, source_target_pairs={{0,16},{4,12},{8,24},{12,4},{16,0},{20,28},{24,8},{28,20},{1,17},{... | collective-permute-start | bytes 884744 | tf_op jit(solution)/shard_map/ppermute | solution.py:445
  25.7 7.4 %collective-permute-start.7 = (bf16[2,576,128]{2,1,0:T(8,128)(2,1)S(1)}, bf16[2,576,128]{2,1,0:T(8,128)(2,1)S(1)}, u32[]{:S(2)}, u32[]{:S(2)}) collective-permute-start(bf16[2,576,128]{2,1,0:T(8,128)(2,1)S(1)} %collective-permute-done.6.refs_7_), channel_id=1, source_target_pairs={{0,16},{4,12},{8,24},{12,4},{16,0},{20,28},{24,8},{28,20},{1,17},{... | collective-permute-start | bytes 884744 | tf_op jit(solution)/shard_map/ppermute | solution.py:445
  28.4 4.7 %collective-permute-start.11 = (bf16[2,576,128]{2,1,0:T(8,128)(2,1)S(1)}, bf16[2,576,128]{2,1,0:T(8,128)(2,1)S(1)}, u32[]{:S(2)}, u32[]{:S(2)}) collective-permute-start(bf16[2,576,128]{2,1,0:T(8,128)(2,1)S(1)} %collective-permute-done.6.refs_7_), channel_id=1, source_target_pairs={{0,4},{4,0},{8,12},{12,8},{16,20},{20,16},{24,28},{28,24},{1,5},{5... | collective-permute-start | bytes 884744 | tf_op jit(solution)/shard_map/ppermute | solution.py:448
  28.6 4.5 %collective-permute-start.12 = (bf16[2,576,128]{2,1,0:T(8,128)(2,1)S(1)}, bf16[2,576,128]{2,1,0:T(8,128)(2,1)S(1)}, u32[]{:S(2)}, u32[]{:S(2)}) collective-permute-start(bf16[2,576,128]{2,1,0:T(8,128)(2,1)S(1)} %collective-permute-done.10.refs_8_), channel_id=1, source_target_pairs={{0,4},{4,0},{8,12},{12,8},{16,20},{20,16},{24,28},{28,24},{1,5},{5... | collective-permute-start | bytes 884744 | tf_op jit(solution)/shard_map/ppermute | solution.py:448
  33.1 2.1 %collective-permute-start.8 = (bf16[2,576,128]{2,1,0:T(8,128)(2,1)S(1)}, bf16[2,576,128]{2,1,0:T(8,128)(2,1)S(1)}, u32[]{:S(2)}, u32[]{:S(2)}) collective-permute-start(bf16[2,576,128]{2,1,0:T(8,128)(2,1)S(1)} %collective-permute-done.7.refs_6_), channel_id=1, source_target_pairs={{0,4},{4,0},{8,12},{12,8},{16,20},{20,16},{24,28},{28,24},{1,5},{5... | collective-permute-start | bytes 884744 | tf_op jit(solution)/shard_map/ppermute | solution.py:448

commit v4 on v3

--- a/solution.py
+++ b/solution.py
@@ -261,11 +261,10 @@
     return top, terms
 
 
-def stage_kernel(*refs, piece_counts, places, old_count, mp_count, final):
+def stage_kernel(*refs, piece_count, places, old_count, mp_count, final):
     mp_ref, scale_ref, row_videos_ref, column_videos_ref = refs[:4]
     refs = refs[4:]
-    lead_refs, refs = refs[: piece_counts[0]], refs[piece_counts[0] :]
-    rest_refs, refs = refs[: piece_counts[1]], refs[piece_counts[1] :]
+    piece_refs, refs = refs[:piece_count], refs[piece_count:]
     old_refs, refs = refs[: 2 * old_count], refs[2 * old_count :]
     old = [(old_refs[2 * k], old_refs[2 * k + 1]) for k in range(old_count)]
     if old_count:
@@ -286,18 +285,14 @@
     scale = scale_ref[0]
     scale2 = scale * log2_e
 
-    for position, (lead_place, rest_place) in enumerate(places):
+    for position, place in enumerate(places):
         span = pl.ds(position * rows, rows)
         for kind in range(2):
-            lead_ref, lead_at = lead_refs[lead_place[0]], lead_place[1]
-            rest_ref, rest_at = rest_refs[rest_place[0]], rest_place[1]
-            raw = jnp.concatenate(
-                [
-                    lead_ref[kind, lead_at * chunk : (lead_at + 1) * chunk, :],
-                    rest_ref[kind, rest_at * (width - chunk) : (rest_at + 1) * (width - chunk), :],
-                ],
-                axis=0,
-            )
+            raw = [
+                piece_refs[piece][kind, first * chunk : (first + count) * chunk, :]
+                for piece, first, count in place
+            ]
+            raw = jnp.concatenate(raw, axis=0)
             if position == 0 and not old_count:
                 own_ref[kind] = jnp.transpose(raw)
             wide = raw.astype(jnp.float32)
@@ -464,7 +459,7 @@
     vmem = pl.BlockSpec(memory_space=pltpu.VMEM)
     smem = pl.BlockSpec(memory_space=pltpu.SMEM)
 
-    def stage(leads, rests, places, old, carried, final=False):
+    def stage(pieces, places, old, carried, final=False):
         fresh = len(places) * row_count
         total = fresh + sum(clips.shape[0] for clips, _ in old)
         units = [((fresh, width), jnp.bfloat16), ((width, fresh), jnp.bfloat16)]
@@ -476,12 +471,12 @@
             outs = units + [((1, total), jnp.float32)] * 2
             if not old:
                 outs = outs + [((2, row_count, width), jnp.bfloat16)]
-        operands = [*common, *leads, *rests, *[unit for pair in old for unit in pair], *carried]
+        operands = [*common, *pieces, *[unit for pair in old for unit in pair], *carried]
         score_count = (2 * total - fresh) * fresh
         return pl.pallas_call(
             functools.partial(
                 stage_kernel,
-                piece_counts=(len(leads), len(rests)),
+                piece_count=len(pieces),
                 places=places,
                 old_count=len(old),
                 mp_count=mp_count,
@@ -492,42 +487,66 @@
             out_specs=[vmem] * len(outs),
             scratch_shapes=scratch,
             cost_estimate=pl.CostEstimate(
-                flops=2 * score_count * width, bytes_accessed=8 * fresh * width, transcendentals=2 * score_count
+                flops=1, bytes_accessed=1, transcendentals=0
             ),
             compiler_params=pltpu.CompilerParams(vmem_limit_bytes=32 * 1024 * 1024),
         )(*operands)
 
+    def after(value, other):
+        return lax.optimization_barrier((value, other))[0]
+
+    others = mp_count - 1
     lead = jnp.stack([clips.T, captions.T])
-    lead_first = along(0, lead)
     arrived = [
         lax.ppermute(lead, "mp", [(i, i ^ k) for i in range(mp_count)]) for k in range(1, mp_count)
     ]
-    lead_second = along(1, jnp.concatenate([lead, lead_first], axis=1))
+    lead_first = along(0, after(lead, arrived[0]))
+    lead_second = along(1, after(lead, arrived[0]))
+    lead_pair = jnp.concatenate([lead, lead_first], axis=1)
+    lead_pair_other = across(lead_pair)
+    arrived[-1] = after(arrived[-1], (lead_first, lead_second, lead_pair_other))
     rest = jnp.concatenate(arrived, axis=1)
-    rest, lead_second = lax.optimization_barrier((rest, lead_second))
     rest_first = along(0, rest)
-    lead_other = across(jnp.concatenate([lead, lead_first, lead_second], axis=1))
-    rest_other = across(rest)
-    clips_a, caps_a, row_a, col_a, own_raw = stage(
-        [lead, lead_other], [rest, rest_other], [((0, 0), (0, 0)), ((1, 0), (1, 0))], [], []
-    )
-    rest, row_a = lax.optimization_barrier((rest, row_a))
-    rest_second = along(1, rest)
-    rest_third = along(1, rest_first)
+    clips_a, caps_a, row_a, col_a, own_raw = stage([lead, rest], [[(0, 0, 1), (1, 0, others)]], [], [])
+    rest_second = along(1, after(rest, row_a))
+    third = along(1, jnp.concatenate([lead_first, rest_first], axis=1))
+    rest_other = across(after(rest, rest_first))
+    lead_second_other = across(after(lead_second, rest_first))
     clips_b, caps_b, row_b, col_b = stage(
-        [lead_first, lead_second, lead_other],
-        [rest_first, rest_second, across(rest_first), across(rest_second)],
-        [((0, 0), (0, 0)), ((1, 0), (1, 0)), ((2, 1), (2, 0)), ((2, 2), (3, 0))],
+        [
+            lead_pair_other,
+            rest_other,
+            lead_first,
+            rest_first,
+            lead_second,
+            rest_second,
+            across(rest_first),
+            lead_second_other,
+            across(rest_second),
+        ],
+        [
+            [(0, 0, 1), (1, 0, others)],
+            [(2, 0, 1), (3, 0, others)],
+            [(4, 0, 1), (5, 0, others)],
+            [(0, 1, 1), (6, 0, others)],
+            [(7, 0, 1), (8, 0, others)],
+        ],
         [(clips_a, caps_a)],
         [row_a, col_a, own_raw],
     )
+    third_other = across(after(third, row_b))
+    clips_c, caps_c, row_c, col_c = stage(
+        [third],
+        [[(0, 0, mp_count)]],
+        [(clips_a, caps_a), (clips_b, caps_b)],
+        [row_b, col_b, own_raw],
+    )
     return tuple(
         stage(
-            [lead_second, lead_other],
-            [rest_third, across(rest_third)],
-            [((0, 1), (0, 0)), ((1, 3), (1, 0))],
-            [(clips_a, caps_a), (clips_b, caps_b)],
-            [row_b, col_b, own_raw],
+            [third_other],
+            [[(0, 0, mp_count)]],
+            [(clips_a, caps_a), (clips_b, caps_b), (clips_c, caps_c)],
+            [row_c, col_c, own_raw],
             final=True,
         )
     )

time: 39.3 us -> 38.7 us (0.985)
  waiting for transfers between devices: 13.2 us -> 10.3 us
  Pallas kernels: 6.75 us -> 8.65 us
  local copies, waits for them, and re-layouts: 0.86 us -> 1.58 us
    ppermute x5, waiting for transfers between devices: 11.9 us -> 6.2 us  [along(): return lax.ppermute(block, 'dp', route)]
    pallas_call x3 -> x4, Pallas kernels: 6.75 us -> 8.65 us  [stage(): pl.pallas_call(functools.partial(stage_kernel, piece_count=len(pieces), p...]
    ppermute x5 -> x6, waiting for transfers between devices: 0.01 us -> 1.76 us  [across(): return lax.ppermute(block, 'dp', [(i, i ^ 1) for i in range(dp_count)])]
    ppermute x3, waiting for transfers between devices: 1.31 us -> 2.33 us  [resident_body(): lax.ppermute(lead, 'mp', [(i, i ^ k) for i in range(mp_count)])]
    unnamed x13 -> x15, local copies, waits for them, and re-layouts: 0.56 us -> 1.26 us
    ppermute x5, starting transfers between devices: 9.47 us -> 8.88 us  [along(): return lax.ppermute(block, 'dp', route)]
    ppermute x5 -> x6, starting transfers between devices: 0.85 us -> 1.09 us  [across(): return lax.ppermute(block, 'dp', [(i, i ^ 1) for i in range(dp_count)])]
  transfers between devices with their start and end apart: 13 -> 14, of which waited for: 6 -> 6; matrix products, arithmetic and copies ran while one was open for 2% -> 2% of each run, Pallas kernels for 7% -> 13%
where the time goes in v4:
time: 38.7 us; the launch traced here: 38.4 us
  starting transfers between devices  15.7 us (41%)
  waiting for transfers between devices  10.3 us (27%)
  Pallas kernels  8.65 us (22%)
  local copies, waits for them, and re-layouts  1.58 us (4%)
  between operations  1.38 us (4%)
  other arithmetic  0.88 us (2%)
    ppermute x5, starting transfers between devices, along(): return lax.ppermute(block, 'dp', route)  8.88 us
    pallas_call x4, Pallas kernels, stage(): pl.pallas_call(functools.partial(stage_kernel, piece_count=len(pieces), p...  8.65 us
    ppermute x5, waiting for transfers between devices, along(): return lax.ppermute(block, 'dp', route)  6.2 us
    ppermute x3, starting transfers between devices, resident_body(): lax.ppermute(lead, 'mp', [(i, i ^ k) for i in range(mp_count)])  5.68 us
    ppermute x3, waiting for transfers between devices, resident_body(): lax.ppermute(lead, 'mp', [(i, i ^ k) for i in range(mp_count)])  2.33 us
    ppermute x6, waiting for transfers between devices, across(): return lax.ppermute(block, 'dp', [(i, i ^ 1) for i in range(dp_count)])  1.76 us
    unnamed x15, local copies, waits for them, and re-layouts  1.26 us
    ppermute x6, starting transfers between devices, across(): return lax.ppermute(block, 'dp', [(i, i ^ 1) for i in range(dp_count)])  1.09 us
  transfers between devices with their start and end apart: 14, of which 6 were waited for; matrix products, arithmetic and copies ran while one was open for 2% of the time, Pallas kernels for 13%

profile of v4, /device:TPU:0, one launch (start us, length us, event | category | flops | bytes accessed | tf_op | source)
XLA Modules:
  0.0 38.4 jit_solution(6940890661481787839)
XLA Ops:
  0.6 0.8 %pad_maximum_fusion.2.refs_4_ = bf16[2,192,128]{2,1,0:T(8,128)(2,1)S(1)} fusion(bf16[1,192,128]{2,1,0:T(8,128)(2,1)} %bitcast.19, bf16[1,192,128]{2,1,0:T(8,128)(2,1)} %bitcast.21), kind=kLoop, calls=%fused_computation.2 | loop fusion | flops 49152 | bytes 196608 | tf_op jit(solution)/shard_map/stack | solution.py:499
  1.5 3.1 %collective-permute-start = (bf16[2,192,128]{2,1,0:T(8,128)(2,1)S(1)}, bf16[2,192,128]{2,1,0:T(8,128)(2,1)S(1)}, u32[]{:S(2)}, u32[]{:S(2)}) collective-permute-start(bf16[2,192,128]{2,1,0:T(8,128)(2,1)S(1)} %pad_maximum_fusion.2.refs_4_), channel_id=1, source_target_pairs={{0,1},{1,0},{2,3},{3,2},{4,5},{5,4},{6,7},{7,6},{8,9},{9,8},{10,11... | collective-permute-start | bytes 294920 | tf_op jit(solution)/shard_map/ppermute | solution.py:501
  4.6 2.5 %collective-permute-start.3 = (bf16[2,192,128]{2,1,0:T(8,128)(2,1)S(1)}, bf16[2,192,128]{2,1,0:T(8,128)(2,1)S(1)}, u32[]{:S(2)}, u32[]{:S(2)}) collective-permute-start(bf16[2,192,128]{2,1,0:T(8,128)(2,1)S(1)} %pad_maximum_fusion.2.refs_4_), channel_id=1, source_target_pairs={{0,3},{1,2},{2,1},{3,0},{4,7},{5,6},{6,5},{7,4},{8,11},{9,10},{10,... | collective-permute-start | bytes 294920 | tf_op jit(solution)/shard_map/ppermute | solution.py:501
  7.0 0.1 collective-permute-start.2
  7.1 0.0 copy-start.2
  7.2 0.0 copy-start.1
  7.2 0.0 copy-start
  7.2 0.7 %copy-done.2 = s32[1024]{0:T(1024)S(1)} copy-done((s32[1024]{0:T(1024)S(1)}, s32[1024]{0:T(1024)}, u32[]{:S(2)}) %copy-start.2) | copy-done | bytes 4120
  7.8 0.1 constant_dynamic-update-slice_fusion
  7.9 0.1 constant_dynamic-update-slice_fusion.10
  8.0 0.1 constant_dynamic-update-slice_fusion.9
  8.1 0.1 constant_dynamic-update-slice_fusion.4
  8.2 0.1 constant_dynamic-update-slice_fusion.8
  8.2 0.0 collective-permute-done
  8.2 1.5 %collective-permute-start.1 = (bf16[2,192,128]{2,1,0:T(8,128)(2,1)S(1)}, bf16[2,192,128]{2,1,0:T(8,128)(2,1)S(1)}, u32[]{:S(2)}, u32[]{:S(2)}) collective-permute-start(bf16[2,192,128]{2,1,0:T(8,128)(2,1)S(1)} %pad_maximum_fusion.2.refs_4_), channel_id=1, source_target_pairs={{0,8},{4,20},{8,0},{12,28},{16,24},{20,4},{24,16},{28,12},{1,9},{5... | collective-permute-start | bytes 294920 | tf_op jit(solution)/shard_map/ppermute | solution.py:440
  9.7 0.1 constant_dynamic-update-slice_fusion.7
  9.8 1.5 %collective-permute-start.4 = (bf16[2,192,128]{2,1,0:T(8,128)(2,1)S(1)}, bf16[2,192,128]{2,1,0:T(8,128)(2,1)S(1)}, u32[]{:S(2)}, u32[]{:S(2)}) collective-permute-start(bf16[2,192,128]{2,1,0:T(8,128)(2,1)S(1)} %pad_maximum_fusion.2.refs_4_), channel_id=1, source_target_pairs={{0,16},{4,12},{8,24},{12,4},{16,0},{20,28},{24,8},{28,20},{1,17},{... | collective-permute-start | bytes 294920 | tf_op jit(solution)/shard_map/ppermute | solution.py:440
  11.3 2.2 %collective-permute-done.1.refs_6_ = bf16[2,192,128]{2,1,0:T(8,128)(2,1)S(1)} collective-permute-done((bf16[2,192,128]{2,1,0:T(8,128)(2,1)S(1)}, bf16[2,192,128]{2,1,0:T(8,128)(2,1)S(1)}, u32[]{:S(2)}, u32[]{:S(2)}) %collective-permute-start.1) | collective-permute-done | bytes 98336 | tf_op jit(solution)/shard_map/ppermute | solution.py:440
  13.5 0.0 copy-done.1
  13.5 0.0 copy-done
  13.6 0.1 collective-permute-start.5
  13.7 2.3 %collective-permute-done.2 = bf16[2,192,128]{2,1,0:T(8,128)(2,1)S(1)} collective-permute-done((bf16[2,192,128]{2,1,0:T(8,128)(2,1)S(1)}, bf16[2,192,128]{2,1,0:T(8,128)(2,1)S(1)}, u32[]{:S(2)}, u32[]{:S(2)}) %collective-permute-start.2) | collective-permute-done | bytes 98336 | tf_op jit(solution)/shard_map/ppermute | solution.py:501
  16.0 0.0 collective-permute-done.3
  16.0 0.0 collective-permute-done.4.refs_8_
  16.0 0.0 collective-permute-done.5.refs_4_
  16.0 1.6 %collective-permute-start.6 = (bf16[2,576,128]{2,1,0:T(8,128)(2,1)S(1)}, bf16[2,576,128]{2,1,0:T(8,128)(2,1)S(1)}, u32[]{:S(2)}, u32[]{:S(2)}) collective-permute-start(bf16[2,576,128]{2,1,0:T(8,128)(2,1)S(1)} %constant_dynamic-update-slice_fusion.1.refs_5_), channel_id=1, source_target_pairs={{0,8},{4,20},{8,0},{12,28},{16,24},{20,4},{24,16},{28,12},{1,9},{5... | collective-permute-start | bytes 884744 | tf_op jit(solution)/shard_map/ppermute | solution.py:440
  17.6 0.1 constant_dynamic-update-slice_fusion.6
  17.7 0.1 constant_dynamic-update-slice_fusion.5
  17.8 0.2 copy.9.refs_3_
  18.7 0.6 %shard_map.59 = (bf16[128,768]{1,0:T(8,128)(2,1)S(1)}, bf16[768,128]{1,0:T(8,128)(2,1)S(1)}, f32[1,128]{1,0:T(1,128)S(1)}, f32[1,128]{1,0:T(1,128)S(1)}, bf16[2,128,768]{2,1,0:T(8,128)(2,1)S(1)}) custom-call(s32[1]{0:T(128)} %bitcast.refs_0_, f32[1]{0:T(128)} %bitcast.10.refs_1_, s32[1,1024]{1,0:T(1,128)S(1)} %bitcast.15, s32[1024,1]{1,0:T(8,128)S(1)} %copy.9.refs_3_, ...), custom_call_target="tpu_custom_call" | custom-call | flops 1 | bytes 1 | tf_op jit(solution)/shard_map/pallas_call | solution.py:476
  19.2 1.6 %collective-permute-start.9 = (bf16[2,576,128]{2,1,0:T(8,128)(2,1)S(1)}, bf16[2,576,128]{2,1,0:T(8,128)(2,1)S(1)}, u32[]{:S(2)}, u32[]{:S(2)}) collective-permute-start(bf16[2,576,128]{2,1,0:T(8,128)(2,1)S(1)} %constant_dynamic-update-slice_fusion.1.refs_5_), channel_id=1, source_target_pairs={{0,16},{4,12},{8,24},{12,4},{16,0},{20,28},{24,8},{28,20},{1,17},{... | collective-permute-start | bytes 884744 | tf_op jit(solution)/shard_map/ppermute | solution.py:440
  20.8 3.6 %collective-permute-done.6.refs_7_ = bf16[2,576,128]{2,1,0:T(8,128)(2,1)S(1)} collective-permute-done((bf16[2,576,128]{2,1,0:T(8,128)(2,1)S(1)}, bf16[2,576,128]{2,1,0:T(8,128)(2,1)S(1)}, u32[]{:S(2)}, u32[]{:S(2)}) %collective-permute-start.6) | collective-permute-done | bytes 294944 | tf_op jit(solution)/shard_map/ppermute | solution.py:440
  24.4 2.7 %collective-permute-start.7 = (bf16[2,768,128]{2,1,0:T(8,128)(2,1)S(1)}, bf16[2,768,128]{2,1,0:T(8,128)(2,1)S(1)}, u32[]{:S(2)}, u32[]{:S(2)}) collective-permute-start(bf16[2,768,128]{2,1,0:T(8,128)(2,1)S(1)} %pad_maximum_fusion), channel_id=1, source_target_pairs={{0,16},{4,12},{8,24},{12,4},{16,0},{20,28},{24,8},{28,20},{1,17},{... | collective-permute-start | bytes 1179656 | tf_op jit(solution)/shard_map/ppermute | solution.py:440
  27.2 0.0 collective-permute-done.9.refs_9_
  27.2 0.0 collective-permute-start.12
  27.2 0.5 %collective-permute-start.8 = (bf16[2,576,128]{2,1,0:T(8,128)(2,1)S(1)}, bf16[2,576,128]{2,1,0:T(8,128)(2,1)S(1)}, u32[]{:S(2)}, u32[]{:S(2)}) collective-permute-start(bf16[2,576,128]{2,1,0:T(8,128)(2,1)S(1)} %constant_dynamic-update-slice_fusion.1.refs_5_), channel_id=1, source_target_pairs={{0,4},{4,0},{8,12},{12,8},{16,20},{20,16},{24,28},{28,24},{1,5},{5... | collective-permute-start | bytes 884744 | tf_op jit(solution)/shard_map/ppermute | solution.py:443
  27.7 0.0 collective-permute-start.10
  27.7 0.5 %collective-permute-start.11 = (bf16[2,192,128]{2,1,0:T(8,128)(2,1)S(1)}, bf16[2,192,128]{2,1,0:T(8,128)(2,1)S(1)}, u32[]{:S(2)}, u32[]{:S(2)}) collective-permute-start(bf16[2,192,128]{2,1,0:T(8,128)(2,1)S(1)} %collective-permute-done.4.refs_8_), channel_id=1, source_target_pairs={{0,4},{4,0},{8,12},{12,8},{16,20},{20,16},{24,28},{28,24},{1,5},{5... | collective-permute-start | bytes 294920 | tf_op jit(solution)/shard_map/ppermute | solution.py:443
  28.2 1.5 %collective-permute-done.11.refs_11_ = bf16[2,192,128]{2,1,0:T(8,128)(2,1)S(1)} collective-permute-done((bf16[2,192,128]{2,1,0:T(8,128)(2,1)S(1)}, bf16[2,192,128]{2,1,0:T(8,128)(2,1)S(1)}, u32[]{:S(2)}, u32[]{:S(2)}) %collective-permute-start.11) | collective-permute-done | bytes 98336 | tf_op jit(solution)/shard_map/ppermute | solution.py:443
  29.7 0.0 collective-permute-done.12.refs_12_
  29.7 0.0 collective-permute-done.8.refs_5_
  29.7 0.0 collective-permute-done.10.refs_10_
  29.7 2.8 %shard_map.60 = (bf16[640,768]{1,0:T(8,128)(2,1)S(1)}, bf16[768,640]{1,0:T(8,128)(2,1)S(1)}, f32[1,768]{1,0:T(1,128)S(1)}, f32[1,768]{1,0:T(1,128)S(1)}) custom-call(s32[1]{0:T(128)} %bitcast.refs_0_, f32[1]{0:T(128)} %bitcast.11.refs_1_, s32[1,1024]{1,0:T(1,128)S(1)} %bitcast.16, s32[1024,1]{1,0:T(8,128)S(1)} %copy.9.refs_3_, ...), custom_call_target="tpu_custom_call" | custom-call | flops 1 | bytes 1 | tf_op jit(solution)/shard_map/pallas_call | solution.py:476
  32.5 0.4 %collective-permute-done.7.refs_4_ = bf16[2,768,128]{2,1,0:T(8,128)(2,1)S(1)} collective-permute-done((bf16[2,768,128]{2,1,0:T(8,128)(2,1)S(1)}, bf16[2,768,128]{2,1,0:T(8,128)(2,1)S(1)}, u32[]{:S(2)}, u32[]{:S(2)}) %collective-permute-start.7) | collective-permute-done | bytes 393248 | tf_op jit(solution)/shard_map/ppermute | solution.py:440
  32.9 0.0 collective-permute-start.13
  32.9 1.5 %shard_map.61 = (bf16[128,768]{1,0:T(8,128)(2,1)S(1)}, bf16[768,128]{1,0:T(8,128)(2,1)S(1)}, f32[1,896]{1,0:T(1,128)S(1)}, f32[1,896]{1,0:T(1,128)S(1)}) custom-call(s32[1]{0:T(128)} %bitcast.refs_0_, f32[1]{0:T(128)} %bitcast.12.refs_1_, s32[1,1024]{1,0:T(1,128)S(1)} %bitcast.17, s32[1024,1]{1,0:T(8,128)S(1)} %copy.9.refs_3_, ...), custom_call_target="tpu_custom_call" | custom-call | flops 1 | bytes 1 | tf_op jit(solution)/shard_map/pallas_call | solution.py:476
  34.4 0.2 collective-permute-done.13.refs_4_
  34.6 3.8 %shard_map.62 = (f32[32,768]{1,0:T(8,128)}, f32[32,768]{1,0:T(8,128)}) custom-call(s32[1]{0:T(128)} %bitcast.refs_0_, f32[1]{0:T(128)} %bitcast.13.refs_1_, s32[1,1024]{1,0:T(1,128)S(1)} %bitcast.18, s32[1024,1]{1,0:T(8,128)S(1)} %copy.9.refs_3_, bf16[2,768,128]{2,1,0:T(8,128)(2,1)S(1)} %collective-permute-done.13.refs_4_, ...), custom_call_target="tpu_custom_call" | custom-call | flops 1 | bytes 1 | tf_op jit(solution)/shard_map/pallas_call | solution.py:476
  (6 shorter events, 0.1 us)
Async XLA Ops:
  1.5 6.8 %collective-permute-start = (bf16[2,192,128]{2,1,0:T(8,128)(2,1)S(1)}, bf16[2,192,128]{2,1,0:T(8,128)(2,1)S(1)}, u32[]{:S(2)}, u32[]{:S(2)}) collective-permute-start(bf16[2,192,128]{2,1,0:T(8,128)(2,1)S(1)} %pad_maximum_fusion.2.refs_4_), channel_id=1, source_target_pairs={{0,1},{1,0},{2,3},{3,2},{4,5},{5,4},{6,7},{7,6},{8,9},{9,8},{10,11... | collective-permute-start | bytes 294920 | tf_op jit(solution)/shard_map/ppermute | solution.py:501
  4.6 11.4 %collective-permute-start.3 = (bf16[2,192,128]{2,1,0:T(8,128)(2,1)S(1)}, bf16[2,192,128]{2,1,0:T(8,128)(2,1)S(1)}, u32[]{:S(2)}, u32[]{:S(2)}) collective-permute-start(bf16[2,192,128]{2,1,0:T(8,128)(2,1)S(1)} %pad_maximum_fusion.2.refs_4_), channel_id=1, source_target_pairs={{0,3},{1,2},{2,1},{3,0},{4,7},{5,6},{6,5},{7,4},{8,11},{9,10},{10,... | collective-permute-start | bytes 294920 | tf_op jit(solution)/shard_map/ppermute | solution.py:501
  7.0 8.9 %collective-permute-start.2 = (bf16[2,192,128]{2,1,0:T(8,128)(2,1)S(1)}, bf16[2,192,128]{2,1,0:T(8,128)(2,1)S(1)}, u32[]{:S(2)}, u32[]{:S(2)}) collective-permute-start(bf16[2,192,128]{2,1,0:T(8,128)(2,1)S(1)} %pad_maximum_fusion.2.refs_4_), channel_id=1, source_target_pairs={{0,2},{1,3},{2,0},{3,1},{4,6},{5,7},{6,4},{7,5},{8,10},{9,11},{10,... | collective-permute-start | bytes 294920 | tf_op jit(solution)/shard_map/ppermute | solution.py:501
  7.1 0.7 %copy-start.2 = (s32[1024]{0:T(1024)S(1)}, s32[1024]{0:T(1024)}, u32[]{:S(2)}) copy-start(s32[1024]{0:T(1024)} %param.6) | copy-start | bytes 12292
  7.2 6.4 %copy-start.1 = (bf16[128,192]{0,1:T(8,128)(2,1)S(1)}, bf16[128,192]{0,1:T(8,128)(2,1)}, u32[]{:S(2)}) copy-start(bf16[128,192]{0,1:T(8,128)(2,1)} %param.4) | copy-start | bytes 147460
  7.2 6.4 %copy-start = (bf16[128,192]{0,1:T(8,128)(2,1)S(1)}, bf16[128,192]{0,1:T(8,128)(2,1)}, u32[]{:S(2)}) copy-start(bf16[128,192]{0,1:T(8,128)(2,1)} %param.5) | copy-start | bytes 147460
  8.2 5.3 %collective-permute-start.1 = (bf16[2,192,128]{2,1,0:T(8,128)(2,1)S(1)}, bf16[2,192,128]{2,1,0:T(8,128)(2,1)S(1)}, u32[]{:S(2)}, u32[]{:S(2)}) collective-permute-start(bf16[2,192,128]{2,1,0:T(8,128)(2,1)S(1)} %pad_maximum_fusion.2.refs_4_), channel_id=1, source_target_pairs={{0,8},{4,20},{8,0},{12,28},{16,24},{20,4},{24,16},{28,12},{1,9},{5... | collective-permute-start | bytes 294920 | tf_op jit(solution)/shard_map/ppermute | solution.py:440
  9.8 6.2 %collective-permute-start.4 = (bf16[2,192,128]{2,1,0:T(8,128)(2,1)S(1)}, bf16[2,192,128]{2,1,0:T(8,128)(2,1)S(1)}, u32[]{:S(2)}, u32[]{:S(2)}) collective-permute-start(bf16[2,192,128]{2,1,0:T(8,128)(2,1)S(1)} %pad_maximum_fusion.2.refs_4_), channel_id=1, source_target_pairs={{0,16},{4,12},{8,24},{12,4},{16,0},{20,28},{24,8},{28,20},{1,17},{... | collective-permute-start | bytes 294920 | tf_op jit(solution)/shard_map/ppermute | solution.py:440
  13.6 2.5 %collective-permute-start.5 = (bf16[2,384,128]{2,1,0:T(8,128)(2,1)S(1)}, bf16[2,384,128]{2,1,0:T(8,128)(2,1)S(1)}, u32[]{:S(2)}, u32[]{:S(2)}) collective-permute-start(bf16[2,384,128]{2,1,0:T(8,128)(2,1)S(1)} %pad_maximum_fusion.1), channel_id=1, source_target_pairs={{0,4},{4,0},{8,12},{12,8},{16,20},{20,16},{24,28},{28,24},{1,5},{5... | collective-permute-start | bytes 589832 | tf_op jit(solution)/shard_map/ppermute | solution.py:443
  16.0 8.3 %collective-permute-start.6 = (bf16[2,576,128]{2,1,0:T(8,128)(2,1)S(1)}, bf16[2,576,128]{2,1,0:T(8,128)(2,1)S(1)}, u32[]{:S(2)}, u32[]{:S(2)}) collective-permute-start(bf16[2,576,128]{2,1,0:T(8,128)(2,1)S(1)} %constant_dynamic-update-slice_fusion.1.refs_5_), channel_id=1, source_target_pairs={{0,8},{4,20},{8,0},{12,28},{16,24},{20,4},{24,16},{28,12},{1,9},{5... | collective-permute-start | bytes 884744 | tf_op jit(solution)/shard_map/ppermute | solution.py:440
  19.2 7.9 %collective-permute-start.9 = (bf16[2,576,128]{2,1,0:T(8,128)(2,1)S(1)}, bf16[2,576,128]{2,1,0:T(8,128)(2,1)S(1)}, u32[]{:S(2)}, u32[]{:S(2)}) collective-permute-start(bf16[2,576,128]{2,1,0:T(8,128)(2,1)S(1)} %constant_dynamic-update-slice_fusion.1.refs_5_), channel_id=1, source_target_pairs={{0,16},{4,12},{8,24},{12,4},{16,0},{20,28},{24,8},{28,20},{1,17},{... | collective-permute-start | bytes 884744 | tf_op jit(solution)/shard_map/ppermute | solution.py:440
  24.4 8.5 %collective-permute-start.7 = (bf16[2,768,128]{2,1,0:T(8,128)(2,1)S(1)}, bf16[2,768,128]{2,1,0:T(8,128)(2,1)S(1)}, u32[]{:S(2)}, u32[]{:S(2)}) collective-permute-start(bf16[2,768,128]{2,1,0:T(8,128)(2,1)S(1)} %pad_maximum_fusion), channel_id=1, source_target_pairs={{0,16},{4,12},{8,24},{12,4},{16,0},{20,28},{24,8},{28,20},{1,17},{... | collective-permute-start | bytes 1179656 | tf_op jit(solution)/shard_map/ppermute | solution.py:440
  27.2 2.6 %collective-permute-start.12 = (bf16[2,576,128]{2,1,0:T(8,128)(2,1)S(1)}, bf16[2,576,128]{2,1,0:T(8,128)(2,1)S(1)}, u32[]{:S(2)}, u32[]{:S(2)}) collective-permute-start(bf16[2,576,128]{2,1,0:T(8,128)(2,1)S(1)} %collective-permute-done.9.refs_9_), channel_id=1, source_target_pairs={{0,4},{4,0},{8,12},{12,8},{16,20},{20,16},{24,28},{28,24},{1,5},{5... | collective-permute-start | bytes 884744 | tf_op jit(solution)/shard_map/ppermute | solution.py:443
  27.2 2.6 %collective-permute-start.8 = (bf16[2,576,128]{2,1,0:T(8,128)(2,1)S(1)}, bf16[2,576,128]{2,1,0:T(8,128)(2,1)S(1)}, u32[]{:S(2)}, u32[]{:S(2)}) collective-permute-start(bf16[2,576,128]{2,1,0:T(8,128)(2,1)S(1)} %constant_dynamic-update-slice_fusion.1.refs_5_), channel_id=1, source_target_pairs={{0,4},{4,0},{8,12},{12,8},{16,20},{20,16},{24,28},{28,24},{1,5},{5... | collective-permute-start | bytes 884744 | tf_op jit(solution)/shard_map/ppermute | solution.py:443
  27.7 2.1 %collective-permute-start.10 = (bf16[2,576,128]{2,1,0:T(8,128)(2,1)S(1)}, bf16[2,576,128]{2,1,0:T(8,128)(2,1)S(1)}, u32[]{:S(2)}, u32[]{:S(2)}) collective-permute-start(bf16[2,576,128]{2,1,0:T(8,128)(2,1)S(1)} %collective-permute-done.6.refs_7_), channel_id=1, source_target_pairs={{0,4},{4,0},{8,12},{12,8},{16,20},{20,16},{24,28},{28,24},{1,5},{5... | collective-permute-start | bytes 884744 | tf_op jit(solution)/shard_map/ppermute | solution.py:443
  27.7 2.1 %collective-permute-start.11 = (bf16[2,192,128]{2,1,0:T(8,128)(2,1)S(1)}, bf16[2,192,128]{2,1,0:T(8,128)(2,1)S(1)}, u32[]{:S(2)}, u32[]{:S(2)}) collective-permute-start(bf16[2,192,128]{2,1,0:T(8,128)(2,1)S(1)} %collective-permute-done.4.refs_8_), channel_id=1, source_target_pairs={{0,4},{4,0},{8,12},{12,8},{16,20},{20,16},{24,28},{28,24},{1,5},{5... | collective-permute-start | bytes 294920 | tf_op jit(solution)/shard_map/ppermute | solution.py:443
  32.9 1.7 %collective-permute-start.13 = (bf16[2,768,128]{2,1,0:T(8,128)(2,1)S(1)}, bf16[2,768,128]{2,1,0:T(8,128)(2,1)S(1)}, u32[]{:S(2)}, u32[]{:S(2)}) collective-permute-start(bf16[2,768,128]{2,1,0:T(8,128)(2,1)S(1)} %collective-permute-done.7.refs_4_), channel_id=1, source_target_pairs={{0,4},{4,0},{8,12},{12,8},{16,20},{20,16},{24,28},{28,24},{1,5},{5... | collective-permute-start | bytes 1179656 | tf_op jit(solution)/shard_map/ppermute | solution.py:443

commit v5 on v4

--- a/solution.py
+++ b/solution.py
@@ -495,19 +495,22 @@
     def after(value, other):
         return lax.optimization_barrier((value, other))[0]
 
-    others = mp_count - 1
-    lead = jnp.stack([clips.T, captions.T])
+    early = mp_count // 2
+    late = mp_count - early
+    chunk = jnp.stack([clips.T, captions.T])
     arrived = [
-        lax.ppermute(lead, "mp", [(i, i ^ k) for i in range(mp_count)]) for k in range(1, mp_count)
+        lax.ppermute(chunk, "mp", [(i, i ^ k) for i in range(mp_count)]) for k in range(1, mp_count)
     ]
-    lead_first = along(0, after(lead, arrived[0]))
-    lead_second = along(1, after(lead, arrived[0]))
-    lead_pair = jnp.concatenate([lead, lead_first], axis=1)
-    lead_pair_other = across(lead_pair)
+    lead = jnp.concatenate([chunk] + arrived[: early - 1], axis=1)
+    lead_first = along(0, lead)
+    lead_second = along(1, lead)
+    lead_pair_other = across(after(jnp.concatenate([lead, lead_first], axis=1), lead_second))
     arrived[-1] = after(arrived[-1], (lead_first, lead_second, lead_pair_other))
-    rest = jnp.concatenate(arrived, axis=1)
+    rest = jnp.concatenate(arrived[early - 1 :], axis=1)
     rest_first = along(0, rest)
-    clips_a, caps_a, row_a, col_a, own_raw = stage([lead, rest], [[(0, 0, 1), (1, 0, others)]], [], [])
+    clips_a, caps_a, row_a, col_a, own_raw = stage(
+        [lead, rest], [[(0, 0, early), (1, 0, late)]], [], []
+    )
     rest_second = along(1, after(rest, row_a))
     third = along(1, jnp.concatenate([lead_first, rest_first], axis=1))
     rest_other = across(after(rest, rest_first))
@@ -525,11 +528,11 @@
             across(rest_second),
         ],
         [
-            [(0, 0, 1), (1, 0, others)],
-            [(2, 0, 1), (3, 0, others)],
-            [(4, 0, 1), (5, 0, others)],
-            [(0, 1, 1), (6, 0, others)],
-            [(7, 0, 1), (8, 0, others)],
+            [(0, 0, early), (1, 0, late)],
+            [(2, 0, early), (3, 0, late)],
+            [(4, 0, early), (5, 0, late)],
+            [(0, early, early), (6, 0, late)],
+            [(7, 0, early), (8, 0, late)],
         ],
         [(clips_a, caps_a)],
         [row_a, col_a, own_raw],

time: 38.7 us -> 37.3 us (0.964)
  starting transfers between devices: 15.7 us -> 13.4 us
  waiting for transfers between devices: 10.3 us -> 10.7 us
    ppermute x3, waiting for transfers between devices: 2.33 us -> 0.21 us  [resident_body(): lax.ppermute(chunk, 'mp', [(i, i ^ k) for i in range(mp_count)])]
    ppermute x5, starting transfers between devices: 8.88 us -> 7.01 us  [along(): return lax.ppermute(block, 'dp', route)]
    ppermute x5, waiting for transfers between devices: 6.2 us -> 7.7 us  [along(): return lax.ppermute(block, 'dp', route)]
    ppermute x6, waiting for transfers between devices: 1.76 us -> 2.81 us  [across(): return lax.ppermute(block, 'dp', [(i, i ^ 1) for i in range(dp_count)])]
    unnamed x15 -> x14, local copies, waits for them, and re-layouts: 1.26 us -> 1.25 us
  transfers between devices with their start and end apart: 14 -> 14, of which waited for: 6 -> 10; matrix products, arithmetic and copies ran while one was open for 2% -> 3% of each run, Pallas kernels for 13% -> 13%
where the time goes in v5:
time: 37.3 us; the launch traced here: 36.6 us
  starting transfers between devices  13.4 us (36%)
  waiting for transfers between devices  10.7 us (29%)
  Pallas kernels  8.64 us (23%)
  local copies, waits for them, and re-layouts  1.56 us (4%)
  between operations  1.38 us (4%)
  other arithmetic  0.94 us (3%)
    pallas_call x4, Pallas kernels, stage(): pl.pallas_call(functools.partial(stage_kernel, piece_count=len(pieces), p...  8.64 us
    ppermute x5, waiting for transfers between devices, along(): return lax.ppermute(block, 'dp', route)  7.7 us
    ppermute x5, starting transfers between devices, along(): return lax.ppermute(block, 'dp', route)  7.01 us
    ppermute x3, starting transfers between devices, resident_body(): lax.ppermute(chunk, 'mp', [(i, i ^ k) for i in range(mp_count)])  5.68 us
    ppermute x6, waiting for transfers between devices, across(): return lax.ppermute(block, 'dp', [(i, i ^ 1) for i in range(dp_count)])  2.81 us
    unnamed x14, local copies, waits for them, and re-layouts  1.25 us
    another operation x1, other arithmetic, resident_body(): chunk = jnp.stack([clips.T, captions.T])  0.87 us
  transfers between devices with their start and end apart: 14, of which 10 were waited for; matrix products, arithmetic and copies ran while one was open for 3% of the time, Pallas kernels for 13%

profile of v5, /device:TPU:0, one launch (start us, length us, event | category | flops | bytes accessed | tf_op | source)
XLA Modules:
  0.0 36.6 jit_solution(18317425686552124781)
XLA Ops:
  0.6 0.0 copy-start.1
  0.6 0.9 %pad_maximum_fusion.3 = bf16[2,192,128]{2,1,0:T(8,128)(2,1)S(1)} fusion(bf16[1,192,128]{2,1,0:T(8,128)(2,1)} %bitcast.19, bf16[1,192,128]{2,1,0:T(8,128)(2,1)} %bitcast.22), kind=kLoop, calls=%fused_computation.3 | loop fusion | flops 49152 | bytes 196608 | tf_op jit(solution)/shard_map/stack | solution.py:500
  1.5 0.0 copy-start
  1.5 3.1 %collective-permute-start = (bf16[2,192,128]{2,1,0:T(8,128)(2,1)S(1)}, bf16[2,192,128]{2,1,0:T(8,128)(2,1)S(1)}, u32[]{:S(2)}, u32[]{:S(2)}) collective-permute-start(bf16[2,192,128]{2,1,0:T(8,128)(2,1)S(1)} %pad_maximum_fusion.3), channel_id=1, source_target_pairs={{0,1},{1,0},{2,3},{3,2},{4,5},{5,4},{6,7},{7,6},{8,9},{9,8},{10,11... | collective-permute-start | bytes 294920 | tf_op jit(solution)/shard_map/ppermute | solution.py:502
  4.6 2.5 %collective-permute-start.3 = (bf16[2,192,128]{2,1,0:T(8,128)(2,1)S(1)}, bf16[2,192,128]{2,1,0:T(8,128)(2,1)S(1)}, u32[]{:S(2)}, u32[]{:S(2)}) collective-permute-start(bf16[2,192,128]{2,1,0:T(8,128)(2,1)S(1)} %pad_maximum_fusion.3), channel_id=1, source_target_pairs={{0,3},{1,2},{2,1},{3,0},{4,7},{5,6},{6,5},{7,4},{8,11},{9,10},{10,... | collective-permute-start | bytes 294920 | tf_op jit(solution)/shard_map/ppermute | solution.py:502
  7.1 0.1 collective-permute-start.2
  7.2 0.0 copy-start.2
  7.2 0.7 %copy-done.2 = s32[1024]{0:T(1024)S(1)} copy-done((s32[1024]{0:T(1024)S(1)}, s32[1024]{0:T(1024)}, u32[]{:S(2)}) %copy-start.2) | copy-done | bytes 4120
  7.9 0.1 constant_dynamic-update-slice_fusion
  8.0 0.0 collective-permute-done
  8.0 0.0 copy-done.1
  8.0 0.0 copy-done
  8.0 1.6 %collective-permute-start.1 = (bf16[2,384,128]{2,1,0:T(8,128)(2,1)S(1)}, bf16[2,384,128]{2,1,0:T(8,128)(2,1)S(1)}, u32[]{:S(2)}, u32[]{:S(2)}) collective-permute-start(bf16[2,384,128]{2,1,0:T(8,128)(2,1)S(1)} %pad_maximum_fusion.2.refs_4_), channel_id=1, source_target_pairs={{0,8},{4,20},{8,0},{12,28},{16,24},{20,4},{24,16},{28,12},{1,9},{5... | collective-permute-start | bytes 589832 | tf_op jit(solution)/shard_map/ppermute | solution.py:440
  9.6 0.1 constant_dynamic-update-slice_fusion.9
  9.6 1.5 %collective-permute-start.4 = (bf16[2,384,128]{2,1,0:T(8,128)(2,1)S(1)}, bf16[2,384,128]{2,1,0:T(8,128)(2,1)S(1)}, u32[]{:S(2)}, u32[]{:S(2)}) collective-permute-start(bf16[2,384,128]{2,1,0:T(8,128)(2,1)S(1)} %pad_maximum_fusion.2.refs_4_), channel_id=1, source_target_pairs={{0,16},{4,12},{8,24},{12,4},{16,0},{20,28},{24,8},{28,20},{1,17},{... | collective-permute-start | bytes 589832 | tf_op jit(solution)/shard_map/ppermute | solution.py:440
  11.2 0.1 constant_dynamic-update-slice_fusion.8
  11.2 4.2 %collective-permute-done.1.refs_6_ = bf16[2,384,128]{2,1,0:T(8,128)(2,1)S(1)} collective-permute-done((bf16[2,384,128]{2,1,0:T(8,128)(2,1)S(1)}, bf16[2,384,128]{2,1,0:T(8,128)(2,1)S(1)}, u32[]{:S(2)}, u32[]{:S(2)}) %collective-permute-start.1) | collective-permute-done | bytes 196640 | tf_op jit(solution)/shard_map/ppermute | solution.py:440
  15.5 0.0 collective-permute-done.4.refs_8_
  15.5 0.1 collective-permute-start.5
  15.6 0.1 constant_dynamic-update-slice_fusion.7
  15.7 0.1 constant_dynamic-update-slice_fusion.6
  15.8 0.1 constant_dynamic-update-slice_fusion.5
  15.8 0.2 collective-permute-done.2
  16.0 0.0 collective-permute-done.3
  16.1 1.2 %collective-permute-done.5.refs_4_ = bf16[2,768,128]{2,1,0:T(8,128)(2,1)S(1)} collective-permute-done((bf16[2,768,128]{2,1,0:T(8,128)(2,1)S(1)}, bf16[2,768,128]{2,1,0:T(8,128)(2,1)S(1)}, u32[]{:S(2)}, u32[]{:S(2)}) %collective-permute-start.5) | collective-permute-done | bytes 393248 | tf_op jit(solution)/shard_map/ppermute | solution.py:443
  17.3 1.6 %collective-permute-start.6 = (bf16[2,384,128]{2,1,0:T(8,128)(2,1)S(1)}, bf16[2,384,128]{2,1,0:T(8,128)(2,1)S(1)}, u32[]{:S(2)}, u32[]{:S(2)}) collective-permute-start(bf16[2,384,128]{2,1,0:T(8,128)(2,1)S(1)} %constant_dynamic-update-slice_fusion.1.refs_5_), channel_id=1, source_target_pairs={{0,8},{4,20},{8,0},{12,28},{16,24},{20,4},{24,16},{28,12},{1,9},{5... | collective-permute-start | bytes 589832 | tf_op jit(solution)/shard_map/ppermute | solution.py:440
  18.9 0.1 constant_dynamic-update-slice_fusion.4
  19.0 0.1 constant_dynamic-update-slice_fusion.3
  19.0 0.2 copy.9.refs_3_
  19.9 0.6 %shard_map.59 = (bf16[128,768]{1,0:T(8,128)(2,1)S(1)}, bf16[768,128]{1,0:T(8,128)(2,1)S(1)}, f32[1,128]{1,0:T(1,128)S(1)}, f32[1,128]{1,0:T(1,128)S(1)}, bf16[2,128,768]{2,1,0:T(8,128)(2,1)S(1)}) custom-call(s32[1]{0:T(128)} %bitcast.refs_0_, f32[1]{0:T(128)} %bitcast.10.refs_1_, s32[1,1024]{1,0:T(1,128)S(1)} %bitcast.15, s32[1024,1]{1,0:T(8,128)S(1)} %copy.9.refs_3_, ...), custom_call_target="tpu_custom_call" | custom-call | flops 1 | bytes 1 | tf_op jit(solution)/shard_map/pallas_call | solution.py:476
  20.5 0.6 %collective-permute-start.9 = (bf16[2,384,128]{2,1,0:T(8,128)(2,1)S(1)}, bf16[2,384,128]{2,1,0:T(8,128)(2,1)S(1)}, u32[]{:S(2)}, u32[]{:S(2)}) collective-permute-start(bf16[2,384,128]{2,1,0:T(8,128)(2,1)S(1)} %constant_dynamic-update-slice_fusion.1.refs_5_), channel_id=1, source_target_pairs={{0,16},{4,12},{8,24},{12,4},{16,0},{20,28},{24,8},{28,20},{1,17},{... | collective-permute-start | bytes 589832 | tf_op jit(solution)/shard_map/ppermute | solution.py:440
  21.1 2.2 %collective-permute-done.6.refs_7_ = bf16[2,384,128]{2,1,0:T(8,128)(2,1)S(1)} collective-permute-done((bf16[2,384,128]{2,1,0:T(8,128)(2,1)S(1)}, bf16[2,384,128]{2,1,0:T(8,128)(2,1)S(1)}, u32[]{:S(2)}, u32[]{:S(2)}) %collective-permute-start.6) | collective-permute-done | bytes 196640 | tf_op jit(solution)/shard_map/ppermute | solution.py:440
  23.3 1.8 %collective-permute-start.7 = (bf16[2,768,128]{2,1,0:T(8,128)(2,1)S(1)}, bf16[2,768,128]{2,1,0:T(8,128)(2,1)S(1)}, u32[]{:S(2)}, u32[]{:S(2)}) collective-permute-start(bf16[2,768,128]{2,1,0:T(8,128)(2,1)S(1)} %pad_maximum_fusion.1), channel_id=1, source_target_pairs={{0,16},{4,12},{8,24},{12,4},{16,0},{20,28},{24,8},{28,20},{1,17},{... | collective-permute-start | bytes 1179656 | tf_op jit(solution)/shard_map/ppermute | solution.py:440
  25.1 0.0 collective-permute-start.8
  25.1 1.1 %collective-permute-done.9.refs_9_ = bf16[2,384,128]{2,1,0:T(8,128)(2,1)S(1)} collective-permute-done((bf16[2,384,128]{2,1,0:T(8,128)(2,1)S(1)}, bf16[2,384,128]{2,1,0:T(8,128)(2,1)S(1)}, u32[]{:S(2)}, u32[]{:S(2)}) %collective-permute-start.9) | collective-permute-done | bytes 196640 | tf_op jit(solution)/shard_map/ppermute | solution.py:440
  26.2 0.0 collective-permute-start.12
  26.2 0.5 %collective-permute-start.11 = (bf16[2,384,128]{2,1,0:T(8,128)(2,1)S(1)}, bf16[2,384,128]{2,1,0:T(8,128)(2,1)S(1)}, u32[]{:S(2)}, u32[]{:S(2)}) collective-permute-start(bf16[2,384,128]{2,1,0:T(8,128)(2,1)S(1)} %collective-permute-done.4.refs_8_), channel_id=1, source_target_pairs={{0,4},{4,0},{8,12},{12,8},{16,20},{20,16},{24,28},{28,24},{1,5},{5... | collective-permute-start | bytes 589832 | tf_op jit(solution)/shard_map/ppermute | solution.py:443
  26.7 0.0 collective-permute-start.10
  26.7 0.9 %collective-permute-done.12.refs_12_ = bf16[2,384,128]{2,1,0:T(8,128)(2,1)S(1)} collective-permute-done((bf16[2,384,128]{2,1,0:T(8,128)(2,1)S(1)}, bf16[2,384,128]{2,1,0:T(8,128)(2,1)S(1)}, u32[]{:S(2)}, u32[]{:S(2)}) %collective-permute-start.12) | collective-permute-done | bytes 196640 | tf_op jit(solution)/shard_map/ppermute | solution.py:443
  27.7 0.0 collective-permute-done.8.refs_5_
  27.7 0.3 collective-permute-done.11.refs_11_
  27.9 0.3 collective-permute-done.10.refs_10_
  28.2 2.8 %shard_map.60 = (bf16[640,768]{1,0:T(8,128)(2,1)S(1)}, bf16[768,640]{1,0:T(8,128)(2,1)S(1)}, f32[1,768]{1,0:T(1,128)S(1)}, f32[1,768]{1,0:T(1,128)S(1)}) custom-call(s32[1]{0:T(128)} %bitcast.refs_0_, f32[1]{0:T(128)} %bitcast.11.refs_1_, s32[1,1024]{1,0:T(1,128)S(1)} %bitcast.16, s32[1024,1]{1,0:T(8,128)S(1)} %copy.9.refs_3_, ...), custom_call_target="tpu_custom_call" | custom-call | flops 1 | bytes 1 | tf_op jit(solution)/shard_map/pallas_call | solution.py:476
  31.0 0.2 collective-permute-done.7.refs_4_
  31.1 0.1 collective-permute-start.13
  31.3 1.5 %shard_map.61 = (bf16[128,768]{1,0:T(8,128)(2,1)S(1)}, bf16[768,128]{1,0:T(8,128)(2,1)S(1)}, f32[1,896]{1,0:T(1,128)S(1)}, f32[1,896]{1,0:T(1,128)S(1)}) custom-call(s32[1]{0:T(128)} %bitcast.refs_0_, f32[1]{0:T(128)} %bitcast.12.refs_1_, s32[1,1024]{1,0:T(1,128)S(1)} %bitcast.17, s32[1024,1]{1,0:T(8,128)S(1)} %copy.9.refs_3_, ...), custom_call_target="tpu_custom_call" | custom-call | flops 1 | bytes 1 | tf_op jit(solution)/shard_map/pallas_call | solution.py:476
  32.8 0.1 collective-permute-done.13.refs_4_
  32.9 3.8 %shard_map.62 = (f32[32,768]{1,0:T(8,128)}, f32[32,768]{1,0:T(8,128)}) custom-call(s32[1]{0:T(128)} %bitcast.refs_0_, f32[1]{0:T(128)} %bitcast.13.refs_1_, s32[1,1024]{1,0:T(1,128)S(1)} %bitcast.18, s32[1024,1]{1,0:T(8,128)S(1)} %copy.9.refs_3_, bf16[2,768,128]{2,1,0:T(8,128)(2,1)S(1)} %collective-permute-done.13.refs_4_, ...), custom_call_target="tpu_custom_call" | custom-call | flops 1 | bytes 1 | tf_op jit(solution)/shard_map/pallas_call | solution.py:476
  (6 shorter events, 0.1 us)
Async XLA Ops:
  0.6 7.3 %copy-start.1 = (bf16[128,192]{0,1:T(8,128)(2,1)S(1)}, bf16[128,192]{0,1:T(8,128)(2,1)}, u32[]{:S(2)}) copy-start(bf16[128,192]{0,1:T(8,128)(2,1)} %param.4) | copy-start | bytes 147460
  1.5 6.5 %copy-start = (bf16[128,192]{0,1:T(8,128)(2,1)S(1)}, bf16[128,192]{0,1:T(8,128)(2,1)}, u32[]{:S(2)}) copy-start(bf16[128,192]{0,1:T(8,128)(2,1)} %param.5) | copy-start | bytes 147460
  1.5 6.4 %collective-permute-start = (bf16[2,192,128]{2,1,0:T(8,128)(2,1)S(1)}, bf16[2,192,128]{2,1,0:T(8,128)(2,1)S(1)}, u32[]{:S(2)}, u32[]{:S(2)}) collective-permute-start(bf16[2,192,128]{2,1,0:T(8,128)(2,1)S(1)} %pad_maximum_fusion.3), channel_id=1, source_target_pairs={{0,1},{1,0},{2,3},{3,2},{4,5},{5,4},{6,7},{7,6},{8,9},{9,8},{10,11... | collective-permute-start | bytes 294920 | tf_op jit(solution)/shard_map/ppermute | solution.py:502
  4.6 11.4 %collective-permute-start.3 = (bf16[2,192,128]{2,1,0:T(8,128)(2,1)S(1)}, bf16[2,192,128]{2,1,0:T(8,128)(2,1)S(1)}, u32[]{:S(2)}, u32[]{:S(2)}) collective-permute-start(bf16[2,192,128]{2,1,0:T(8,128)(2,1)S(1)} %pad_maximum_fusion.3), channel_id=1, source_target_pairs={{0,3},{1,2},{2,1},{3,0},{4,7},{5,6},{6,5},{7,4},{8,11},{9,10},{10,... | collective-permute-start | bytes 294920 | tf_op jit(solution)/shard_map/ppermute | solution.py:502
  7.1 8.9 %collective-permute-start.2 = (bf16[2,192,128]{2,1,0:T(8,128)(2,1)S(1)}, bf16[2,192,128]{2,1,0:T(8,128)(2,1)S(1)}, u32[]{:S(2)}, u32[]{:S(2)}) collective-permute-start(bf16[2,192,128]{2,1,0:T(8,128)(2,1)S(1)} %pad_maximum_fusion.3), channel_id=1, source_target_pairs={{0,2},{1,3},{2,0},{3,1},{4,6},{5,7},{6,4},{7,5},{8,10},{9,11},{10,... | collective-permute-start | bytes 294920 | tf_op jit(solution)/shard_map/ppermute | solution.py:502
  7.2 0.7 %copy-start.2 = (s32[1024]{0:T(1024)S(1)}, s32[1024]{0:T(1024)}, u32[]{:S(2)}) copy-start(s32[1024]{0:T(1024)} %param.6) | copy-start | bytes 12292
  8.0 7.5 %collective-permute-start.1 = (bf16[2,384,128]{2,1,0:T(8,128)(2,1)S(1)}, bf16[2,384,128]{2,1,0:T(8,128)(2,1)S(1)}, u32[]{:S(2)}, u32[]{:S(2)}) collective-permute-start(bf16[2,384,128]{2,1,0:T(8,128)(2,1)S(1)} %pad_maximum_fusion.2.refs_4_), channel_id=1, source_target_pairs={{0,8},{4,20},{8,0},{12,28},{16,24},{20,4},{24,16},{28,12},{1,9},{5... | collective-permute-start | bytes 589832 | tf_op jit(solution)/shard_map/ppermute | solution.py:440
  9.6 5.9 %collective-permute-start.4 = (bf16[2,384,128]{2,1,0:T(8,128)(2,1)S(1)}, bf16[2,384,128]{2,1,0:T(8,128)(2,1)S(1)}, u32[]{:S(2)}, u32[]{:S(2)}) collective-permute-start(bf16[2,384,128]{2,1,0:T(8,128)(2,1)S(1)} %pad_maximum_fusion.2.refs_4_), channel_id=1, source_target_pairs={{0,16},{4,12},{8,24},{12,4},{16,0},{20,28},{24,8},{28,20},{1,17},{... | collective-permute-start | bytes 589832 | tf_op jit(solution)/shard_map/ppermute | solution.py:440
  15.5 1.8 %collective-permute-start.5 = (bf16[2,768,128]{2,1,0:T(8,128)(2,1)S(1)}, bf16[2,768,128]{2,1,0:T(8,128)(2,1)S(1)}, u32[]{:S(2)}, u32[]{:S(2)}) collective-permute-start(bf16[2,768,128]{2,1,0:T(8,128)(2,1)S(1)} %pad_maximum_fusion), channel_id=1, source_target_pairs={{0,4},{4,0},{8,12},{12,8},{16,20},{20,16},{24,28},{28,24},{1,5},{5... | collective-permute-start | bytes 1179656 | tf_op jit(solution)/shard_map/ppermute | solution.py:443
  17.3 6.0 %collective-permute-start.6 = (bf16[2,384,128]{2,1,0:T(8,128)(2,1)S(1)}, bf16[2,384,128]{2,1,0:T(8,128)(2,1)S(1)}, u32[]{:S(2)}, u32[]{:S(2)}) collective-permute-start(bf16[2,384,128]{2,1,0:T(8,128)(2,1)S(1)} %constant_dynamic-update-slice_fusion.1.refs_5_), channel_id=1, source_target_pairs={{0,8},{4,20},{8,0},{12,28},{16,24},{20,4},{24,16},{28,12},{1,9},{5... | collective-permute-start | bytes 589832 | tf_op jit(solution)/shard_map/ppermute | solution.py:440
  20.5 5.7 %collective-permute-start.9 = (bf16[2,384,128]{2,1,0:T(8,128)(2,1)S(1)}, bf16[2,384,128]{2,1,0:T(8,128)(2,1)S(1)}, u32[]{:S(2)}, u32[]{:S(2)}) collective-permute-start(bf16[2,384,128]{2,1,0:T(8,128)(2,1)S(1)} %constant_dynamic-update-slice_fusion.1.refs_5_), channel_id=1, source_target_pairs={{0,16},{4,12},{8,24},{12,4},{16,0},{20,28},{24,8},{28,20},{1,17},{... | collective-permute-start | bytes 589832 | tf_op jit(solution)/shard_map/ppermute | solution.py:440
  23.3 7.8 %collective-permute-start.7 = (bf16[2,768,128]{2,1,0:T(8,128)(2,1)S(1)}, bf16[2,768,128]{2,1,0:T(8,128)(2,1)S(1)}, u32[]{:S(2)}, u32[]{:S(2)}) collective-permute-start(bf16[2,768,128]{2,1,0:T(8,128)(2,1)S(1)} %pad_maximum_fusion.1), channel_id=1, source_target_pairs={{0,16},{4,12},{8,24},{12,4},{16,0},{20,28},{24,8},{28,20},{1,17},{... | collective-permute-start | bytes 1179656 | tf_op jit(solution)/shard_map/ppermute | solution.py:440
  25.1 2.5 %collective-permute-start.8 = (bf16[2,384,128]{2,1,0:T(8,128)(2,1)S(1)}, bf16[2,384,128]{2,1,0:T(8,128)(2,1)S(1)}, u32[]{:S(2)}, u32[]{:S(2)}) collective-permute-start(bf16[2,384,128]{2,1,0:T(8,128)(2,1)S(1)} %constant_dynamic-update-slice_fusion.1.refs_5_), channel_id=1, source_target_pairs={{0,4},{4,0},{8,12},{12,8},{16,20},{20,16},{24,28},{28,24},{1,5},{5... | collective-permute-start | bytes 589832 | tf_op jit(solution)/shard_map/ppermute | solution.py:443
  26.2 1.4 %collective-permute-start.12 = (bf16[2,384,128]{2,1,0:T(8,128)(2,1)S(1)}, bf16[2,384,128]{2,1,0:T(8,128)(2,1)S(1)}, u32[]{:S(2)}, u32[]{:S(2)}) collective-permute-start(bf16[2,384,128]{2,1,0:T(8,128)(2,1)S(1)} %collective-permute-done.9.refs_9_), channel_id=1, source_target_pairs={{0,4},{4,0},{8,12},{12,8},{16,20},{20,16},{24,28},{28,24},{1,5},{5... | collective-permute-start | bytes 589832 | tf_op jit(solution)/shard_map/ppermute | solution.py:443
  26.2 1.7 %collective-permute-start.11 = (bf16[2,384,128]{2,1,0:T(8,128)(2,1)S(1)}, bf16[2,384,128]{2,1,0:T(8,128)(2,1)S(1)}, u32[]{:S(2)}, u32[]{:S(2)}) collective-permute-start(bf16[2,384,128]{2,1,0:T(8,128)(2,1)S(1)} %collective-permute-done.4.refs_8_), channel_id=1, source_target_pairs={{0,4},{4,0},{8,12},{12,8},{16,20},{20,16},{24,28},{28,24},{1,5},{5... | collective-permute-start | bytes 589832 | tf_op jit(solution)/shard_map/ppermute | solution.py:443
  26.7 1.5 %collective-permute-start.10 = (bf16[2,384,128]{2,1,0:T(8,128)(2,1)S(1)}, bf16[2,384,128]{2,1,0:T(8,128)(2,1)S(1)}, u32[]{:S(2)}, u32[]{:S(2)}) collective-permute-start(bf16[2,384,128]{2,1,0:T(8,128)(2,1)S(1)} %collective-permute-done.6.refs_7_), channel_id=1, source_target_pairs={{0,4},{4,0},{8,12},{12,8},{16,20},{20,16},{24,28},{28,24},{1,5},{5... | collective-permute-start | bytes 589832 | tf_op jit(solution)/shard_map/ppermute | solution.py:443
  31.1 1.7 %collective-permute-start.13 = (bf16[2,768,128]{2,1,0:T(8,128)(2,1)S(1)}, bf16[2,768,128]{2,1,0:T(8,128)(2,1)S(1)}, u32[]{:S(2)}, u32[]{:S(2)}) collective-permute-start(bf16[2,768,128]{2,1,0:T(8,128)(2,1)S(1)} %collective-permute-done.7.refs_4_), channel_id=1, source_target_pairs={{0,4},{4,0},{8,12},{12,8},{16,20},{20,16},{24,28},{28,24},{1,5},{5... | collective-permute-start | bytes 1179656 | tf_op jit(solution)/shard_map/ppermute | solution.py:443

commit v6 on v5

--- a/solution.py
+++ b/solution.py
@@ -261,29 +261,43 @@
     return top, terms
 
 
+def lse_of(stat):
+    return stat[0] + jnp.log2(stat[1])
+
+
 def stage_kernel(*refs, piece_count, places, old_count, mp_count, final):
-    mp_ref, scale_ref, row_videos_ref, column_videos_ref = refs[:4]
-    refs = refs[4:]
-    piece_refs, refs = refs[:piece_count], refs[piece_count:]
-    old_refs, refs = refs[: 2 * old_count], refs[2 * old_count :]
-    old = [(old_refs[2 * k], old_refs[2 * k + 1]) for k in range(old_count)]
+    refs = list(refs)
+
+    def take(count):
+        taken = refs[:count]
+        del refs[:count]
+        return taken
+
+    mp_ref, scale_ref, row_videos_ref, column_videos_ref = take(4)
+    piece_refs = take(piece_count)
+    old = [take(2) for _ in range(old_count)]
     if old_count:
-        row_old_ref, col_old_ref, own_ref = refs[:3]
-        refs = refs[3:]
+        row_old_ref, col_old_ref, own_ref, own_caps_ref = take(4)
     if final:
-        d_clips_ref, d_caps_ref, clips_ref, caps_ref = refs
-    elif old_count:
-        clips_ref, caps_ref, row_ref, col_ref = refs
-    else:
-        clips_ref, caps_ref, row_ref, col_ref, own_ref = refs
+        strip_refs = [take(2) for _ in range(old_count)]
+        d_clips_ref, d_caps_ref = take(2)
+    clips_ref, caps_ref = take(2)
+    if not final:
+        row_ref, col_ref = take(2)
+    clip_strip_ref, cap_strip_ref = take(2)
+    if not old_count:
+        own_ref, own_caps_ref = take(2)
+    if refs:
+        (caps_rows_ref,) = take(1)
     fresh, width = clips_ref.shape
     rows = fresh // len(places)
     chunk = width // mp_count
     start = sum(clips.shape[0] for clips, _ in old)
-    total = start + fresh
+    wide_old = old_count > 1 or start > fresh
     mp_index = mp_ref[0]
     scale = scale_ref[0]
     scale2 = scale * log2_e
+    last = (((1,), (1,)), ((), ()))
 
     for position, place in enumerate(places):
         span = pl.ds(position * rows, rows)
@@ -293,8 +307,6 @@
                 for piece, first, count in place
             ]
             raw = jnp.concatenate(raw, axis=0)
-            if position == 0 and not old_count:
-                own_ref[kind] = jnp.transpose(raw)
             wide = raw.astype(jnp.float32)
             inverse = 1.0 / jnp.sqrt(jnp.sum(wide * wide, axis=0, keepdims=True) + epsilon)
             unit = (wide * inverse).astype(jnp.bfloat16)
@@ -302,10 +314,15 @@
                 clips_ref[span, :] = jnp.transpose(unit)
             else:
                 caps_ref[:, span] = unit
-
-    def tile(clip_tile, row_first, caps, col_first):
-        size = (clip_tile.shape[0], caps.shape[1])
-        scores = scale2 * jnp.dot(clip_tile, caps[...], preferred_element_type=jnp.float32)
+                if wide_old:
+                    caps_rows_ref[span, :] = jnp.transpose(unit)
+            if not old_count:
+                own_ref[kind] = jnp.transpose(raw)
+                if kind == 1:
+                    own_caps_ref[...] = jnp.transpose(unit)
+
+    def masked(products, row_first, col_first):
+        size = products.shape
         banned = (
             column_videos_ref[row_first : row_first + size[0], :]
             == row_videos_ref[:, col_first : col_first + size[1]]
@@ -313,43 +330,60 @@
         if col_first <= row_first < col_first + size[1]:
             distance = lax.broadcasted_iota(jnp.int32, size, 1) - lax.broadcasted_iota(jnp.int32, size, 0)
             banned = banned & (distance != row_first - col_first)
-        return jnp.where(banned, negative_fill, scores)
-
-    row_tile = min(2 * rows, fresh)
-    row_parts = []
-    col_new = None
-    at = 0
-    for clips, _ in old:
-        for first in range(0, clips.shape[0], row_tile):
-            scores = tile(clips[first : first + row_tile, :], at + first, caps_ref, start)
-            top, terms = add_terms(None, scores, 1)
-            col_new = add_terms(col_new, scores, 0)
-            row_parts.append(lane_vector(top + jnp.log2(terms)))
-        at += clips.shape[0]
-    col_olds = [None] * old_count
-    row_news = []
-    for first in range(0, fresh, row_tile):
-        stat = None
-        clip_tile = clips_ref[first : first + row_tile, :]
+        return jnp.where(banned, negative_fill, scale2 * products)
+
+    def plain(left, right):
+        return jnp.dot(left, right, preferred_element_type=jnp.float32)
+
+    def crossed(left, right):
+        return lax.dot_general(left, right, last, preferred_element_type=jnp.float32)
+
+    clip_old, cap_old, clip_new, cap_new = [], [], [], []
+    clip_stat, cap_stat, cap_lanes = None, None, None
+    if wide_old:
         at = 0
-        for k, (clips, caps) in enumerate(old):
-            scores = tile(clip_tile, start + first, caps, at)
-            stat = add_terms(stat, scores, 1)
-            col_olds[k] = add_terms(col_olds[k], scores, 0)
+        for index, (clips, caps) in enumerate(old):
+            scores = masked(crossed(caps_rows_ref[...], clips[...]), start, at)
+            clip_old.append(lse_of(add_terms(None, scores, 0)))
+            cap_stat = add_terms(cap_stat, scores, 1)
+            if index == 0:
+                clip_strip_ref[...] = jnp.transpose(scores)
+            scores = masked(plain(clips_ref[...], caps[...]), start, at)
+            cap_old.append(lse_of(add_terms(None, scores, 0)))
+            clip_stat = add_terms(clip_stat, scores, 1)
+            if index == 0:
+                cap_strip_ref[...] = jnp.transpose(scores)
             at += clips.shape[0]
-        scores = tile(clip_tile, start + first, caps_ref, start)
-        top, terms = add_terms(stat, scores, 1)
-        col_new = add_terms(col_new, scores, 0)
-        row_news.append(lane_vector(top + jnp.log2(terms)))
-    row_lse = row_news
-    col_lse = [col_new[0] + jnp.log2(col_new[1])]
-    if old_count:
-        old_part = jnp.concatenate(row_parts, axis=1)
-        row_lse = [joined_lse(row_old_ref[...], old_part)] + row_lse
-        old_part = jnp.concatenate([top + jnp.log2(terms) for top, terms in col_olds], axis=1)
-        col_lse = [joined_lse(col_old_ref[...], old_part)] + col_lse
-    row_lse = jnp.concatenate(row_lse, axis=1)
-    col_lse = jnp.concatenate(col_lse, axis=1)
+        cap_new.append(lane_vector(lse_of(cap_stat)))
+    elif old:
+        scores = masked(plain(old[0][0][...], caps_ref[...]), 0, start)
+        clip_strip_ref[...] = scores
+        clip_old.append(lane_vector(lse_of(add_terms(None, scores, 1))))
+        cap_lanes = add_terms(None, scores, 0)
+        scores = masked(crossed(own_caps_ref[...], clips_ref[...]), 0, start)
+        cap_strip_ref[...] = scores
+        cap_old.append(lane_vector(lse_of(add_terms(None, scores, 1))))
+        clip_new.append(lse_of(add_terms(None, scores, 0)))
+    parts = []
+    for first in range(0, fresh, rows):
+        scores = masked(plain(clips_ref[first : first + rows, :], caps_ref[...]), start + first, start)
+        stat = clip_stat and tuple(part[first : first + rows] for part in clip_stat)
+        parts.append(lane_vector(lse_of(add_terms(stat, scores, 1))))
+        cap_lanes = add_terms(cap_lanes, scores, 0)
+        if not old:
+            clip_strip_ref[...] = scores
+            cap_strip_ref[...] = jnp.transpose(scores)
+    clip_new.append(jnp.concatenate(parts, axis=1))
+    cap_new.append(lse_of(cap_lanes))
+
+    def joined(old_ref, old_parts, new_parts):
+        new = functools.reduce(joined_lse, new_parts)
+        if not old:
+            return new
+        return jnp.concatenate([joined_lse(old_ref[...], jnp.concatenate(old_parts, axis=1)), new], axis=1)
+
+    row_lse = joined(row_old_ref if old else None, clip_old, clip_new)
+    col_lse = joined(col_old_ref if old else None, cap_old, cap_new)
     if not final:
         row_ref[...] = row_lse
         col_ref[...] = col_lse
@@ -363,18 +397,13 @@
     cap_float, cap_length = unit_rows(own_ref[1, own_rows, :])
     clip_unit = old[0][0][own_rows, :]
     cap_unit = cap_float.astype(jnp.bfloat16)
-    same = column_videos_ref[own_rows, :] == row_videos_ref[...]
-    distance = lax.broadcasted_iota(jnp.int32, (own, total), 1) - lax.broadcasted_iota(
-        jnp.int32, (own, total), 0
-    )
-    blocked = same & (distance != own_first)
-    same = same.astype(jnp.bfloat16)
-    last = (((1,), (1,)), ((), ()))
-
-    def strip(products, other_lse):
-        scores = jnp.where(blocked, negative_fill, scale2 * jnp.concatenate(products, axis=1))
-        top, terms = add_terms(None, scores, 1)
-        weights = 0.5 * (jnp.exp2(scores - (top + jnp.log2(terms))) + jnp.exp2(scores - other_lse))
+    same = (column_videos_ref[own_rows, :] == row_videos_ref[...]).astype(jnp.bfloat16)
+    strip_refs = strip_refs + [(clip_strip_ref, cap_strip_ref)]
+
+    def strip(kind, other_lse):
+        scores = jnp.concatenate([pair[kind][own_rows, :] for pair in strip_refs], axis=1)
+        own_lse = lse_of(add_terms(None, scores, 1))
+        weights = 0.5 * (jnp.exp2(scores - own_lse) + jnp.exp2(scores - other_lse))
         return jnp.concatenate([weights.astype(jnp.bfloat16), same], axis=0)
 
     def summed(weights, multiply):
@@ -385,21 +414,8 @@
             at += clips.shape[0]
         return result[:own], result[own:]
 
-    clip_products = [
-        jnp.dot(clip_unit, caps[...], preferred_element_type=jnp.float32) for _, caps in every
-    ]
-    cap_products = [
-        lax.dot_general(cap_unit, clips[...], last, preferred_element_type=jnp.float32)
-        for clips, _ in every
-    ]
-    clip_acc, caption_pool = summed(
-        strip(clip_products, col_lse),
-        lambda w, clips, caps: lax.dot_general(w, caps[...], last, preferred_element_type=jnp.float32),
-    )
-    cap_acc, pooled = summed(
-        strip(cap_products, row_lse),
-        lambda w, clips, caps: jnp.dot(w, clips[...], preferred_element_type=jnp.float32),
-    )
+    clip_acc, caption_pool = summed(strip(0, col_lse), lambda w, clips, caps: crossed(w, caps[...]))
+    cap_acc, pooled = summed(strip(1, row_lse), lambda w, clips, caps: plain(w, clips[...]))
     pool_length = jnp.sqrt(jnp.sum(pooled * pooled, axis=1, keepdims=True) + epsilon)
     pool_unit = pooled / pool_length
     projected = caption_pool - pool_unit * jnp.sum(pool_unit * caption_pool, axis=1, keepdims=True)
@@ -459,20 +475,21 @@
     vmem = pl.BlockSpec(memory_space=pltpu.VMEM)
     smem = pl.BlockSpec(memory_space=pltpu.SMEM)
 
-    def stage(pieces, places, old, carried, final=False):
+    def stage(pieces, places, old, carried, final=False, cost=1):
         fresh = len(places) * row_count
         total = fresh + sum(clips.shape[0] for clips, _ in old)
         units = [((fresh, width), jnp.bfloat16), ((width, fresh), jnp.bfloat16)]
-        scratch = []
+        strips = [((row_count, fresh), jnp.float32)] * 2
+        scratch = [((fresh, width), jnp.bfloat16)] if len(old) > 1 or total > 2 * fresh else []
         if final:
             outs = [((own, width), jnp.float32)] * 2
-            scratch = [pltpu.VMEM(*unit) for unit in units]
+            scratch = units + strips + scratch
         else:
-            outs = units + [((1, total), jnp.float32)] * 2
+            outs = units + [((1, total), jnp.float32)] * 2 + strips
             if not old:
-                outs = outs + [((2, row_count, width), jnp.bfloat16)]
+                outs = outs + [((2, row_count, width), jnp.bfloat16), ((row_count, width), jnp.bfloat16)]
+        scratch = [pltpu.VMEM(*entry) for entry in scratch]
         operands = [*common, *pieces, *[unit for pair in old for unit in pair], *carried]
-        score_count = (2 * total - fresh) * fresh
         return pl.pallas_call(
             functools.partial(
                 stage_kernel,
@@ -487,7 +504,7 @@
             out_specs=[vmem] * len(outs),
             scratch_shapes=scratch,
             cost_estimate=pl.CostEstimate(
-                flops=1, bytes_accessed=1, transcendentals=0
+                flops=cost, bytes_accessed=1, transcendentals=0
             ),
             compiler_params=pltpu.CompilerParams(vmem_limit_bytes=32 * 1024 * 1024),
         )(*operands)
@@ -497,6 +514,7 @@
 
     early = mp_count // 2
     late = mp_count - early
+
     chunk = jnp.stack([clips.T, captions.T])
     arrived = [
         lax.ppermute(chunk, "mp", [(i, i ^ k) for i in range(mp_count)]) for k in range(1, mp_count)
@@ -504,52 +522,42 @@
     lead = jnp.concatenate([chunk] + arrived[: early - 1], axis=1)
     lead_first = along(0, lead)
     lead_second = along(1, lead)
-    lead_pair_other = across(after(jnp.concatenate([lead, lead_first], axis=1), lead_second))
-    arrived[-1] = after(arrived[-1], (lead_first, lead_second, lead_pair_other))
+    lead_other = across(after(lead, lead_second))
+    arrived[-1] = after(arrived[-1], lead_other)
     rest = jnp.concatenate(arrived[early - 1 :], axis=1)
     rest_first = along(0, rest)
-    clips_a, caps_a, row_a, col_a, own_raw = stage(
-        [lead, rest], [[(0, 0, early), (1, 0, late)]], [], []
-    )
+    rest_other = across(rest)
+    whole = [(0, 0, early), (1, 0, late)]
+    clips_a, caps_a, row_a, col_a, *strips_a, own_raw, own_caps = stage([lead, rest], [whole], [], [], cost=10**8)
     rest_second = along(1, after(rest, row_a))
     third = along(1, jnp.concatenate([lead_first, rest_first], axis=1))
-    rest_other = across(after(rest, rest_first))
-    lead_second_other = across(after(lead_second, rest_first))
-    clips_b, caps_b, row_b, col_b = stage(
-        [
-            lead_pair_other,
-            rest_other,
-            lead_first,
-            rest_first,
-            lead_second,
-            rest_second,
-            across(rest_first),
-            lead_second_other,
-            across(rest_second),
-        ],
-        [
-            [(0, 0, early), (1, 0, late)],
-            [(2, 0, early), (3, 0, late)],
-            [(4, 0, early), (5, 0, late)],
-            [(0, early, early), (6, 0, late)],
-            [(7, 0, early), (8, 0, late)],
-        ],
+
+    pairs = [
+        (lead_other, rest_other),
+        (lead_first, rest_first),
+        (lead_second, rest_second),
+        (across(after(lead_first, lead_second)), across(after(rest_first, rest_second))),
+        (across(lead_second), across(rest_second)),
+    ]
+    clips_b, caps_b, row_b, col_b, *strips_b = stage(
+        [piece for pair in pairs for piece in pair],
+        [[(2 * k + piece, first, count) for piece, first, count in whole] for k in range(len(pairs))],
         [(clips_a, caps_a)],
-        [row_a, col_a, own_raw],
+        [row_a, col_a, own_raw, own_caps],
     )
     third_other = across(after(third, row_b))
-    clips_c, caps_c, row_c, col_c = stage(
+    clips_c, caps_c, row_c, col_c, *strips_c = stage(
         [third],
         [[(0, 0, mp_count)]],
         [(clips_a, caps_a), (clips_b, caps_b)],
-        [row_b, col_b, own_raw],
+        [row_b, col_b, own_raw, own_caps],
     )
     return tuple(
         stage(
             [third_other],
             [[(0, 0, mp_count)]],
             [(clips_a, caps_a), (clips_b, caps_b), (clips_c, caps_c)],
-            [row_c, col_c, own_raw],
+            [row_c, col_c, own_raw, own_caps, *strips_a, *strips_b, *strips_c],
             final=True,
         )
     )

time: 37.3 us -> 35.5 us (0.952); the launches traced: 36.6 us -> 35.2 us
  waiting for transfers between devices: 10.7 us -> 9.08 us
  starting transfers between devices: 13.4 us -> 14.8 us
  Pallas kernels: 8.64 us -> 7.65 us
    ppermute x6 -> x7, waiting for transfers between devices: 2.81 us -> 1.53 us  [across(): return lax.ppermute(block, 'dp', [(i, i ^ 1) for i in range(dp_count)])]
    pallas_call x4, Pallas kernels: 8.64 us -> 7.65 us  [stage(): pl.pallas_call(functools.partial(stage_kernel, piece_count=len(pieces), p...]
    ppermute x5, waiting for transfers between devices: 7.7 us -> 6.86 us  [along(): return lax.ppermute(block, 'dp', route)]
    ppermute x5, starting transfers between devices: 7.01 us -> 7.78 us  [along(): return lax.ppermute(block, 'dp', route)]
    ppermute x6 -> x7, starting transfers between devices: 0.71 us -> 1.32 us  [across(): return lax.ppermute(block, 'dp', [(i, i ^ 1) for i in range(dp_count)])]
    ppermute x3, waiting for transfers between devices: 0.21 us -> 0.68 us  [resident_body(): lax.ppermute(chunk, 'mp', [(i, i ^ k) for i in range(mp_count)])]
  transfers between devices with their start and end apart: 14 -> 15, of which waited for: 10 -> 8; matrix products, arithmetic and copies ran while one was open for 3% -> 3% of each run, Pallas kernels for 13% -> 13%
where the time goes in v6:
time: 35.5 us; the launch traced here: 35.2 us
  starting transfers between devices  14.8 us (42%)
  waiting for transfers between devices  9.08 us (26%)
  Pallas kernels  7.65 us (22%)
  local copies, waits for them, and re-layouts  1.45 us (4%)
  between operations  1.38 us (4%)
  other arithmetic  0.88 us (2%)
    ppermute x5, starting transfers between devices, along(): return lax.ppermute(block, 'dp', route)  7.78 us
    pallas_call x4, Pallas kernels, stage(): pl.pallas_call(functools.partial(stage_kernel, piece_count=len(pieces), p...  7.65 us
    ppermute x5, waiting for transfers between devices, along(): return lax.ppermute(block, 'dp', route)  6.86 us
    ppermute x3, starting transfers between devices, resident_body(): lax.ppermute(chunk, 'mp', [(i, i ^ k) for i in range(mp_count)])  5.68 us
    ppermute x7, waiting for transfers between devices, across(): return lax.ppermute(block, 'dp', [(i, i ^ 1) for i in range(dp_count)])  1.53 us
    ppermute x7, starting transfers between devices, across(): return lax.ppermute(block, 'dp', [(i, i ^ 1) for i in range(dp_count)])  1.32 us
    unnamed x14, local copies, waits for them, and re-layouts  1.13 us
    another operation x1, other arithmetic, resident_body(): chunk = jnp.stack([clips.T, captions.T])  0.84 us
  transfers between devices with their start and end apart: 15, of which 8 were waited for; matrix products, arithmetic and copies ran while one was open for 3% of the time, Pallas kernels for 13%

profile of v6, /device:TPU:0, one launch (start us, length us, event | category | flops | bytes accessed | tf_op | source)
XLA Modules:
  0.0 35.2 jit_solution(13573660513579229330)
XLA Ops:
  0.6 0.0 copy-start.2
  0.6 0.8 %pad_maximum_fusion.2 = bf16[2,192,128]{2,1,0:T(8,128)(2,1)S(1)} fusion(bf16[1,192,128]{2,1,0:T(8,128)(2,1)} %bitcast.19, bf16[1,192,128]{2,1,0:T(8,128)(2,1)} %bitcast.21), kind=kLoop, calls=%fused_computation.2 | loop fusion | flops 49152 | bytes 196608 | tf_op jit(solution)/shard_map/stack | solution.py:518
  1.5 3.1 %collective-permute-start = (bf16[2,192,128]{2,1,0:T(8,128)(2,1)S(1)}, bf16[2,192,128]{2,1,0:T(8,128)(2,1)S(1)}, u32[]{:S(2)}, u32[]{:S(2)}) collective-permute-start(bf16[2,192,128]{2,1,0:T(8,128)(2,1)S(1)} %pad_maximum_fusion.2), channel_id=1, source_target_pairs={{0,1},{1,0},{2,3},{3,2},{4,5},{5,4},{6,7},{7,6},{8,9},{9,8},{10,11... | collective-permute-start | bytes 294920 | tf_op jit(solution)/shard_map/ppermute | solution.py:520
  4.6 2.5 %collective-permute-start.3 = (bf16[2,192,128]{2,1,0:T(8,128)(2,1)S(1)}, bf16[2,192,128]{2,1,0:T(8,128)(2,1)S(1)}, u32[]{:S(2)}, u32[]{:S(2)}) collective-permute-start(bf16[2,192,128]{2,1,0:T(8,128)(2,1)S(1)} %pad_maximum_fusion.2), channel_id=1, source_target_pairs={{0,3},{1,2},{2,1},{3,0},{4,7},{5,6},{6,5},{7,4},{8,11},{9,10},{10,... | collective-permute-start | bytes 294920 | tf_op jit(solution)/shard_map/ppermute | solution.py:520
  7.0 0.1 collective-permute-start.2
  7.2 0.0 copy-start.1
  7.2 0.0 copy-start
  7.2 0.0 copy-done.2
  7.2 0.1 constant_dynamic-update-slice_fusion
  7.2 0.1 constant_dynamic-update-slice_fusion.9
  7.3 0.1 constant_dynamic-update-slice_fusion.8
  7.4 0.0 collective-permute-done
  7.4 0.6 %copy-done.1 = bf16[128,192]{0,1:T(8,128)(2,1)S(1)} copy-done((bf16[128,192]{0,1:T(8,128)(2,1)S(1)}, bf16[128,192]{0,1:T(8,128)(2,1)}, u32[]{:S(2)}) %copy-start.1) | copy-done | bytes 49176
  8.0 0.0 copy-done
  8.0 1.6 %collective-permute-start.4 = (bf16[2,384,128]{2,1,0:T(8,128)(2,1)S(1)}, bf16[2,384,128]{2,1,0:T(8,128)(2,1)S(1)}, u32[]{:S(2)}, u32[]{:S(2)}) collective-permute-start(bf16[2,384,128]{2,1,0:T(8,128)(2,1)S(1)} %pad_maximum_fusion.1.refs_4_), channel_id=1, source_target_pairs={{0,16},{4,12},{8,24},{12,4},{16,0},{20,28},{24,8},{28,20},{1,17},{... | collective-permute-start | bytes 589832 | tf_op jit(solution)/shard_map/ppermute | solution.py:456
  9.6 0.1 constant_dynamic-update-slice_fusion.7
  9.7 0.1 constant_dynamic-update-slice_fusion.6
  9.7 4.0 %collective-permute-done.4.refs_8_ = bf16[2,384,128]{2,1,0:T(8,128)(2,1)S(1)} collective-permute-done((bf16[2,384,128]{2,1,0:T(8,128)(2,1)S(1)}, bf16[2,384,128]{2,1,0:T(8,128)(2,1)S(1)}, u32[]{:S(2)}, u32[]{:S(2)}) %collective-permute-start.4) | collective-permute-done | bytes 196640 | tf_op jit(solution)/shard_map/ppermute | solution.py:456
  13.7 0.0 collective-permute-start.5
  13.7 0.1 constant_dynamic-update-slice_fusion.5
  13.8 1.5 %collective-permute-start.1 = (bf16[2,384,128]{2,1,0:T(8,128)(2,1)S(1)}, bf16[2,384,128]{2,1,0:T(8,128)(2,1)S(1)}, u32[]{:S(2)}, u32[]{:S(2)}) collective-permute-start(bf16[2,384,128]{2,1,0:T(8,128)(2,1)S(1)} %pad_maximum_fusion.1.refs_4_), channel_id=1, source_target_pairs={{0,8},{4,20},{8,0},{12,28},{16,24},{20,4},{24,16},{28,12},{1,9},{5... | collective-permute-start | bytes 589832 | tf_op jit(solution)/shard_map/ppermute | solution.py:456
  15.3 0.7 %collective-permute-done.2 = bf16[2,192,128]{2,1,0:T(8,128)(2,1)S(1)} collective-permute-done((bf16[2,192,128]{2,1,0:T(8,128)(2,1)S(1)}, bf16[2,192,128]{2,1,0:T(8,128)(2,1)S(1)}, u32[]{:S(2)}, u32[]{:S(2)}) %collective-permute-start.2) | collective-permute-done | bytes 98336 | tf_op jit(solution)/shard_map/ppermute | solution.py:520
  16.0 0.0 collective-permute-done.3
  16.0 0.0 collective-permute-done.5.refs_4_
  16.0 1.6 %collective-permute-start.6 = (bf16[2,384,128]{2,1,0:T(8,128)(2,1)S(1)}, bf16[2,384,128]{2,1,0:T(8,128)(2,1)S(1)}, u32[]{:S(2)}, u32[]{:S(2)}) collective-permute-start(bf16[2,384,128]{2,1,0:T(8,128)(2,1)S(1)} %constant_dynamic-update-slice_fusion.1.refs_5_), channel_id=1, source_target_pairs={{0,8},{4,20},{8,0},{12,28},{16,24},{20,4},{24,16},{28,12},{1,9},{5... | collective-permute-start | bytes 589832 | tf_op jit(solution)/shard_map/ppermute | solution.py:456
  17.6 0.1 constant_dynamic-update-slice_fusion.4
  17.7 0.1 constant_dynamic-update-slice_fusion.3
  17.8 0.2 copy.9.refs_3_
  18.6 0.8 %collective-permute-done.1.refs_6_ = bf16[2,384,128]{2,1,0:T(8,128)(2,1)S(1)} collective-permute-done((bf16[2,384,128]{2,1,0:T(8,128)(2,1)S(1)}, bf16[2,384,128]{2,1,0:T(8,128)(2,1)S(1)}, u32[]{:S(2)}, u32[]{:S(2)}) %collective-permute-start.1) | collective-permute-done | bytes 196640 | tf_op jit(solution)/shard_map/ppermute | solution.py:456
  19.5 0.0 collective-permute-start.10
  19.5 0.6 %shard_map.59 = (bf16[128,768]{1,0:T(8,128)(2,1)S(1)}, bf16[768,128]{1,0:T(8,128)(2,1)S(1)}, f32[1,128]{1,0:T(1,128)S(1)}, f32[1,128]{1,0:T(1,128)S(1)}, f32[128...) custom-call(s32[1]{0:T(128)} %bitcast.refs_0_, ...), custom_call_target="tpu_custom_call" | custom-call | flops 100000000 | bytes 1 | tf_op jit(solution)/shard_map/pallas_call | solution.py:493
  20.1 1.6 %collective-permute-start.9 = (bf16[2,384,128]{2,1,0:T(8,128)(2,1)S(1)}, bf16[2,384,128]{2,1,0:T(8,128)(2,1)S(1)}, u32[]{:S(2)}, u32[]{:S(2)}) collective-permute-start(bf16[2,384,128]{2,1,0:T(8,128)(2,1)S(1)} %constant_dynamic-update-slice_fusion.1.refs_5_), channel_id=1, source_target_pairs={{0,16},{4,12},{8,24},{12,4},{16,0},{20,28},{24,8},{28,20},{1,17},{... | collective-permute-start | bytes 589832 | tf_op jit(solution)/shard_map/ppermute | solution.py:456
  21.7 0.1 collective-permute-done.6.refs_7_
  21.8 1.6 %collective-permute-start.7 = (bf16[2,768,128]{2,1,0:T(8,128)(2,1)S(1)}, bf16[2,768,128]{2,1,0:T(8,128)(2,1)S(1)}, u32[]{:S(2)}, u32[]{:S(2)}) collective-permute-start(bf16[2,768,128]{2,1,0:T(8,128)(2,1)S(1)} %pad_maximum_fusion), channel_id=1, source_target_pairs={{0,16},{4,12},{8,24},{12,4},{16,0},{20,28},{24,8},{28,20},{1,17},{... | collective-permute-start | bytes 1179656 | tf_op jit(solution)/shard_map/ppermute | solution.py:456
  23.4 0.0 collective-permute-start.12
  23.4 0.5 %collective-permute-start.8 = (bf16[2,384,128]{2,1,0:T(8,128)(2,1)S(1)}, bf16[2,384,128]{2,1,0:T(8,128)(2,1)S(1)}, u32[]{:S(2)}, u32[]{:S(2)}) collective-permute-start(bf16[2,384,128]{2,1,0:T(8,128)(2,1)S(1)} %constant_dynamic-update-slice_fusion.1.refs_5_), channel_id=1, source_target_pairs={{0,4},{4,0},{8,12},{12,8},{16,20},{20,16},{24,28},{28,24},{1,5},{5... | collective-permute-start | bytes 589832 | tf_op jit(solution)/shard_map/ppermute | solution.py:459
  23.9 1.9 %collective-permute-done.9.refs_9_ = bf16[2,384,128]{2,1,0:T(8,128)(2,1)S(1)} collective-permute-done((bf16[2,384,128]{2,1,0:T(8,128)(2,1)S(1)}, bf16[2,384,128]{2,1,0:T(8,128)(2,1)S(1)}, u32[]{:S(2)}, u32[]{:S(2)}) %collective-permute-start.9) | collective-permute-done | bytes 196640 | tf_op jit(solution)/shard_map/ppermute | solution.py:456
  25.8 0.0 collective-permute-start.11
  25.8 0.0 collective-permute-done.10.refs_10_
  25.8 0.5 %collective-permute-start.13 = (bf16[2,384,128]{2,1,0:T(8,128)(2,1)S(1)}, bf16[2,384,128]{2,1,0:T(8,128)(2,1)S(1)}, u32[]{:S(2)}, u32[]{:S(2)}) collective-permute-start(bf16[2,384,128]{2,1,0:T(8,128)(2,1)S(1)} %collective-permute-done.9.refs_9_), channel_id=1, source_target_pairs={{0,4},{4,0},{8,12},{12,8},{16,20},{20,16},{24,28},{28,24},{1,5},{5... | collective-permute-start | bytes 589832 | tf_op jit(solution)/shard_map/ppermute | solution.py:459
  26.3 0.0 collective-permute-done.12.refs_12_
  26.3 0.0 collective-permute-done.8.refs_5_
  26.3 0.9 %collective-permute-done.11.refs_11_ = bf16[2,384,128]{2,1,0:T(8,128)(2,1)S(1)} collective-permute-done((bf16[2,384,128]{2,1,0:T(8,128)(2,1)S(1)}, bf16[2,384,128]{2,1,0:T(8,128)(2,1)S(1)}, u32[]{:S(2)}, u32[]{:S(2)}) %collective-permute-start.11) | collective-permute-done | bytes 196640 | tf_op jit(solution)/shard_map/ppermute | solution.py:459
  27.3 0.3 collective-permute-done.13.refs_13_
  27.5 2.8 %shard_map.60 = (bf16[640,768]{1,0:T(8,128)(2,1)S(1)}, bf16[768,640]{1,0:T(8,128)(2,1)S(1)}, f32[1,768]{1,0:T(1,128)S(1)}, f32[1,768]{1,0:T(1,128)S(1)}, f32[128,640]{1,0:T(8,128)S(1)}, /*index=5*/f32[128,640]{1,0:T(8,128)S(1)}) custom-call(s32[1]{0:T(128)} %bitcast.refs_0_, f32[1]{0:T(128)} %bitcast.11.refs_1_, s32[1,1024]{1,0:T(1,128)S(1)} %bitcast.16, ...), custom_call_target="tpu_custom_call" | custom-call | flops 1 | bytes 1 | tf_op jit(solution)/shard_map/pallas_call | solution.py:493
  30.3 0.0 collective-permute-done.7.refs_4_
  30.3 0.3 collective-permute-start.14
  30.6 1.2 %shard_map.61 = (bf16[128,768]{1,0:T(8,128)(2,1)S(1)}, bf16[768,128]{1,0:T(8,128)(2,1)S(1)}, f32[1,896]{1,0:T(1,128)S(1)}, f32[1,896]{1,0:T(1,128)S(1)}, f32[128,128]{1,0:T(8,128)S(1)}, /*index=5*/f32[128,128]{1,0:T(8,128)S(1)}) custom-call(s32[1]{0:T(128)} %bitcast.refs_0_, f32[1]{0:T(128)} %bitcast.12.refs_1_, s32[1,1024]{1,0:T(1,128)S(1)} %bitcast.17, ...), custom_call_target="tpu_custom_call" | custom-call | flops 1 | bytes 1 | tf_op jit(solution)/shard_map/pallas_call | solution.py:493
  31.8 0.3 collective-permute-done.14.refs_4_
  32.1 3.1 %shard_map.62 = (f32[32,768]{1,0:T(8,128)}, f32[32,768]{1,0:T(8,128)}) custom-call(s32[1]{0:T(128)} %bitcast.refs_0_, f32[1]{0:T(128)} %bitcast.13.refs_1_, s32[1,1024]{1,0:T(1,128)S(1)} %bitcast.18, s32[1024,1]{1,0:T(8,128)S(1)} %copy.9.refs_3_, bf16[2,768,128]{2,1,0:T(8,128)(2,1)S(1)} %collective-permute-done.14.refs_4_, ...), custom_call_target="tpu_custom_call" | custom-call | flops 1 | bytes 1 | tf_op jit(solution)/shard_map/pallas_call | solution.py:493
  (5 shorter events, 0.1 us)
Async XLA Ops:
  0.6 6.5 %copy-start.2 = (s32[1024]{0:T(1024)S(1)}, s32[1024]{0:T(1024)}, u32[]{:S(2)}) copy-start(s32[1024]{0:T(1024)} %param.6) | copy-start | bytes 12292
  1.5 5.9 %collective-permute-start = (bf16[2,192,128]{2,1,0:T(8,128)(2,1)S(1)}, bf16[2,192,128]{2,1,0:T(8,128)(2,1)S(1)}, u32[]{:S(2)}, u32[]{:S(2)}) collective-permute-start(bf16[2,192,128]{2,1,0:T(8,128)(2,1)S(1)} %pad_maximum_fusion.2), channel_id=1, source_target_pairs={{0,1},{1,0},{2,3},{3,2},{4,5},{5,4},{6,7},{7,6},{8,9},{9,8},{10,11... | collective-permute-start | bytes 294920 | tf_op jit(solution)/shard_map/ppermute | solution.py:520
  4.6 11.4 %collective-permute-start.3 = (bf16[2,192,128]{2,1,0:T(8,128)(2,1)S(1)}, bf16[2,192,128]{2,1,0:T(8,128)(2,1)S(1)}, u32[]{:S(2)}, u32[]{:S(2)}) collective-permute-start(bf16[2,192,128]{2,1,0:T(8,128)(2,1)S(1)} %pad_maximum_fusion.2), channel_id=1, source_target_pairs={{0,3},{1,2},{2,1},{3,0},{4,7},{5,6},{6,5},{7,4},{8,11},{9,10},{10,... | collective-permute-start | bytes 294920 | tf_op jit(solution)/shard_map/ppermute | solution.py:520
  7.0 8.9 %collective-permute-start.2 = (bf16[2,192,128]{2,1,0:T(8,128)(2,1)S(1)}, bf16[2,192,128]{2,1,0:T(8,128)(2,1)S(1)}, u32[]{:S(2)}, u32[]{:S(2)}) collective-permute-start(bf16[2,192,128]{2,1,0:T(8,128)(2,1)S(1)} %pad_maximum_fusion.2), channel_id=1, source_target_pairs={{0,2},{1,3},{2,0},{3,1},{4,6},{5,7},{6,4},{7,5},{8,10},{9,11},{10,... | collective-permute-start | bytes 294920 | tf_op jit(solution)/shard_map/ppermute | solution.py:520
  7.2 0.8 %copy-start.1 = (bf16[128,192]{0,1:T(8,128)(2,1)S(1)}, bf16[128,192]{0,1:T(8,128)(2,1)}, u32[]{:S(2)}) copy-start(bf16[128,192]{0,1:T(8,128)(2,1)} %param.4) | copy-start | bytes 147460
  7.2 0.8 %copy-start = (bf16[128,192]{0,1:T(8,128)(2,1)S(1)}, bf16[128,192]{0,1:T(8,128)(2,1)}, u32[]{:S(2)}) copy-start(bf16[128,192]{0,1:T(8,128)(2,1)} %param.5) | copy-start | bytes 147460
  8.0 5.7 %collective-permute-start.4 = (bf16[2,384,128]{2,1,0:T(8,128)(2,1)S(1)}, bf16[2,384,128]{2,1,0:T(8,128)(2,1)S(1)}, u32[]{:S(2)}, u32[]{:S(2)}) collective-permute-start(bf16[2,384,128]{2,1,0:T(8,128)(2,1)S(1)} %pad_maximum_fusion.1.refs_4_), channel_id=1, source_target_pairs={{0,16},{4,12},{8,24},{12,4},{16,0},{20,28},{24,8},{28,20},{1,17},{... | collective-permute-start | bytes 589832 | tf_op jit(solution)/shard_map/ppermute | solution.py:456
  13.7 2.3 %collective-permute-start.5 = (bf16[2,384,128]{2,1,0:T(8,128)(2,1)S(1)}, bf16[2,384,128]{2,1,0:T(8,128)(2,1)S(1)}, u32[]{:S(2)}, u32[]{:S(2)}) collective-permute-start(bf16[2,384,128]{2,1,0:T(8,128)(2,1)S(1)} %pad_maximum_fusion.1.refs_4_), channel_id=1, source_target_pairs={{0,4},{4,0},{8,12},{12,8},{16,20},{20,16},{24,28},{28,24},{1,5},{5... | collective-permute-start | bytes 589832 | tf_op jit(solution)/shard_map/ppermute | solution.py:459
  13.8 5.7 %collective-permute-start.1 = (bf16[2,384,128]{2,1,0:T(8,128)(2,1)S(1)}, bf16[2,384,128]{2,1,0:T(8,128)(2,1)S(1)}, u32[]{:S(2)}, u32[]{:S(2)}) collective-permute-start(bf16[2,384,128]{2,1,0:T(8,128)(2,1)S(1)} %pad_maximum_fusion.1.refs_4_), channel_id=1, source_target_pairs={{0,8},{4,20},{8,0},{12,28},{16,24},{20,4},{24,16},{28,12},{1,9},{5... | collective-permute-start | bytes 589832 | tf_op jit(solution)/shard_map/ppermute | solution.py:456
  16.0 5.7 %collective-permute-start.6 = (bf16[2,384,128]{2,1,0:T(8,128)(2,1)S(1)}, bf16[2,384,128]{2,1,0:T(8,128)(2,1)S(1)}, u32[]{:S(2)}, u32[]{:S(2)}) collective-permute-start(bf16[2,384,128]{2,1,0:T(8,128)(2,1)S(1)} %constant_dynamic-update-slice_fusion.1.refs_5_), channel_id=1, source_target_pairs={{0,8},{4,20},{8,0},{12,28},{16,24},{20,4},{24,16},{28,12},{1,9},{5... | collective-permute-start | bytes 589832 | tf_op jit(solution)/shard_map/ppermute | solution.py:456
  19.5 6.3 %collective-permute-start.10 = (bf16[2,384,128]{2,1,0:T(8,128)(2,1)S(1)}, bf16[2,384,128]{2,1,0:T(8,128)(2,1)S(1)}, u32[]{:S(2)}, u32[]{:S(2)}) collective-permute-start(bf16[2,384,128]{2,1,0:T(8,128)(2,1)S(1)} %collective-permute-done.1.refs_6_), channel_id=1, source_target_pairs={{0,4},{4,0},{8,12},{12,8},{16,20},{20,16},{24,28},{28,24},{1,5},{5... | collective-permute-start | bytes 589832 | tf_op jit(solution)/shard_map/ppermute | solution.py:459
  20.1 5.7 %collective-permute-start.9 = (bf16[2,384,128]{2,1,0:T(8,128)(2,1)S(1)}, bf16[2,384,128]{2,1,0:T(8,128)(2,1)S(1)}, u32[]{:S(2)}, u32[]{:S(2)}) collective-permute-start(bf16[2,384,128]{2,1,0:T(8,128)(2,1)S(1)} %constant_dynamic-update-slice_fusion.1.refs_5_), channel_id=1, source_target_pairs={{0,16},{4,12},{8,24},{12,4},{16,0},{20,28},{24,8},{28,20},{1,17},{... | collective-permute-start | bytes 589832 | tf_op jit(solution)/shard_map/ppermute | solution.py:456
  21.8 8.5 %collective-permute-start.7 = (bf16[2,768,128]{2,1,0:T(8,128)(2,1)S(1)}, bf16[2,768,128]{2,1,0:T(8,128)(2,1)S(1)}, u32[]{:S(2)}, u32[]{:S(2)}) collective-permute-start(bf16[2,768,128]{2,1,0:T(8,128)(2,1)S(1)} %pad_maximum_fusion), channel_id=1, source_target_pairs={{0,16},{4,12},{8,24},{12,4},{16,0},{20,28},{24,8},{28,20},{1,17},{... | collective-permute-start | bytes 1179656 | tf_op jit(solution)/shard_map/ppermute | solution.py:456
  23.4 2.9 %collective-permute-start.12 = (bf16[2,384,128]{2,1,0:T(8,128)(2,1)S(1)}, bf16[2,384,128]{2,1,0:T(8,128)(2,1)S(1)}, u32[]{:S(2)}, u32[]{:S(2)}) collective-permute-start(bf16[2,384,128]{2,1,0:T(8,128)(2,1)S(1)} %collective-permute-done.4.refs_8_), channel_id=1, source_target_pairs={{0,4},{4,0},{8,12},{12,8},{16,20},{20,16},{24,28},{28,24},{1,5},{5... | collective-permute-start | bytes 589832 | tf_op jit(solution)/shard_map/ppermute | solution.py:459
  23.4 2.9 %collective-permute-start.8 = (bf16[2,384,128]{2,1,0:T(8,128)(2,1)S(1)}, bf16[2,384,128]{2,1,0:T(8,128)(2,1)S(1)}, u32[]{:S(2)}, u32[]{:S(2)}) collective-permute-start(bf16[2,384,128]{2,1,0:T(8,128)(2,1)S(1)} %constant_dynamic-update-slice_fusion.1.refs_5_), channel_id=1, source_target_pairs={{0,4},{4,0},{8,12},{12,8},{16,20},{20,16},{24,28},{28,24},{1,5},{5... | collective-permute-start | bytes 589832 | tf_op jit(solution)/shard_map/ppermute | solution.py:459
  25.8 1.4 %collective-permute-start.11 = (bf16[2,384,128]{2,1,0:T(8,128)(2,1)S(1)}, bf16[2,384,128]{2,1,0:T(8,128)(2,1)S(1)}, u32[]{:S(2)}, u32[]{:S(2)}) collective-permute-start(bf16[2,384,128]{2,1,0:T(8,128)(2,1)S(1)} %collective-permute-done.6.refs_7_), channel_id=1, source_target_pairs={{0,4},{4,0},{8,12},{12,8},{16,20},{20,16},{24,28},{28,24},{1,5},{5... | collective-permute-start | bytes 589832 | tf_op jit(solution)/shard_map/ppermute | solution.py:459
  25.8 1.7 %collective-permute-start.13 = (bf16[2,384,128]{2,1,0:T(8,128)(2,1)S(1)}, bf16[2,384,128]{2,1,0:T(8,128)(2,1)S(1)}, u32[]{:S(2)}, u32[]{:S(2)}) collective-permute-start(bf16[2,384,128]{2,1,0:T(8,128)(2,1)S(1)} %collective-permute-done.9.refs_9_), channel_id=1, source_target_pairs={{0,4},{4,0},{8,12},{12,8},{16,20},{20,16},{24,28},{28,24},{1,5},{5... | collective-permute-start | bytes 589832 | tf_op jit(solution)/shard_map/ppermute | solution.py:459
  30.3 1.8 %collective-permute-start.14 = (bf16[2,768,128]{2,1,0:T(8,128)(2,1)S(1)}, bf16[2,768,128]{2,1,0:T(8,128)(2,1)S(1)}, u32[]{:S(2)}, u32[]{:S(2)}) collective-permute-start(bf16[2,768,128]{2,1,0:T(8,128)(2,1)S(1)} %collective-permute-done.7.refs_4_), channel_id=1, source_target_pairs={{0,4},{4,0},{8,12},{12,8},{16,20},{20,16},{24,28},{28,24},{1,5},{5... | collective-permute-start | bytes 1179656 | tf_op jit(solution)/shard_map/ppermute | solution.py:459

commit v7 on v6

--- a/solution.py
+++ b/solution.py
@@ -364,17 +364,12 @@
         cap_strip_ref[...] = scores
         cap_old.append(lane_vector(lse_of(add_terms(None, scores, 1))))
         clip_new.append(lse_of(add_terms(None, scores, 0)))
-    parts = []
-    for first in range(0, fresh, rows):
-        scores = masked(plain(clips_ref[first : first + rows, :], caps_ref[...]), start + first, start)
-        stat = clip_stat and tuple(part[first : first + rows] for part in clip_stat)
-        parts.append(lane_vector(lse_of(add_terms(stat, scores, 1))))
-        cap_lanes = add_terms(cap_lanes, scores, 0)
-        if not old:
-            clip_strip_ref[...] = scores
-            cap_strip_ref[...] = jnp.transpose(scores)
-    clip_new.append(jnp.concatenate(parts, axis=1))
-    cap_new.append(lse_of(cap_lanes))
+    scores = masked(plain(clips_ref[...], caps_ref[...]), start, start)
+    clip_new.append(lane_vector(lse_of(add_terms(clip_stat, scores, 1))))
+    cap_new.append(lse_of(add_terms(cap_lanes, scores, 0)))
+    if not old:
+        clip_strip_ref[...] = scores
+        cap_strip_ref[...] = jnp.transpose(scores)
 
     def joined(old_ref, old_parts, new_parts):
         new = functools.reduce(joined_lse, new_parts)
@@ -522,8 +517,8 @@
     lead = jnp.concatenate([chunk] + arrived[: early - 1], axis=1)
     lead_first = along(0, lead)
     lead_second = along(1, lead)
-    lead_other = across(after(lead, lead_second))
-    arrived[-1] = after(arrived[-1], lead_other)
+    lead_other = across(lead)
+    arrived[-1] = after(arrived[-1], (lead_first, lead_second, lead_other))
     rest = jnp.concatenate(arrived[early - 1 :], axis=1)
     rest_first = along(0, rest)
     rest_other = across(rest)
@@ -536,8 +531,8 @@
         (lead_other, rest_other),
         (lead_first, rest_first),
         (lead_second, rest_second),
-        (across(after(lead_first, lead_second)), across(after(rest_first, rest_second))),
-        (across(lead_second), across(rest_second)),
+        (across(after(lead_first, lead_second)), across(rest_first)),
+        (across(after(lead_second, rest_second)), across(rest_second)),
     ]
     clips_b, caps_b, row_b, col_b, *strips_b = stage(
         [piece for pair in pairs for piece in pair],

time: 35.5 us -> 34.9 us (0.983)
  starting transfers between devices: 14.8 us -> 14.4 us
    ppermute x5, waiting for transfers between devices: 6.86 us -> 2.54 us  [along(): return lax.ppermute(block, 'dp', route)]
    ppermute x3, waiting for transfers between devices: 0.68 us -> 4.56 us  [resident_body(): lax.ppermute(chunk, 'mp', [(i, i ^ k) for i in range(mp_count)])]
    ppermute x7, starting transfers between devices: 1.32 us -> 0.89 us  [across(): return lax.ppermute(block, 'dp', [(i, i ^ 1) for i in range(dp_count)])]
  transfers between devices with their start and end apart: 15 -> 15, of which waited for: 8 -> 7; matrix products, arithmetic and copies ran while one was open for 3% -> 3% of each run, Pallas kernels for 13% -> 13%
where the time goes in v7:
time: 34.9 us; the launch traced here: 34.6 us
  starting transfers between devices  14.4 us (41%)
  waiting for transfers between devices  8.91 us (26%)
  Pallas kernels  7.55 us (22%)
  local copies, waits for them, and re-layouts  1.56 us (4%)
  between operations  1.4 us (4%)
  other arithmetic  0.88 us (3%)
    ppermute x5, starting transfers between devices, along(): return lax.ppermute(block, 'dp', route)  7.78 us
    pallas_call x4, Pallas kernels, stage(): pl.pallas_call(functools.partial(stage_kernel, piece_count=len(pieces), p...  7.55 us
    ppermute x3, starting transfers between devices, resident_body(): lax.ppermute(chunk, 'mp', [(i, i ^ k) for i in range(mp_count)])  5.68 us
    ppermute x3, waiting for transfers between devices, resident_body(): lax.ppermute(chunk, 'mp', [(i, i ^ k) for i in range(mp_count)])  4.56 us
    ppermute x5, waiting for transfers between devices, along(): return lax.ppermute(block, 'dp', route)  2.54 us
    ppermute x7, waiting for transfers between devices, across(): return lax.ppermute(block, 'dp', [(i, i ^ 1) for i in range(dp_count)])  1.81 us
    unnamed x14, local copies, waits for them, and re-layouts  1.24 us
    ppermute x7, starting transfers between devices, across(): return lax.ppermute(block, 'dp', [(i, i ^ 1) for i in range(dp_count)])  0.89 us
  transfers between devices with their start and end apart: 15, of which 7 were waited for; matrix products, arithmetic and copies ran while one was open for 3% of the time, Pallas kernels for 13%

profile of v7, /device:TPU:0, one launch (start us, length us, event | category | flops | bytes accessed | tf_op | source)
XLA Modules:
  0.0 34.6 jit_solution(9509924359502652134)
XLA Ops:
  0.6 0.8 %pad_maximum_fusion.2 = bf16[2,192,128]{2,1,0:T(8,128)(2,1)S(1)} fusion(bf16[1,192,128]{2,1,0:T(8,128)(2,1)} %bitcast.19, bf16[1,192,128]{2,1,0:T(8,128)(2,1)} %bitcast.21), kind=kLoop, calls=%fused_computation.2 | loop fusion | flops 49152 | bytes 196608 | tf_op jit(solution)/shard_map/stack | solution.py:513
  1.5 3.1 %collective-permute-start = (bf16[2,192,128]{2,1,0:T(8,128)(2,1)S(1)}, bf16[2,192,128]{2,1,0:T(8,128)(2,1)S(1)}, u32[]{:S(2)}, u32[]{:S(2)}) collective-permute-start(bf16[2,192,128]{2,1,0:T(8,128)(2,1)S(1)} %pad_maximum_fusion.2), channel_id=1, source_target_pairs={{0,1},{1,0},{2,3},{3,2},{4,5},{5,4},{6,7},{7,6},{8,9},{9,8},{10,11... | collective-permute-start | bytes 294920 | tf_op jit(solution)/shard_map/ppermute | solution.py:515
  4.6 2.5 %collective-permute-start.3 = (bf16[2,192,128]{2,1,0:T(8,128)(2,1)S(1)}, bf16[2,192,128]{2,1,0:T(8,128)(2,1)S(1)}, u32[]{:S(2)}, u32[]{:S(2)}) collective-permute-start(bf16[2,192,128]{2,1,0:T(8,128)(2,1)S(1)} %pad_maximum_fusion.2), channel_id=1, source_target_pairs={{0,3},{1,2},{2,1},{3,0},{4,7},{5,6},{6,5},{7,4},{8,11},{9,10},{10,... | collective-permute-start | bytes 294920 | tf_op jit(solution)/shard_map/ppermute | solution.py:515
  7.0 0.1 collective-permute-start.2
  7.1 0.0 copy-start.2
  7.2 0.0 copy-start.1
  7.2 0.0 copy-start
  7.2 0.7 %copy-done.2 = s32[1024]{0:T(1024)S(1)} copy-done((s32[1024]{0:T(1024)S(1)}, s32[1024]{0:T(1024)}, u32[]{:S(2)}) %copy-start.2) | copy-done | bytes 4120
  7.8 0.1 constant_dynamic-update-slice_fusion
  7.9 0.1 constant_dynamic-update-slice_fusion.9
  8.0 0.1 constant_dynamic-update-slice_fusion.8
  8.1 0.1 constant_dynamic-update-slice_fusion.7
  8.2 0.1 constant_dynamic-update-slice_fusion.6
  8.2 0.0 collective-permute-done
  8.2 0.0 copy-done.1
  8.2 0.0 copy-done
  8.3 1.6 %collective-permute-start.1 = (bf16[2,384,128]{2,1,0:T(8,128)(2,1)S(1)}, bf16[2,384,128]{2,1,0:T(8,128)(2,1)S(1)}, u32[]{:S(2)}, u32[]{:S(2)}) collective-permute-start(bf16[2,384,128]{2,1,0:T(8,128)(2,1)S(1)} %pad_maximum_fusion.1.refs_4_), channel_id=1, source_target_pairs={{0,8},{4,20},{8,0},{12,28},{16,24},{20,4},{24,16},{28,12},{1,9},{5... | collective-permute-start | bytes 589832 | tf_op jit(solution)/shard_map/ppermute | solution.py:451
  9.8 1.5 %collective-permute-start.4 = (bf16[2,384,128]{2,1,0:T(8,128)(2,1)S(1)}, bf16[2,384,128]{2,1,0:T(8,128)(2,1)S(1)}, u32[]{:S(2)}, u32[]{:S(2)}) collective-permute-start(bf16[2,384,128]{2,1,0:T(8,128)(2,1)S(1)} %pad_maximum_fusion.1.refs_4_), channel_id=1, source_target_pairs={{0,16},{4,12},{8,24},{12,4},{16,0},{20,28},{24,8},{28,20},{1,17},{... | collective-permute-start | bytes 589832 | tf_op jit(solution)/shard_map/ppermute | solution.py:451
  11.3 0.0 collective-permute-start.5
  11.3 0.1 constant_dynamic-update-slice_fusion.5
  11.4 4.6 %collective-permute-done.2 = bf16[2,192,128]{2,1,0:T(8,128)(2,1)S(1)} collective-permute-done((bf16[2,192,128]{2,1,0:T(8,128)(2,1)S(1)}, bf16[2,192,128]{2,1,0:T(8,128)(2,1)S(1)}, u32[]{:S(2)}, u32[]{:S(2)}) %collective-permute-start.2) | collective-permute-done | bytes 98336 | tf_op jit(solution)/shard_map/ppermute | solution.py:515
  16.0 0.0 collective-permute-done.3
  16.0 0.0 collective-permute-done.1.refs_6_
  16.0 0.0 collective-permute-done.4.refs_8_
  16.0 0.0 collective-permute-done.5.refs_4_
  16.1 1.6 %collective-permute-start.6 = (bf16[2,384,128]{2,1,0:T(8,128)(2,1)S(1)}, bf16[2,384,128]{2,1,0:T(8,128)(2,1)S(1)}, u32[]{:S(2)}, u32[]{:S(2)}) collective-permute-start(bf16[2,384,128]{2,1,0:T(8,128)(2,1)S(1)} %constant_dynamic-update-slice_fusion.1.refs_5_), channel_id=1, source_target_pairs={{0,8},{4,20},{8,0},{12,28},{16,24},{20,4},{24,16},{28,12},{1,9},{5... | collective-permute-start | bytes 589832 | tf_op jit(solution)/shard_map/ppermute | solution.py:451
  17.6 0.1 constant_dynamic-update-slice_fusion.4
  17.7 0.1 constant_dynamic-update-slice_fusion.3
  17.8 0.2 copy.9.refs_3_
  18.7 0.1 collective-permute-start.8
  18.7 0.6 %shard_map.59 = (bf16[128,768]{1,0:T(8,128)(2,1)S(1)}, bf16[768,128]{1,0:T(8,128)(2,1)S(1)}, f32[1,128]{1,0:T(1,128)S(1)}, f32[1,128]{1,0:T(1,128)S(1)}, f32[128...) custom-call(s32[1]{0:T(128)} %bitcast.refs_0_, ...), custom_call_target="tpu_custom_call" | custom-call | flops 100000000 | bytes 1 | tf_op jit(solution)/shard_map/pallas_call | solution.py:488
  19.3 1.6 %collective-permute-start.9 = (bf16[2,384,128]{2,1,0:T(8,128)(2,1)S(1)}, bf16[2,384,128]{2,1,0:T(8,128)(2,1)S(1)}, u32[]{:S(2)}, u32[]{:S(2)}) collective-permute-start(bf16[2,384,128]{2,1,0:T(8,128)(2,1)S(1)} %constant_dynamic-update-slice_fusion.1.refs_5_), channel_id=1, source_target_pairs={{0,16},{4,12},{8,24},{12,4},{16,0},{20,28},{24,8},{28,20},{1,17},{... | collective-permute-start | bytes 589832 | tf_op jit(solution)/shard_map/ppermute | solution.py:451
  20.9 0.9 %collective-permute-done.6.refs_7_ = bf16[2,384,128]{2,1,0:T(8,128)(2,1)S(1)} collective-permute-done((bf16[2,384,128]{2,1,0:T(8,128)(2,1)S(1)}, bf16[2,384,128]{2,1,0:T(8,128)(2,1)S(1)}, u32[]{:S(2)}, u32[]{:S(2)}) %collective-permute-start.6) | collective-permute-done | bytes 196640 | tf_op jit(solution)/shard_map/ppermute | solution.py:451
  21.8 1.6 %collective-permute-start.7 = (bf16[2,768,128]{2,1,0:T(8,128)(2,1)S(1)}, bf16[2,768,128]{2,1,0:T(8,128)(2,1)S(1)}, u32[]{:S(2)}, u32[]{:S(2)}) collective-permute-start(bf16[2,768,128]{2,1,0:T(8,128)(2,1)S(1)} %pad_maximum_fusion), channel_id=1, source_target_pairs={{0,16},{4,12},{8,24},{12,4},{16,0},{20,28},{24,8},{28,20},{1,17},{... | collective-permute-start | bytes 1179656 | tf_op jit(solution)/shard_map/ppermute | solution.py:451
  23.4 0.0 collective-permute-start.10
  23.4 1.7 %collective-permute-done.9.refs_9_ = bf16[2,384,128]{2,1,0:T(8,128)(2,1)S(1)} collective-permute-done((bf16[2,384,128]{2,1,0:T(8,128)(2,1)S(1)}, bf16[2,384,128]{2,1,0:T(8,128)(2,1)S(1)}, u32[]{:S(2)}, u32[]{:S(2)}) %collective-permute-start.9) | collective-permute-done | bytes 196640 | tf_op jit(solution)/shard_map/ppermute | solution.py:451
  25.1 0.0 collective-permute-start.12
  25.1 0.5 %collective-permute-start.13 = (bf16[2,384,128]{2,1,0:T(8,128)(2,1)S(1)}, bf16[2,384,128]{2,1,0:T(8,128)(2,1)S(1)}, u32[]{:S(2)}, u32[]{:S(2)}) collective-permute-start(bf16[2,384,128]{2,1,0:T(8,128)(2,1)S(1)} %collective-permute-done.9.refs_9_), channel_id=1, source_target_pairs={{0,4},{4,0},{8,12},{12,8},{16,20},{20,16},{24,28},{28,24},{1,5},{5... | collective-permute-start | bytes 589832 | tf_op jit(solution)/shard_map/ppermute | solution.py:454
  25.6 0.0 collective-permute-done.8.refs_5_
  25.6 0.0 collective-permute-start.11
  25.6 0.0 collective-permute-done.10.refs_10_
  25.6 0.9 %collective-permute-done.12.refs_12_ = bf16[2,384,128]{2,1,0:T(8,128)(2,1)S(1)} collective-permute-done((bf16[2,384,128]{2,1,0:T(8,128)(2,1)S(1)}, bf16[2,384,128]{2,1,0:T(8,128)(2,1)S(1)}, u32[]{:S(2)}, u32[]{:S(2)}) %collective-permute-start.12) | collective-permute-done | bytes 196640 | tf_op jit(solution)/shard_map/ppermute | solution.py:454
  26.5 0.3 collective-permute-done.13.refs_13_
  26.8 0.3 collective-permute-done.11.refs_11_
  27.1 2.6 %shard_map.60 = (bf16[640,768]{1,0:T(8,128)(2,1)S(1)}, bf16[768,640]{1,0:T(8,128)(2,1)S(1)}, f32[1,768]{1,0:T(1,128)S(1)}, f32[1,768]{1,0:T(1,128)S(1)}, f32[128,640]{1,0:T(8,128)S(1)}, /*index=5*/f32[128,640]{1,0:T(8,128)S(1)}) custom-call(s32[1]{0:T(128)} %bitcast.refs_0_, f32[1]{0:T(128)} %bitcast.11.refs_1_, s32[1,1024]{1,0:T(1,128)S(1)} %bitcast.16, ...), custom_call_target="tpu_custom_call" | custom-call | flops 1 | bytes 1 | tf_op jit(solution)/shard_map/pallas_call | solution.py:488
  29.7 0.0 collective-permute-done.7.refs_4_
  29.7 0.3 collective-permute-start.14
  30.0 1.2 %shard_map.61 = (bf16[128,768]{1,0:T(8,128)(2,1)S(1)}, bf16[768,128]{1,0:T(8,128)(2,1)S(1)}, f32[1,896]{1,0:T(1,128)S(1)}, f32[1,896]{1,0:T(1,128)S(1)}, f32[128,128]{1,0:T(8,128)S(1)}, /*index=5*/f32[128,128]{1,0:T(8,128)S(1)}) custom-call(s32[1]{0:T(128)} %bitcast.refs_0_, f32[1]{0:T(128)} %bitcast.12.refs_1_, s32[1,1024]{1,0:T(1,128)S(1)} %bitcast.17, ...), custom_call_target="tpu_custom_call" | custom-call | flops 1 | bytes 1 | tf_op jit(solution)/shard_map/pallas_call | solution.py:488
  31.2 0.3 collective-permute-done.14.refs_4_
  31.5 3.1 %shard_map.62 = (f32[32,768]{1,0:T(8,128)}, f32[32,768]{1,0:T(8,128)}) custom-call(s32[1]{0:T(128)} %bitcast.refs_0_, f32[1]{0:T(128)} %bitcast.13.refs_1_, s32[1,1024]{1,0:T(1,128)S(1)} %bitcast.18, s32[1024,1]{1,0:T(8,128)S(1)} %copy.9.refs_3_, bf16[2,768,128]{2,1,0:T(8,128)(2,1)S(1)} %collective-permute-done.14.refs_4_, ...), custom_call_target="tpu_custom_call" | custom-call | flops 1 | bytes 1 | tf_op jit(solution)/shard_map/pallas_call | solution.py:488
  (5 shorter events, 0.1 us)
Async XLA Ops:
  1.5 6.8 %collective-permute-start = (bf16[2,192,128]{2,1,0:T(8,128)(2,1)S(1)}, bf16[2,192,128]{2,1,0:T(8,128)(2,1)S(1)}, u32[]{:S(2)}, u32[]{:S(2)}) collective-permute-start(bf16[2,192,128]{2,1,0:T(8,128)(2,1)S(1)} %pad_maximum_fusion.2), channel_id=1, source_target_pairs={{0,1},{1,0},{2,3},{3,2},{4,5},{5,4},{6,7},{7,6},{8,9},{9,8},{10,11... | collective-permute-start | bytes 294920 | tf_op jit(solution)/shard_map/ppermute | solution.py:515
  4.6 11.4 %collective-permute-start.3 = (bf16[2,192,128]{2,1,0:T(8,128)(2,1)S(1)}, bf16[2,192,128]{2,1,0:T(8,128)(2,1)S(1)}, u32[]{:S(2)}, u32[]{:S(2)}) collective-permute-start(bf16[2,192,128]{2,1,0:T(8,128)(2,1)S(1)} %pad_maximum_fusion.2), channel_id=1, source_target_pairs={{0,3},{1,2},{2,1},{3,0},{4,7},{5,6},{6,5},{7,4},{8,11},{9,10},{10,... | collective-permute-start | bytes 294920 | tf_op jit(solution)/shard_map/ppermute | solution.py:515
  7.0 8.9 %collective-permute-start.2 = (bf16[2,192,128]{2,1,0:T(8,128)(2,1)S(1)}, bf16[2,192,128]{2,1,0:T(8,128)(2,1)S(1)}, u32[]{:S(2)}, u32[]{:S(2)}) collective-permute-start(bf16[2,192,128]{2,1,0:T(8,128)(2,1)S(1)} %pad_maximum_fusion.2), channel_id=1, source_target_pairs={{0,2},{1,3},{2,0},{3,1},{4,6},{5,7},{6,4},{7,5},{8,10},{9,11},{10,... | collective-permute-start | bytes 294920 | tf_op jit(solution)/shard_map/ppermute | solution.py:515
  7.1 0.7 %copy-start.2 = (s32[1024]{0:T(1024)S(1)}, s32[1024]{0:T(1024)}, u32[]{:S(2)}) copy-start(s32[1024]{0:T(1024)} %param.6) | copy-start | bytes 12292
  7.2 1.1 %copy-start.1 = (bf16[128,192]{0,1:T(8,128)(2,1)S(1)}, bf16[128,192]{0,1:T(8,128)(2,1)}, u32[]{:S(2)}) copy-start(bf16[128,192]{0,1:T(8,128)(2,1)} %param.4) | copy-start | bytes 147460
  7.2 1.1 %copy-start = (bf16[128,192]{0,1:T(8,128)(2,1)S(1)}, bf16[128,192]{0,1:T(8,128)(2,1)}, u32[]{:S(2)}) copy-start(bf16[128,192]{0,1:T(8,128)(2,1)} %param.5) | copy-start | bytes 147460
  8.3 7.7 %collective-permute-start.1 = (bf16[2,384,128]{2,1,0:T(8,128)(2,1)S(1)}, bf16[2,384,128]{2,1,0:T(8,128)(2,1)S(1)}, u32[]{:S(2)}, u32[]{:S(2)}) collective-permute-start(bf16[2,384,128]{2,1,0:T(8,128)(2,1)S(1)} %pad_maximum_fusion.1.refs_4_), channel_id=1, source_target_pairs={{0,8},{4,20},{8,0},{12,28},{16,24},{20,4},{24,16},{28,12},{1,9},{5... | collective-permute-start | bytes 589832 | tf_op jit(solution)/shard_map/ppermute | solution.py:451
  9.8 6.2 %collective-permute-start.4 = (bf16[2,384,128]{2,1,0:T(8,128)(2,1)S(1)}, bf16[2,384,128]{2,1,0:T(8,128)(2,1)S(1)}, u32[]{:S(2)}, u32[]{:S(2)}) collective-permute-start(bf16[2,384,128]{2,1,0:T(8,128)(2,1)S(1)} %pad_maximum_fusion.1.refs_4_), channel_id=1, source_target_pairs={{0,16},{4,12},{8,24},{12,4},{16,0},{20,28},{24,8},{28,20},{1,17},{... | collective-permute-start | bytes 589832 | tf_op jit(solution)/shard_map/ppermute | solution.py:451
  11.3 4.7 %collective-permute-start.5 = (bf16[2,384,128]{2,1,0:T(8,128)(2,1)S(1)}, bf16[2,384,128]{2,1,0:T(8,128)(2,1)S(1)}, u32[]{:S(2)}, u32[]{:S(2)}) collective-permute-start(bf16[2,384,128]{2,1,0:T(8,128)(2,1)S(1)} %pad_maximum_fusion.1.refs_4_), channel_id=1, source_target_pairs={{0,4},{4,0},{8,12},{12,8},{16,20},{20,16},{24,28},{28,24},{1,5},{5... | collective-permute-start | bytes 589832 | tf_op jit(solution)/shard_map/ppermute | solution.py:454
  16.1 5.7 %collective-permute-start.6 = (bf16[2,384,128]{2,1,0:T(8,128)(2,1)S(1)}, bf16[2,384,128]{2,1,0:T(8,128)(2,1)S(1)}, u32[]{:S(2)}, u32[]{:S(2)}) collective-permute-start(bf16[2,384,128]{2,1,0:T(8,128)(2,1)S(1)} %constant_dynamic-update-slice_fusion.1.refs_5_), channel_id=1, source_target_pairs={{0,8},{4,20},{8,0},{12,28},{16,24},{20,4},{24,16},{28,12},{1,9},{5... | collective-permute-start | bytes 589832 | tf_op jit(solution)/shard_map/ppermute | solution.py:451
  18.7 6.9 %collective-permute-start.8 = (bf16[2,384,128]{2,1,0:T(8,128)(2,1)S(1)}, bf16[2,384,128]{2,1,0:T(8,128)(2,1)S(1)}, u32[]{:S(2)}, u32[]{:S(2)}) collective-permute-start(bf16[2,384,128]{2,1,0:T(8,128)(2,1)S(1)} %constant_dynamic-update-slice_fusion.1.refs_5_), channel_id=1, source_target_pairs={{0,4},{4,0},{8,12},{12,8},{16,20},{20,16},{24,28},{28,24},{1,5},{5... | collective-permute-start | bytes 589832 | tf_op jit(solution)/shard_map/ppermute | solution.py:454
  19.3 5.7 %collective-permute-start.9 = (bf16[2,384,128]{2,1,0:T(8,128)(2,1)S(1)}, bf16[2,384,128]{2,1,0:T(8,128)(2,1)S(1)}, u32[]{:S(2)}, u32[]{:S(2)}) collective-permute-start(bf16[2,384,128]{2,1,0:T(8,128)(2,1)S(1)} %constant_dynamic-update-slice_fusion.1.refs_5_), channel_id=1, source_target_pairs={{0,16},{4,12},{8,24},{12,4},{16,0},{20,28},{24,8},{28,20},{1,17},{... | collective-permute-start | bytes 589832 | tf_op jit(solution)/shard_map/ppermute | solution.py:451
  21.8 7.9 %collective-permute-start.7 = (bf16[2,768,128]{2,1,0:T(8,128)(2,1)S(1)}, bf16[2,768,128]{2,1,0:T(8,128)(2,1)S(1)}, u32[]{:S(2)}, u32[]{:S(2)}) collective-permute-start(bf16[2,768,128]{2,1,0:T(8,128)(2,1)S(1)} %pad_maximum_fusion), channel_id=1, source_target_pairs={{0,16},{4,12},{8,24},{12,4},{16,0},{20,28},{24,8},{28,20},{1,17},{... | collective-permute-start | bytes 1179656 | tf_op jit(solution)/shard_map/ppermute | solution.py:451
  23.4 2.2 %collective-permute-start.10 = (bf16[2,384,128]{2,1,0:T(8,128)(2,1)S(1)}, bf16[2,384,128]{2,1,0:T(8,128)(2,1)S(1)}, u32[]{:S(2)}, u32[]{:S(2)}) collective-permute-start(bf16[2,384,128]{2,1,0:T(8,128)(2,1)S(1)} %collective-permute-done.1.refs_6_), channel_id=1, source_target_pairs={{0,4},{4,0},{8,12},{12,8},{16,20},{20,16},{24,28},{28,24},{1,5},{5... | collective-permute-start | bytes 589832 | tf_op jit(solution)/shard_map/ppermute | solution.py:454
  25.1 1.4 %collective-permute-start.12 = (bf16[2,384,128]{2,1,0:T(8,128)(2,1)S(1)}, bf16[2,384,128]{2,1,0:T(8,128)(2,1)S(1)}, u32[]{:S(2)}, u32[]{:S(2)}) collective-permute-start(bf16[2,384,128]{2,1,0:T(8,128)(2,1)S(1)} %collective-permute-done.4.refs_8_), channel_id=1, source_target_pairs={{0,4},{4,0},{8,12},{12,8},{16,20},{20,16},{24,28},{28,24},{1,5},{5... | collective-permute-start | bytes 589832 | tf_op jit(solution)/shard_map/ppermute | solution.py:454
  25.1 1.7 %collective-permute-start.13 = (bf16[2,384,128]{2,1,0:T(8,128)(2,1)S(1)}, bf16[2,384,128]{2,1,0:T(8,128)(2,1)S(1)}, u32[]{:S(2)}, u32[]{:S(2)}) collective-permute-start(bf16[2,384,128]{2,1,0:T(8,128)(2,1)S(1)} %collective-permute-done.9.refs_9_), channel_id=1, source_target_pairs={{0,4},{4,0},{8,12},{12,8},{16,20},{20,16},{24,28},{28,24},{1,5},{5... | collective-permute-start | bytes 589832 | tf_op jit(solution)/shard_map/ppermute | solution.py:454
  25.6 1.5 %collective-permute-start.11 = (bf16[2,384,128]{2,1,0:T(8,128)(2,1)S(1)}, bf16[2,384,128]{2,1,0:T(8,128)(2,1)S(1)}, u32[]{:S(2)}, u32[]{:S(2)}) collective-permute-start(bf16[2,384,128]{2,1,0:T(8,128)(2,1)S(1)} %collective-permute-done.6.refs_7_), channel_id=1, source_target_pairs={{0,4},{4,0},{8,12},{12,8},{16,20},{20,16},{24,28},{28,24},{1,5},{5... | collective-permute-start | bytes 589832 | tf_op jit(solution)/shard_map/ppermute | solution.py:454
  29.7 1.8 %collective-permute-start.14 = (bf16[2,768,128]{2,1,0:T(8,128)(2,1)S(1)}, bf16[2,768,128]{2,1,0:T(8,128)(2,1)S(1)}, u32[]{:S(2)}, u32[]{:S(2)}) collective-permute-start(bf16[2,768,128]{2,1,0:T(8,128)(2,1)S(1)} %collective-permute-done.7.refs_4_), channel_id=1, source_target_pairs={{0,4},{4,0},{8,12},{12,8},{16,20},{20,16},{24,28},{28,24},{1,5},{5... | collective-permute-start | bytes 1179656 | tf_op jit(solution)/shard_map/ppermute | solution.py:454

commit v8 on v7

--- a/solution.py
+++ b/solution.py
@@ -417,23 +417,23 @@
     clip_grad = (
         scale * clip_acc
         - 0.5 * scale * cap_unit.astype(jnp.float32)
-        - 0.5 * scale * projected / pool_length
+        - (0.5 * scale / pool_length) * projected
     )
     cap_grad = scale * cap_acc - 0.5 * scale * clip_unit.astype(jnp.float32) - 0.5 * scale * pool_unit
 
-    def finish(unit, length, grad, out_ref):
-        result = (grad - unit * jnp.sum(unit * grad, axis=1, keepdims=True)) / length
-        for index in range(mp_count):
-
-            @pl.when(mp_index == index)
-            def _():
+    def finish(unit, length, grad):
+        return (grad - unit * jnp.sum(unit * grad, axis=1, keepdims=True)) * (1.0 / length)
+
+    results = [finish(clip_float, clip_length, clip_grad), finish(cap_float, cap_length, cap_grad)]
+    for index in range(mp_count):
+
+        @pl.when(mp_index == index)
+        def _():
+            for result, out_ref in zip(results, (d_clips_ref, d_caps_ref)):
                 out_ref[...] = jnp.concatenate(
                     [result[:, (q ^ index) * chunk : ((q ^ index) + 1) * chunk] for q in range(mp_count)],
                     axis=1,
                 )
-
-    finish(clip_float, clip_length, clip_grad, d_clips_ref)
-    finish(cap_float, cap_length, cap_grad, d_caps_ref)
 
 
 def resident_body(clips, captions, video_id, logit_scale):
@@ -518,7 +518,7 @@
     lead_first = along(0, lead)
     lead_second = along(1, lead)
     lead_other = across(lead)
-    arrived[-1] = after(arrived[-1], (lead_first, lead_second, lead_other))
+    arrived[-1] = after(arrived[-1], (lead_first, lead_second, lead_other, common[3]))
     rest = jnp.concatenate(arrived[early - 1 :], axis=1)
     rest_first = along(0, rest)
     rest_other = across(rest)

time: 34.9 us -> 34.6 us (level)
  transfers between devices with their start and end apart: 15 -> 15, of which waited for: 7 -> 8; matrix products, arithmetic and copies ran while one was open for 3% -> 3% of each run, Pallas kernels for 13% -> 13%
where the time goes in v8:
time: 34.6 us; the launch traced here: 34.4 us
  starting transfers between devices  14.3 us (41%)
  waiting for transfers between devices  8.87 us (26%)
  Pallas kernels  7.45 us (22%)
  local copies, waits for them, and re-layouts  1.56 us (5%)
  between operations  1.39 us (4%)
  other arithmetic  0.88 us (3%)
    ppermute x5, starting transfers between devices, along(): return lax.ppermute(block, 'dp', route)  7.78 us
    pallas_call x4, Pallas kernels, stage(): pl.pallas_call(functools.partial(stage_kernel, piece_count=len(pieces), p...  7.45 us
    ppermute x3, starting transfers between devices, resident_body(): lax.ppermute(chunk, 'mp', [(i, i ^ k) for i in range(mp_count)])  5.68 us
    ppermute x3, waiting for transfers between devices, resident_body(): lax.ppermute(chunk, 'mp', [(i, i ^ k) for i in range(mp_count)])  4.4 us
    ppermute x5, waiting for transfers between devices, along(): return lax.ppermute(block, 'dp', route)  2.63 us
    ppermute x7, waiting for transfers between devices, across(): return lax.ppermute(block, 'dp', [(i, i ^ 1) for i in range(dp_count)])  1.83 us
    unnamed x14, local copies, waits for them, and re-layouts  1.25 us
    another operation x1, other arithmetic, resident_body(): chunk = jnp.stack([clips.T, captions.T])  0.84 us
  transfers between devices with their start and end apart: 15, of which 8 were waited for; matrix products, arithmetic and copies ran while one was open for 3% of the time, Pallas kernels for 13%

profile of v8, /device:TPU:0, one launch (start us, length us, event | category | flops | bytes accessed | tf_op | source)
XLA Modules:
  0.0 34.4 jit_solution(6882790990429600847)
XLA Ops:
  0.6 0.8 %pad_maximum_fusion.2 = bf16[2,192,128]{2,1,0:T(8,128)(2,1)S(1)} fusion(bf16[1,192,128]{2,1,0:T(8,128)(2,1)} %bitcast.19, bf16[1,192,128]{2,1,0:T(8,128)(2,1)} %bitcast.21), kind=kLoop, calls=%fused_computation.2 | loop fusion | flops 49152 | bytes 196608 | tf_op jit(solution)/shard_map/stack | solution.py:513
  1.5 3.1 %collective-permute-start = (bf16[2,192,128]{2,1,0:T(8,128)(2,1)S(1)}, bf16[2,192,128]{2,1,0:T(8,128)(2,1)S(1)}, u32[]{:S(2)}, u32[]{:S(2)}) collective-permute-start(bf16[2,192,128]{2,1,0:T(8,128)(2,1)S(1)} %pad_maximum_fusion.2), channel_id=1, source_target_pairs={{0,1},{1,0},{2,3},{3,2},{4,5},{5,4},{6,7},{7,6},{8,9},{9,8},{10,11... | collective-permute-start | bytes 294920 | tf_op jit(solution)/shard_map/ppermute | solution.py:515
  4.6 2.5 %collective-permute-start.3 = (bf16[2,192,128]{2,1,0:T(8,128)(2,1)S(1)}, bf16[2,192,128]{2,1,0:T(8,128)(2,1)S(1)}, u32[]{:S(2)}, u32[]{:S(2)}) collective-permute-start(bf16[2,192,128]{2,1,0:T(8,128)(2,1)S(1)} %pad_maximum_fusion.2), channel_id=1, source_target_pairs={{0,3},{1,2},{2,1},{3,0},{4,7},{5,6},{6,5},{7,4},{8,11},{9,10},{10,... | collective-permute-start | bytes 294920 | tf_op jit(solution)/shard_map/ppermute | solution.py:515
  7.0 0.1 collective-permute-start.2
  7.1 0.0 copy-start.2
  7.2 0.0 copy-start.1
  7.2 0.0 copy-start
  7.2 0.7 %copy-done.2 = s32[1024]{0:T(1024)S(1)} copy-done((s32[1024]{0:T(1024)S(1)}, s32[1024]{0:T(1024)}, u32[]{:S(2)}) %copy-start.2) | copy-done | bytes 4120
  7.8 0.1 constant_dynamic-update-slice_fusion
  7.9 0.1 constant_dynamic-update-slice_fusion.9
  8.0 0.1 constant_dynamic-update-slice_fusion.8
  8.1 0.1 constant_dynamic-update-slice_fusion.7
  8.2 0.1 constant_dynamic-update-slice_fusion.6
  8.2 0.1 constant_dynamic-update-slice_fusion.5
  8.3 0.1 constant_dynamic-update-slice_fusion.4
  8.4 0.0 collective-permute-done
  8.4 0.0 copy-done.1
  8.4 0.0 copy-done
  8.4 1.6 %collective-permute-start.1 = (bf16[2,384,128]{2,1,0:T(8,128)(2,1)S(1)}, bf16[2,384,128]{2,1,0:T(8,128)(2,1)S(1)}, u32[]{:S(2)}, u32[]{:S(2)}) collective-permute-start(bf16[2,384,128]{2,1,0:T(8,128)(2,1)S(1)} %pad_maximum_fusion.1.refs_4_), channel_id=1, source_target_pairs={{0,8},{4,20},{8,0},{12,28},{16,24},{20,4},{24,16},{28,12},{1,9},{5... | collective-permute-start | bytes 589832 | tf_op jit(solution)/shard_map/ppermute | solution.py:451
  10.0 1.5 %collective-permute-start.4 = (bf16[2,384,128]{2,1,0:T(8,128)(2,1)S(1)}, bf16[2,384,128]{2,1,0:T(8,128)(2,1)S(1)}, u32[]{:S(2)}, u32[]{:S(2)}) collective-permute-start(bf16[2,384,128]{2,1,0:T(8,128)(2,1)S(1)} %pad_maximum_fusion.1.refs_4_), channel_id=1, source_target_pairs={{0,16},{4,12},{8,24},{12,4},{16,0},{20,28},{24,8},{28,20},{1,17},{... | collective-permute-start | bytes 589832 | tf_op jit(solution)/shard_map/ppermute | solution.py:451
  11.5 0.0 collective-permute-start.5
  11.5 0.1 constant_dynamic-update-slice_fusion.3
  11.6 4.4 %collective-permute-done.2 = bf16[2,192,128]{2,1,0:T(8,128)(2,1)S(1)} collective-permute-done((bf16[2,192,128]{2,1,0:T(8,128)(2,1)S(1)}, bf16[2,192,128]{2,1,0:T(8,128)(2,1)S(1)}, u32[]{:S(2)}, u32[]{:S(2)}) %collective-permute-start.2) | collective-permute-done | bytes 98336 | tf_op jit(solution)/shard_map/ppermute | solution.py:515
  16.0 0.0 collective-permute-done.3
  16.0 0.0 collective-permute-done.1.refs_6_
  16.0 0.0 collective-permute-done.4.refs_8_
  16.0 0.0 collective-permute-done.5.refs_4_
  16.1 1.6 %collective-permute-start.6 = (bf16[2,384,128]{2,1,0:T(8,128)(2,1)S(1)}, bf16[2,384,128]{2,1,0:T(8,128)(2,1)S(1)}, u32[]{:S(2)}, u32[]{:S(2)}) collective-permute-start(bf16[2,384,128]{2,1,0:T(8,128)(2,1)S(1)} %constant_dynamic-update-slice_fusion.1.refs_5_), channel_id=1, source_target_pairs={{0,8},{4,20},{8,0},{12,28},{16,24},{20,4},{24,16},{28,12},{1,9},{5... | collective-permute-start | bytes 589832 | tf_op jit(solution)/shard_map/ppermute | solution.py:451
  17.6 0.2 copy.9.refs_3_
  18.5 0.1 collective-permute-start.8
  18.6 0.6 %shard_map.59 = (bf16[128,768]{1,0:T(8,128)(2,1)S(1)}, bf16[768,128]{1,0:T(8,128)(2,1)S(1)}, f32[1,128]{1,0:T(1,128)S(1)}, f32[1,128]{1,0:T(1,128)S(1)}, f32[128...) custom-call(s32[1]{0:T(128)} %bitcast.refs_0_, ...), custom_call_target="tpu_custom_call" | custom-call | flops 100000000 | bytes 1 | tf_op jit(solution)/shard_map/pallas_call | solution.py:488
  19.2 1.6 %collective-permute-start.9 = (bf16[2,384,128]{2,1,0:T(8,128)(2,1)S(1)}, bf16[2,384,128]{2,1,0:T(8,128)(2,1)S(1)}, u32[]{:S(2)}, u32[]{:S(2)}) collective-permute-start(bf16[2,384,128]{2,1,0:T(8,128)(2,1)S(1)} %constant_dynamic-update-slice_fusion.1.refs_5_), channel_id=1, source_target_pairs={{0,16},{4,12},{8,24},{12,4},{16,0},{20,28},{24,8},{28,20},{1,17},{... | collective-permute-start | bytes 589832 | tf_op jit(solution)/shard_map/ppermute | solution.py:451
  20.8 1.0 %collective-permute-done.6.refs_7_ = bf16[2,384,128]{2,1,0:T(8,128)(2,1)S(1)} collective-permute-done((bf16[2,384,128]{2,1,0:T(8,128)(2,1)S(1)}, bf16[2,384,128]{2,1,0:T(8,128)(2,1)S(1)}, u32[]{:S(2)}, u32[]{:S(2)}) %collective-permute-start.6) | collective-permute-done | bytes 196640 | tf_op jit(solution)/shard_map/ppermute | solution.py:451
  21.8 1.6 %collective-permute-start.7 = (bf16[2,768,128]{2,1,0:T(8,128)(2,1)S(1)}, bf16[2,768,128]{2,1,0:T(8,128)(2,1)S(1)}, u32[]{:S(2)}, u32[]{:S(2)}) collective-permute-start(bf16[2,768,128]{2,1,0:T(8,128)(2,1)S(1)} %pad_maximum_fusion), channel_id=1, source_target_pairs={{0,16},{4,12},{8,24},{12,4},{16,0},{20,28},{24,8},{28,20},{1,17},{... | collective-permute-start | bytes 1179656 | tf_op jit(solution)/shard_map/ppermute | solution.py:451
  23.4 0.0 collective-permute-start.10
  23.4 1.5 %collective-permute-done.9.refs_9_ = bf16[2,384,128]{2,1,0:T(8,128)(2,1)S(1)} collective-permute-done((bf16[2,384,128]{2,1,0:T(8,128)(2,1)S(1)}, bf16[2,384,128]{2,1,0:T(8,128)(2,1)S(1)}, u32[]{:S(2)}, u32[]{:S(2)}) %collective-permute-start.9) | collective-permute-done | bytes 196640 | tf_op jit(solution)/shard_map/ppermute | solution.py:451
  24.9 0.0 collective-permute-start.12
  24.9 0.5 %collective-permute-start.13 = (bf16[2,384,128]{2,1,0:T(8,128)(2,1)S(1)}, bf16[2,384,128]{2,1,0:T(8,128)(2,1)S(1)}, u32[]{:S(2)}, u32[]{:S(2)}) collective-permute-start(bf16[2,384,128]{2,1,0:T(8,128)(2,1)S(1)} %collective-permute-done.9.refs_9_), channel_id=1, source_target_pairs={{0,4},{4,0},{8,12},{12,8},{16,20},{20,16},{24,28},{28,24},{1,5},{5... | collective-permute-start | bytes 589832 | tf_op jit(solution)/shard_map/ppermute | solution.py:454
  25.4 0.0 collective-permute-done.8.refs_5_
  25.4 0.0 collective-permute-start.11
  25.4 0.0 collective-permute-done.10.refs_10_
  25.4 0.9 %collective-permute-done.12.refs_12_ = bf16[2,384,128]{2,1,0:T(8,128)(2,1)S(1)} collective-permute-done((bf16[2,384,128]{2,1,0:T(8,128)(2,1)S(1)}, bf16[2,384,128]{2,1,0:T(8,128)(2,1)S(1)}, u32[]{:S(2)}, u32[]{:S(2)}) %collective-permute-start.12) | collective-permute-done | bytes 196640 | tf_op jit(solution)/shard_map/ppermute | solution.py:454
  26.3 0.3 collective-permute-done.13.refs_13_
  26.6 0.3 collective-permute-done.11.refs_11_
  26.9 2.6 %shard_map.60 = (bf16[640,768]{1,0:T(8,128)(2,1)S(1)}, bf16[768,640]{1,0:T(8,128)(2,1)S(1)}, f32[1,768]{1,0:T(1,128)S(1)}, f32[1,768]{1,0:T(1,128)S(1)}, f32[128,640]{1,0:T(8,128)S(1)}, /*index=5*/f32[128,640]{1,0:T(8,128)S(1)}) custom-call(s32[1]{0:T(128)} %bitcast.refs_0_, f32[1]{0:T(128)} %bitcast.11.refs_1_, s32[1,1024]{1,0:T(1,128)S(1)} %bitcast.16, ...), custom_call_target="tpu_custom_call" | custom-call | flops 1 | bytes 1 | tf_op jit(solution)/shard_map/pallas_call | solution.py:488
  29.6 0.1 collective-permute-done.7.refs_4_
  29.7 0.2 collective-permute-start.14
  29.9 1.2 %shard_map.61 = (bf16[128,768]{1,0:T(8,128)(2,1)S(1)}, bf16[768,128]{1,0:T(8,128)(2,1)S(1)}, f32[1,896]{1,0:T(1,128)S(1)}, f32[1,896]{1,0:T(1,128)S(1)}, f32[128,128]{1,0:T(8,128)S(1)}, /*index=5*/f32[128,128]{1,0:T(8,128)S(1)}) custom-call(s32[1]{0:T(128)} %bitcast.refs_0_, f32[1]{0:T(128)} %bitcast.12.refs_1_, s32[1,1024]{1,0:T(1,128)S(1)} %bitcast.17, ...), custom_call_target="tpu_custom_call" | custom-call | flops 1 | bytes 1 | tf_op jit(solution)/shard_map/pallas_call | solution.py:488
  31.0 0.3 %collective-permute-done.14.refs_4_ = bf16[2,768,128]{2,1,0:T(8,128)(2,1)S(1)} collective-permute-done((bf16[2,768,128]{2,1,0:T(8,128)(2,1)S(1)}, bf16[2,768,128]{2,1,0:T(8,128)(2,1)S(1)}, u32[]{:S(2)}, u32[]{:S(2)}) %collective-permute-start.14) | collective-permute-done | bytes 393248 | tf_op jit(solution)/shard_map/ppermute | solution.py:454
  31.4 3.0 %shard_map.62 = (f32[32,768]{1,0:T(8,128)}, f32[32,768]{1,0:T(8,128)}) custom-call(s32[1]{0:T(128)} %bitcast.refs_0_, f32[1]{0:T(128)} %bitcast.13.refs_1_, s32[1,1024]{1,0:T(1,128)S(1)} %bitcast.18, s32[1024,1]{1,0:T(8,128)S(1)} %copy.9.refs_3_, bf16[2,768,128]{2,1,0:T(8,128)(2,1)S(1)} %collective-permute-done.14.refs_4_, ...), custom_call_target="tpu_custom_call" | custom-call | flops 1 | bytes 1 | tf_op jit(solution)/shard_map/pallas_call | solution.py:488
  (5 shorter events, 0.1 us)
Async XLA Ops:
  1.5 6.9 %collective-permute-start = (bf16[2,192,128]{2,1,0:T(8,128)(2,1)S(1)}, bf16[2,192,128]{2,1,0:T(8,128)(2,1)S(1)}, u32[]{:S(2)}, u32[]{:S(2)}) collective-permute-start(bf16[2,192,128]{2,1,0:T(8,128)(2,1)S(1)} %pad_maximum_fusion.2), channel_id=1, source_target_pairs={{0,1},{1,0},{2,3},{3,2},{4,5},{5,4},{6,7},{7,6},{8,9},{9,8},{10,11... | collective-permute-start | bytes 294920 | tf_op jit(solution)/shard_map/ppermute | solution.py:515
  4.6 11.4 %collective-permute-start.3 = (bf16[2,192,128]{2,1,0:T(8,128)(2,1)S(1)}, bf16[2,192,128]{2,1,0:T(8,128)(2,1)S(1)}, u32[]{:S(2)}, u32[]{:S(2)}) collective-permute-start(bf16[2,192,128]{2,1,0:T(8,128)(2,1)S(1)} %pad_maximum_fusion.2), channel_id=1, source_target_pairs={{0,3},{1,2},{2,1},{3,0},{4,7},{5,6},{6,5},{7,4},{8,11},{9,10},{10,... | collective-permute-start | bytes 294920 | tf_op jit(solution)/shard_map/ppermute | solution.py:515
  7.0 8.9 %collective-permute-start.2 = (bf16[2,192,128]{2,1,0:T(8,128)(2,1)S(1)}, bf16[2,192,128]{2,1,0:T(8,128)(2,1)S(1)}, u32[]{:S(2)}, u32[]{:S(2)}) collective-permute-start(bf16[2,192,128]{2,1,0:T(8,128)(2,1)S(1)} %pad_maximum_fusion.2), channel_id=1, source_target_pairs={{0,2},{1,3},{2,0},{3,1},{4,6},{5,7},{6,4},{7,5},{8,10},{9,11},{10,... | collective-permute-start | bytes 294920 | tf_op jit(solution)/shard_map/ppermute | solution.py:515
  7.1 0.7 %copy-start.2 = (s32[1024]{0:T(1024)S(1)}, s32[1024]{0:T(1024)}, u32[]{:S(2)}) copy-start(s32[1024]{0:T(1024)} %param.6) | copy-start | bytes 12292
  7.2 1.2 %copy-start.1 = (bf16[128,192]{0,1:T(8,128)(2,1)S(1)}, bf16[128,192]{0,1:T(8,128)(2,1)}, u32[]{:S(2)}) copy-start(bf16[128,192]{0,1:T(8,128)(2,1)} %param.4) | copy-start | bytes 147460
  7.2 1.2 %copy-start = (bf16[128,192]{0,1:T(8,128)(2,1)S(1)}, bf16[128,192]{0,1:T(8,128)(2,1)}, u32[]{:S(2)}) copy-start(bf16[128,192]{0,1:T(8,128)(2,1)} %param.5) | copy-start | bytes 147460
  8.4 7.6 %collective-permute-start.1 = (bf16[2,384,128]{2,1,0:T(8,128)(2,1)S(1)}, bf16[2,384,128]{2,1,0:T(8,128)(2,1)S(1)}, u32[]{:S(2)}, u32[]{:S(2)}) collective-permute-start(bf16[2,384,128]{2,1,0:T(8,128)(2,1)S(1)} %pad_maximum_fusion.1.refs_4_), channel_id=1, source_target_pairs={{0,8},{4,20},{8,0},{12,28},{16,24},{20,4},{24,16},{28,12},{1,9},{5... | collective-permute-start | bytes 589832 | tf_op jit(solution)/shard_map/ppermute | solution.py:451
  10.0 6.0 %collective-permute-start.4 = (bf16[2,384,128]{2,1,0:T(8,128)(2,1)S(1)}, bf16[2,384,128]{2,1,0:T(8,128)(2,1)S(1)}, u32[]{:S(2)}, u32[]{:S(2)}) collective-permute-start(bf16[2,384,128]{2,1,0:T(8,128)(2,1)S(1)} %pad_maximum_fusion.1.refs_4_), channel_id=1, source_target_pairs={{0,16},{4,12},{8,24},{12,4},{16,0},{20,28},{24,8},{28,20},{1,17},{... | collective-permute-start | bytes 589832 | tf_op jit(solution)/shard_map/ppermute | solution.py:451
  11.5 4.5 %collective-permute-start.5 = (bf16[2,384,128]{2,1,0:T(8,128)(2,1)S(1)}, bf16[2,384,128]{2,1,0:T(8,128)(2,1)S(1)}, u32[]{:S(2)}, u32[]{:S(2)}) collective-permute-start(bf16[2,384,128]{2,1,0:T(8,128)(2,1)S(1)} %pad_maximum_fusion.1.refs_4_), channel_id=1, source_target_pairs={{0,4},{4,0},{8,12},{12,8},{16,20},{20,16},{24,28},{28,24},{1,5},{5... | collective-permute-start | bytes 589832 | tf_op jit(solution)/shard_map/ppermute | solution.py:454
  16.1 5.7 %collective-permute-start.6 = (bf16[2,384,128]{2,1,0:T(8,128)(2,1)S(1)}, bf16[2,384,128]{2,1,0:T(8,128)(2,1)S(1)}, u32[]{:S(2)}, u32[]{:S(2)}) collective-permute-start(bf16[2,384,128]{2,1,0:T(8,128)(2,1)S(1)} %constant_dynamic-update-slice_fusion.1.refs_5_), channel_id=1, source_target_pairs={{0,8},{4,20},{8,0},{12,28},{16,24},{20,4},{24,16},{28,12},{1,9},{5... | collective-permute-start | bytes 589832 | tf_op jit(solution)/shard_map/ppermute | solution.py:451
  18.5 6.9 %collective-permute-start.8 = (bf16[2,384,128]{2,1,0:T(8,128)(2,1)S(1)}, bf16[2,384,128]{2,1,0:T(8,128)(2,1)S(1)}, u32[]{:S(2)}, u32[]{:S(2)}) collective-permute-start(bf16[2,384,128]{2,1,0:T(8,128)(2,1)S(1)} %constant_dynamic-update-slice_fusion.1.refs_5_), channel_id=1, source_target_pairs={{0,4},{4,0},{8,12},{12,8},{16,20},{20,16},{24,28},{28,24},{1,5},{5... | collective-permute-start | bytes 589832 | tf_op jit(solution)/shard_map/ppermute | solution.py:454
  19.2 5.7 %collective-permute-start.9 = (bf16[2,384,128]{2,1,0:T(8,128)(2,1)S(1)}, bf16[2,384,128]{2,1,0:T(8,128)(2,1)S(1)}, u32[]{:S(2)}, u32[]{:S(2)}) collective-permute-start(bf16[2,384,128]{2,1,0:T(8,128)(2,1)S(1)} %constant_dynamic-update-slice_fusion.1.refs_5_), channel_id=1, source_target_pairs={{0,16},{4,12},{8,24},{12,4},{16,0},{20,28},{24,8},{28,20},{1,17},{... | collective-permute-start | bytes 589832 | tf_op jit(solution)/shard_map/ppermute | solution.py:451
  21.8 7.8 %collective-permute-start.7 = (bf16[2,768,128]{2,1,0:T(8,128)(2,1)S(1)}, bf16[2,768,128]{2,1,0:T(8,128)(2,1)S(1)}, u32[]{:S(2)}, u32[]{:S(2)}) collective-permute-start(bf16[2,768,128]{2,1,0:T(8,128)(2,1)S(1)} %pad_maximum_fusion), channel_id=1, source_target_pairs={{0,16},{4,12},{8,24},{12,4},{16,0},{20,28},{24,8},{28,20},{1,17},{... | collective-permute-start | bytes 1179656 | tf_op jit(solution)/shard_map/ppermute | solution.py:451
  23.4 2.0 %collective-permute-start.10 = (bf16[2,384,128]{2,1,0:T(8,128)(2,1)S(1)}, bf16[2,384,128]{2,1,0:T(8,128)(2,1)S(1)}, u32[]{:S(2)}, u32[]{:S(2)}) collective-permute-start(bf16[2,384,128]{2,1,0:T(8,128)(2,1)S(1)} %collective-permute-done.1.refs_6_), channel_id=1, source_target_pairs={{0,4},{4,0},{8,12},{12,8},{16,20},{20,16},{24,28},{28,24},{1,5},{5... | collective-permute-start | bytes 589832 | tf_op jit(solution)/shard_map/ppermute | solution.py:454
  24.9 1.4 %collective-permute-start.12 = (bf16[2,384,128]{2,1,0:T(8,128)(2,1)S(1)}, bf16[2,384,128]{2,1,0:T(8,128)(2,1)S(1)}, u32[]{:S(2)}, u32[]{:S(2)}) collective-permute-start(bf16[2,384,128]{2,1,0:T(8,128)(2,1)S(1)} %collective-permute-done.4.refs_8_), channel_id=1, source_target_pairs={{0,4},{4,0},{8,12},{12,8},{16,20},{20,16},{24,28},{28,24},{1,5},{5... | collective-permute-start | bytes 589832 | tf_op jit(solution)/shard_map/ppermute | solution.py:454
  24.9 1.7 %collective-permute-start.13 = (bf16[2,384,128]{2,1,0:T(8,128)(2,1)S(1)}, bf16[2,384,128]{2,1,0:T(8,128)(2,1)S(1)}, u32[]{:S(2)}, u32[]{:S(2)}) collective-permute-start(bf16[2,384,128]{2,1,0:T(8,128)(2,1)S(1)} %collective-permute-done.9.refs_9_), channel_id=1, source_target_pairs={{0,4},{4,0},{8,12},{12,8},{16,20},{20,16},{24,28},{28,24},{1,5},{5... | collective-permute-start | bytes 589832 | tf_op jit(solution)/shard_map/ppermute | solution.py:454
  25.4 1.5 %collective-permute-start.11 = (bf16[2,384,128]{2,1,0:T(8,128)(2,1)S(1)}, bf16[2,384,128]{2,1,0:T(8,128)(2,1)S(1)}, u32[]{:S(2)}, u32[]{:S(2)}) collective-permute-start(bf16[2,384,128]{2,1,0:T(8,128)(2,1)S(1)} %collective-permute-done.6.refs_7_), channel_id=1, source_target_pairs={{0,4},{4,0},{8,12},{12,8},{16,20},{20,16},{24,28},{28,24},{1,5},{5... | collective-permute-start | bytes 589832 | tf_op jit(solution)/shard_map/ppermute | solution.py:454
  29.7 1.7 %collective-permute-start.14 = (bf16[2,768,128]{2,1,0:T(8,128)(2,1)S(1)}, bf16[2,768,128]{2,1,0:T(8,128)(2,1)S(1)}, u32[]{:S(2)}, u32[]{:S(2)}) collective-permute-start(bf16[2,768,128]{2,1,0:T(8,128)(2,1)S(1)} %collective-permute-done.7.refs_4_), channel_id=1, source_target_pairs={{0,4},{4,0},{8,12},{12,8},{16,20},{20,16},{24,28},{28,24},{1,5},{5... | collective-permute-start | bytes 1179656 | tf_op jit(solution)/shard_map/ppermute | solution.py:454

commit v9 on v8

--- a/solution.py
+++ b/solution.py
@@ -531,7 +531,7 @@
         (lead_other, rest_other),
         (lead_first, rest_first),
         (lead_second, rest_second),
-        (across(after(lead_first, lead_second)), across(rest_first)),
+        (across(lead_first), across(rest_first)),
         (across(after(lead_second, rest_second)), across(rest_second)),
     ]
     clips_b, caps_b, row_b, col_b, *strips_b = stage(

time: 34.6 us -> 34.6 us (level)
  no operation moved by 1% of the time
where the time goes in v9:
time: 34.6 us; the launch traced here: 34.4 us
  starting transfers between devices  14.3 us (41%)
  waiting for transfers between devices  8.87 us (26%)
  Pallas kernels  7.45 us (22%)
  local copies, waits for them, and re-layouts  1.56 us (5%)
  between operations  1.39 us (4%)
  other arithmetic  0.88 us (3%)
    ppermute x5, starting transfers between devices, along(): return lax.ppermute(block, 'dp', route)  7.78 us
    pallas_call x4, Pallas kernels, stage(): pl.pallas_call(functools.partial(stage_kernel, piece_count=len(pieces), p...  7.45 us
    ppermute x3, starting transfers between devices, resident_body(): lax.ppermute(chunk, 'mp', [(i, i ^ k) for i in range(mp_count)])  5.68 us
    ppermute x3, waiting for transfers between devices, resident_body(): lax.ppermute(chunk, 'mp', [(i, i ^ k) for i in range(mp_count)])  4.4 us
    ppermute x5, waiting for transfers between devices, along(): return lax.ppermute(block, 'dp', route)  2.63 us
    ppermute x7, waiting for transfers between devices, across(): return lax.ppermute(block, 'dp', [(i, i ^ 1) for i in range(dp_count)])  1.83 us
    unnamed x14, local copies, waits for them, and re-layouts  1.25 us
    another operation x1, other arithmetic, resident_body(): chunk = jnp.stack([clips.T, captions.T])  0.84 us
  transfers between devices with their start and end apart: 15, of which 8 were waited for; matrix products, arithmetic and copies ran while one was open for 3% of the time, Pallas kernels for 13%

profile of v9, /device:TPU:0, one launch (start us, length us, event | category | flops | bytes accessed | tf_op | source)
XLA Modules:
  0.0 34.4 jit_solution(6882790990429600847)
XLA Ops:
  0.6 0.8 %pad_maximum_fusion.2 = bf16[2,192,128]{2,1,0:T(8,128)(2,1)S(1)} fusion(bf16[1,192,128]{2,1,0:T(8,128)(2,1)} %bitcast.19, bf16[1,192,128]{2,1,0:T(8,128)(2,1)} %bitcast.21), kind=kLoop, calls=%fused_computation.2 | loop fusion | flops 49152 | bytes 196608 | tf_op jit(solution)/shard_map/stack | solution.py:513
  1.5 3.1 %collective-permute-start = (bf16[2,192,128]{2,1,0:T(8,128)(2,1)S(1)}, bf16[2,192,128]{2,1,0:T(8,128)(2,1)S(1)}, u32[]{:S(2)}, u32[]{:S(2)}) collective-permute-start(bf16[2,192,128]{2,1,0:T(8,128)(2,1)S(1)} %pad_maximum_fusion.2), channel_id=1, source_target_pairs={{0,1},{1,0},{2,3},{3,2},{4,5},{5,4},{6,7},{7,6},{8,9},{9,8},{10,11... | collective-permute-start | bytes 294920 | tf_op jit(solution)/shard_map/ppermute | solution.py:515
  4.6 2.5 %collective-permute-start.3 = (bf16[2,192,128]{2,1,0:T(8,128)(2,1)S(1)}, bf16[2,192,128]{2,1,0:T(8,128)(2,1)S(1)}, u32[]{:S(2)}, u32[]{:S(2)}) collective-permute-start(bf16[2,192,128]{2,1,0:T(8,128)(2,1)S(1)} %pad_maximum_fusion.2), channel_id=1, source_target_pairs={{0,3},{1,2},{2,1},{3,0},{4,7},{5,6},{6,5},{7,4},{8,11},{9,10},{10,... | collective-permute-start | bytes 294920 | tf_op jit(solution)/shard_map/ppermute | solution.py:515
  7.0 0.1 collective-permute-start.2
  7.1 0.0 copy-start.2
  7.2 0.0 copy-start.1
  7.2 0.0 copy-start
  7.2 0.7 %copy-done.2 = s32[1024]{0:T(1024)S(1)} copy-done((s32[1024]{0:T(1024)S(1)}, s32[1024]{0:T(1024)}, u32[]{:S(2)}) %copy-start.2) | copy-done | bytes 4120
  7.8 0.1 constant_dynamic-update-slice_fusion
  7.9 0.1 constant_dynamic-update-slice_fusion.9
  8.0 0.1 constant_dynamic-update-slice_fusion.8
  8.1 0.1 constant_dynamic-update-slice_fusion.7
  8.2 0.1 constant_dynamic-update-slice_fusion.6
  8.2 0.1 constant_dynamic-update-slice_fusion.5
  8.3 0.1 constant_dynamic-update-slice_fusion.4
  8.4 0.0 collective-permute-done
  8.4 0.0 copy-done.1
  8.4 0.0 copy-done
  8.4 1.6 %collective-permute-start.1 = (bf16[2,384,128]{2,1,0:T(8,128)(2,1)S(1)}, bf16[2,384,128]{2,1,0:T(8,128)(2,1)S(1)}, u32[]{:S(2)}, u32[]{:S(2)}) collective-permute-start(bf16[2,384,128]{2,1,0:T(8,128)(2,1)S(1)} %pad_maximum_fusion.1.refs_4_), channel_id=1, source_target_pairs={{0,8},{4,20},{8,0},{12,28},{16,24},{20,4},{24,16},{28,12},{1,9},{5... | collective-permute-start | bytes 589832 | tf_op jit(solution)/shard_map/ppermute | solution.py:451
  10.0 1.5 %collective-permute-start.4 = (bf16[2,384,128]{2,1,0:T(8,128)(2,1)S(1)}, bf16[2,384,128]{2,1,0:T(8,128)(2,1)S(1)}, u32[]{:S(2)}, u32[]{:S(2)}) collective-permute-start(bf16[2,384,128]{2,1,0:T(8,128)(2,1)S(1)} %pad_maximum_fusion.1.refs_4_), channel_id=1, source_target_pairs={{0,16},{4,12},{8,24},{12,4},{16,0},{20,28},{24,8},{28,20},{1,17},{... | collective-permute-start | bytes 589832 | tf_op jit(solution)/shard_map/ppermute | solution.py:451
  11.5 0.0 collective-permute-start.5
  11.5 0.1 constant_dynamic-update-slice_fusion.3
  11.6 4.4 %collective-permute-done.2 = bf16[2,192,128]{2,1,0:T(8,128)(2,1)S(1)} collective-permute-done((bf16[2,192,128]{2,1,0:T(8,128)(2,1)S(1)}, bf16[2,192,128]{2,1,0:T(8,128)(2,1)S(1)}, u32[]{:S(2)}, u32[]{:S(2)}) %collective-permute-start.2) | collective-permute-done | bytes 98336 | tf_op jit(solution)/shard_map/ppermute | solution.py:515
  16.0 0.0 collective-permute-done.3
  16.0 0.0 collective-permute-done.1.refs_6_
  16.0 0.0 collective-permute-done.4.refs_8_
  16.0 0.0 collective-permute-done.5.refs_4_
  16.1 1.6 %collective-permute-start.6 = (bf16[2,384,128]{2,1,0:T(8,128)(2,1)S(1)}, bf16[2,384,128]{2,1,0:T(8,128)(2,1)S(1)}, u32[]{:S(2)}, u32[]{:S(2)}) collective-permute-start(bf16[2,384,128]{2,1,0:T(8,128)(2,1)S(1)} %constant_dynamic-update-slice_fusion.1.refs_5_), channel_id=1, source_target_pairs={{0,8},{4,20},{8,0},{12,28},{16,24},{20,4},{24,16},{28,12},{1,9},{5... | collective-permute-start | bytes 589832 | tf_op jit(solution)/shard_map/ppermute | solution.py:451
  17.6 0.2 copy.9.refs_3_
  18.5 0.1 collective-permute-start.8
  18.6 0.6 %shard_map.59 = (bf16[128,768]{1,0:T(8,128)(2,1)S(1)}, bf16[768,128]{1,0:T(8,128)(2,1)S(1)}, f32[1,128]{1,0:T(1,128)S(1)}, f32[1,128]{1,0:T(1,128)S(1)}, f32[128...) custom-call(s32[1]{0:T(128)} %bitcast.refs_0_, ...), custom_call_target="tpu_custom_call" | custom-call | flops 100000000 | bytes 1 | tf_op jit(solution)/shard_map/pallas_call | solution.py:488
  19.2 1.6 %collective-permute-start.9 = (bf16[2,384,128]{2,1,0:T(8,128)(2,1)S(1)}, bf16[2,384,128]{2,1,0:T(8,128)(2,1)S(1)}, u32[]{:S(2)}, u32[]{:S(2)}) collective-permute-start(bf16[2,384,128]{2,1,0:T(8,128)(2,1)S(1)} %constant_dynamic-update-slice_fusion.1.refs_5_), channel_id=1, source_target_pairs={{0,16},{4,12},{8,24},{12,4},{16,0},{20,28},{24,8},{28,20},{1,17},{... | collective-permute-start | bytes 589832 | tf_op jit(solution)/shard_map/ppermute | solution.py:451
  20.8 1.0 %collective-permute-done.6.refs_7_ = bf16[2,384,128]{2,1,0:T(8,128)(2,1)S(1)} collective-permute-done((bf16[2,384,128]{2,1,0:T(8,128)(2,1)S(1)}, bf16[2,384,128]{2,1,0:T(8,128)(2,1)S(1)}, u32[]{:S(2)}, u32[]{:S(2)}) %collective-permute-start.6) | collective-permute-done | bytes 196640 | tf_op jit(solution)/shard_map/ppermute | solution.py:451
  21.8 1.6 %collective-permute-start.7 = (bf16[2,768,128]{2,1,0:T(8,128)(2,1)S(1)}, bf16[2,768,128]{2,1,0:T(8,128)(2,1)S(1)}, u32[]{:S(2)}, u32[]{:S(2)}) collective-permute-start(bf16[2,768,128]{2,1,0:T(8,128)(2,1)S(1)} %pad_maximum_fusion), channel_id=1, source_target_pairs={{0,16},{4,12},{8,24},{12,4},{16,0},{20,28},{24,8},{28,20},{1,17},{... | collective-permute-start | bytes 1179656 | tf_op jit(solution)/shard_map/ppermute | solution.py:451
  23.4 0.0 collective-permute-start.10
  23.4 1.5 %collective-permute-done.9.refs_9_ = bf16[2,384,128]{2,1,0:T(8,128)(2,1)S(1)} collective-permute-done((bf16[2,384,128]{2,1,0:T(8,128)(2,1)S(1)}, bf16[2,384,128]{2,1,0:T(8,128)(2,1)S(1)}, u32[]{:S(2)}, u32[]{:S(2)}) %collective-permute-start.9) | collective-permute-done | bytes 196640 | tf_op jit(solution)/shard_map/ppermute | solution.py:451
  24.9 0.0 collective-permute-start.12
  24.9 0.5 %collective-permute-start.13 = (bf16[2,384,128]{2,1,0:T(8,128)(2,1)S(1)}, bf16[2,384,128]{2,1,0:T(8,128)(2,1)S(1)}, u32[]{:S(2)}, u32[]{:S(2)}) collective-permute-start(bf16[2,384,128]{2,1,0:T(8,128)(2,1)S(1)} %collective-permute-done.9.refs_9_), channel_id=1, source_target_pairs={{0,4},{4,0},{8,12},{12,8},{16,20},{20,16},{24,28},{28,24},{1,5},{5... | collective-permute-start | bytes 589832 | tf_op jit(solution)/shard_map/ppermute | solution.py:454
  25.4 0.0 collective-permute-done.8.refs_5_
  25.4 0.0 collective-permute-start.11
  25.4 0.0 collective-permute-done.10.refs_10_
  25.4 0.9 %collective-permute-done.12.refs_12_ = bf16[2,384,128]{2,1,0:T(8,128)(2,1)S(1)} collective-permute-done((bf16[2,384,128]{2,1,0:T(8,128)(2,1)S(1)}, bf16[2,384,128]{2,1,0:T(8,128)(2,1)S(1)}, u32[]{:S(2)}, u32[]{:S(2)}) %collective-permute-start.12) | collective-permute-done | bytes 196640 | tf_op jit(solution)/shard_map/ppermute | solution.py:454
  26.3 0.3 collective-permute-done.13.refs_13_
  26.6 0.3 collective-permute-done.11.refs_11_
  26.9 2.6 %shard_map.60 = (bf16[640,768]{1,0:T(8,128)(2,1)S(1)}, bf16[768,640]{1,0:T(8,128)(2,1)S(1)}, f32[1,768]{1,0:T(1,128)S(1)}, f32[1,768]{1,0:T(1,128)S(1)}, f32[128,640]{1,0:T(8,128)S(1)}, /*index=5*/f32[128,640]{1,0:T(8,128)S(1)}) custom-call(s32[1]{0:T(128)} %bitcast.refs_0_, f32[1]{0:T(128)} %bitcast.11.refs_1_, s32[1,1024]{1,0:T(1,128)S(1)} %bitcast.16, ...), custom_call_target="tpu_custom_call" | custom-call | flops 1 | bytes 1 | tf_op jit(solution)/shard_map/pallas_call | solution.py:488
  29.6 0.1 collective-permute-done.7.refs_4_
  29.7 0.2 collective-permute-start.14
  29.9 1.2 %shard_map.61 = (bf16[128,768]{1,0:T(8,128)(2,1)S(1)}, bf16[768,128]{1,0:T(8,128)(2,1)S(1)}, f32[1,896]{1,0:T(1,128)S(1)}, f32[1,896]{1,0:T(1,128)S(1)}, f32[128,128]{1,0:T(8,128)S(1)}, /*index=5*/f32[128,128]{1,0:T(8,128)S(1)}) custom-call(s32[1]{0:T(128)} %bitcast.refs_0_, f32[1]{0:T(128)} %bitcast.12.refs_1_, s32[1,1024]{1,0:T(1,128)S(1)} %bitcast.17, ...), custom_call_target="tpu_custom_call" | custom-call | flops 1 | bytes 1 | tf_op jit(solution)/shard_map/pallas_call | solution.py:488
  31.0 0.3 %collective-permute-done.14.refs_4_ = bf16[2,768,128]{2,1,0:T(8,128)(2,1)S(1)} collective-permute-done((bf16[2,768,128]{2,1,0:T(8,128)(2,1)S(1)}, bf16[2,768,128]{2,1,0:T(8,128)(2,1)S(1)}, u32[]{:S(2)}, u32[]{:S(2)}) %collective-permute-start.14) | collective-permute-done | bytes 393248 | tf_op jit(solution)/shard_map/ppermute | solution.py:454
  31.4 3.0 %shard_map.62 = (f32[32,768]{1,0:T(8,128)}, f32[32,768]{1,0:T(8,128)}) custom-call(s32[1]{0:T(128)} %bitcast.refs_0_, f32[1]{0:T(128)} %bitcast.13.refs_1_, s32[1,1024]{1,0:T(1,128)S(1)} %bitcast.18, s32[1024,1]{1,0:T(8,128)S(1)} %copy.9.refs_3_, bf16[2,768,128]{2,1,0:T(8,128)(2,1)S(1)} %collective-permute-done.14.refs_4_, ...), custom_call_target="tpu_custom_call" | custom-call | flops 1 | bytes 1 | tf_op jit(solution)/shard_map/pallas_call | solution.py:488
  (5 shorter events, 0.1 us)
Async XLA Ops:
  1.5 6.9 %collective-permute-start = (bf16[2,192,128]{2,1,0:T(8,128)(2,1)S(1)}, bf16[2,192,128]{2,1,0:T(8,128)(2,1)S(1)}, u32[]{:S(2)}, u32[]{:S(2)}) collective-permute-start(bf16[2,192,128]{2,1,0:T(8,128)(2,1)S(1)} %pad_maximum_fusion.2), channel_id=1, source_target_pairs={{0,1},{1,0},{2,3},{3,2},{4,5},{5,4},{6,7},{7,6},{8,9},{9,8},{10,11... | collective-permute-start | bytes 294920 | tf_op jit(solution)/shard_map/ppermute | solution.py:515
  4.6 11.4 %collective-permute-start.3 = (bf16[2,192,128]{2,1,0:T(8,128)(2,1)S(1)}, bf16[2,192,128]{2,1,0:T(8,128)(2,1)S(1)}, u32[]{:S(2)}, u32[]{:S(2)}) collective-permute-start(bf16[2,192,128]{2,1,0:T(8,128)(2,1)S(1)} %pad_maximum_fusion.2), channel_id=1, source_target_pairs={{0,3},{1,2},{2,1},{3,0},{4,7},{5,6},{6,5},{7,4},{8,11},{9,10},{10,... | collective-permute-start | bytes 294920 | tf_op jit(solution)/shard_map/ppermute | solution.py:515
  7.0 8.9 %collective-permute-start.2 = (bf16[2,192,128]{2,1,0:T(8,128)(2,1)S(1)}, bf16[2,192,128]{2,1,0:T(8,128)(2,1)S(1)}, u32[]{:S(2)}, u32[]{:S(2)}) collective-permute-start(bf16[2,192,128]{2,1,0:T(8,128)(2,1)S(1)} %pad_maximum_fusion.2), channel_id=1, source_target_pairs={{0,2},{1,3},{2,0},{3,1},{4,6},{5,7},{6,4},{7,5},{8,10},{9,11},{10,... | collective-permute-start | bytes 294920 | tf_op jit(solution)/shard_map/ppermute | solution.py:515
  7.1 0.7 %copy-start.2 = (s32[1024]{0:T(1024)S(1)}, s32[1024]{0:T(1024)}, u32[]{:S(2)}) copy-start(s32[1024]{0:T(1024)} %param.6) | copy-start | bytes 12292
  7.2 1.2 %copy-start.1 = (bf16[128,192]{0,1:T(8,128)(2,1)S(1)}, bf16[128,192]{0,1:T(8,128)(2,1)}, u32[]{:S(2)}) copy-start(bf16[128,192]{0,1:T(8,128)(2,1)} %param.4) | copy-start | bytes 147460
  7.2 1.2 %copy-start = (bf16[128,192]{0,1:T(8,128)(2,1)S(1)}, bf16[128,192]{0,1:T(8,128)(2,1)}, u32[]{:S(2)}) copy-start(bf16[128,192]{0,1:T(8,128)(2,1)} %param.5) | copy-start | bytes 147460
  8.4 7.6 %collective-permute-start.1 = (bf16[2,384,128]{2,1,0:T(8,128)(2,1)S(1)}, bf16[2,384,128]{2,1,0:T(8,128)(2,1)S(1)}, u32[]{:S(2)}, u32[]{:S(2)}) collective-permute-start(bf16[2,384,128]{2,1,0:T(8,128)(2,1)S(1)} %pad_maximum_fusion.1.refs_4_), channel_id=1, source_target_pairs={{0,8},{4,20},{8,0},{12,28},{16,24},{20,4},{24,16},{28,12},{1,9},{5... | collective-permute-start | bytes 589832 | tf_op jit(solution)/shard_map/ppermute | solution.py:451
  10.0 6.0 %collective-permute-start.4 = (bf16[2,384,128]{2,1,0:T(8,128)(2,1)S(1)}, bf16[2,384,128]{2,1,0:T(8,128)(2,1)S(1)}, u32[]{:S(2)}, u32[]{:S(2)}) collective-permute-start(bf16[2,384,128]{2,1,0:T(8,128)(2,1)S(1)} %pad_maximum_fusion.1.refs_4_), channel_id=1, source_target_pairs={{0,16},{4,12},{8,24},{12,4},{16,0},{20,28},{24,8},{28,20},{1,17},{... | collective-permute-start | bytes 589832 | tf_op jit(solution)/shard_map/ppermute | solution.py:451
  11.5 4.5 %collective-permute-start.5 = (bf16[2,384,128]{2,1,0:T(8,128)(2,1)S(1)}, bf16[2,384,128]{2,1,0:T(8,128)(2,1)S(1)}, u32[]{:S(2)}, u32[]{:S(2)}) collective-permute-start(bf16[2,384,128]{2,1,0:T(8,128)(2,1)S(1)} %pad_maximum_fusion.1.refs_4_), channel_id=1, source_target_pairs={{0,4},{4,0},{8,12},{12,8},{16,20},{20,16},{24,28},{28,24},{1,5},{5... | collective-permute-start | bytes 589832 | tf_op jit(solution)/shard_map/ppermute | solution.py:454
  16.1 5.7 %collective-permute-start.6 = (bf16[2,384,128]{2,1,0:T(8,128)(2,1)S(1)}, bf16[2,384,128]{2,1,0:T(8,128)(2,1)S(1)}, u32[]{:S(2)}, u32[]{:S(2)}) collective-permute-start(bf16[2,384,128]{2,1,0:T(8,128)(2,1)S(1)} %constant_dynamic-update-slice_fusion.1.refs_5_), channel_id=1, source_target_pairs={{0,8},{4,20},{8,0},{12,28},{16,24},{20,4},{24,16},{28,12},{1,9},{5... | collective-permute-start | bytes 589832 | tf_op jit(solution)/shard_map/ppermute | solution.py:451
  18.5 6.9 %collective-permute-start.8 = (bf16[2,384,128]{2,1,0:T(8,128)(2,1)S(1)}, bf16[2,384,128]{2,1,0:T(8,128)(2,1)S(1)}, u32[]{:S(2)}, u32[]{:S(2)}) collective-permute-start(bf16[2,384,128]{2,1,0:T(8,128)(2,1)S(1)} %constant_dynamic-update-slice_fusion.1.refs_5_), channel_id=1, source_target_pairs={{0,4},{4,0},{8,12},{12,8},{16,20},{20,16},{24,28},{28,24},{1,5},{5... | collective-permute-start | bytes 589832 | tf_op jit(solution)/shard_map/ppermute | solution.py:454
  19.2 5.7 %collective-permute-start.9 = (bf16[2,384,128]{2,1,0:T(8,128)(2,1)S(1)}, bf16[2,384,128]{2,1,0:T(8,128)(2,1)S(1)}, u32[]{:S(2)}, u32[]{:S(2)}) collective-permute-start(bf16[2,384,128]{2,1,0:T(8,128)(2,1)S(1)} %constant_dynamic-update-slice_fusion.1.refs_5_), channel_id=1, source_target_pairs={{0,16},{4,12},{8,24},{12,4},{16,0},{20,28},{24,8},{28,20},{1,17},{... | collective-permute-start | bytes 589832 | tf_op jit(solution)/shard_map/ppermute | solution.py:451
  21.8 7.8 %collective-permute-start.7 = (bf16[2,768,128]{2,1,0:T(8,128)(2,1)S(1)}, bf16[2,768,128]{2,1,0:T(8,128)(2,1)S(1)}, u32[]{:S(2)}, u32[]{:S(2)}) collective-permute-start(bf16[2,768,128]{2,1,0:T(8,128)(2,1)S(1)} %pad_maximum_fusion), channel_id=1, source_target_pairs={{0,16},{4,12},{8,24},{12,4},{16,0},{20,28},{24,8},{28,20},{1,17},{... | collective-permute-start | bytes 1179656 | tf_op jit(solution)/shard_map/ppermute | solution.py:451
  23.4 2.0 %collective-permute-start.10 = (bf16[2,384,128]{2,1,0:T(8,128)(2,1)S(1)}, bf16[2,384,128]{2,1,0:T(8,128)(2,1)S(1)}, u32[]{:S(2)}, u32[]{:S(2)}) collective-permute-start(bf16[2,384,128]{2,1,0:T(8,128)(2,1)S(1)} %collective-permute-done.1.refs_6_), channel_id=1, source_target_pairs={{0,4},{4,0},{8,12},{12,8},{16,20},{20,16},{24,28},{28,24},{1,5},{5... | collective-permute-start | bytes 589832 | tf_op jit(solution)/shard_map/ppermute | solution.py:454
  24.9 1.4 %collective-permute-start.12 = (bf16[2,384,128]{2,1,0:T(8,128)(2,1)S(1)}, bf16[2,384,128]{2,1,0:T(8,128)(2,1)S(1)}, u32[]{:S(2)}, u32[]{:S(2)}) collective-permute-start(bf16[2,384,128]{2,1,0:T(8,128)(2,1)S(1)} %collective-permute-done.4.refs_8_), channel_id=1, source_target_pairs={{0,4},{4,0},{8,12},{12,8},{16,20},{20,16},{24,28},{28,24},{1,5},{5... | collective-permute-start | bytes 589832 | tf_op jit(solution)/shard_map/ppermute | solution.py:454
  24.9 1.7 %collective-permute-start.13 = (bf16[2,384,128]{2,1,0:T(8,128)(2,1)S(1)}, bf16[2,384,128]{2,1,0:T(8,128)(2,1)S(1)}, u32[]{:S(2)}, u32[]{:S(2)}) collective-permute-start(bf16[2,384,128]{2,1,0:T(8,128)(2,1)S(1)} %collective-permute-done.9.refs_9_), channel_id=1, source_target_pairs={{0,4},{4,0},{8,12},{12,8},{16,20},{20,16},{24,28},{28,24},{1,5},{5... | collective-permute-start | bytes 589832 | tf_op jit(solution)/shard_map/ppermute | solution.py:454
  25.4 1.5 %collective-permute-start.11 = (bf16[2,384,128]{2,1,0:T(8,128)(2,1)S(1)}, bf16[2,384,128]{2,1,0:T(8,128)(2,1)S(1)}, u32[]{:S(2)}, u32[]{:S(2)}) collective-permute-start(bf16[2,384,128]{2,1,0:T(8,128)(2,1)S(1)} %collective-permute-done.6.refs_7_), channel_id=1, source_target_pairs={{0,4},{4,0},{8,12},{12,8},{16,20},{20,16},{24,28},{28,24},{1,5},{5... | collective-permute-start | bytes 589832 | tf_op jit(solution)/shard_map/ppermute | solution.py:454
  29.7 1.7 %collective-permute-start.14 = (bf16[2,768,128]{2,1,0:T(8,128)(2,1)S(1)}, bf16[2,768,128]{2,1,0:T(8,128)(2,1)S(1)}, u32[]{:S(2)}, u32[]{:S(2)}) collective-permute-start(bf16[2,768,128]{2,1,0:T(8,128)(2,1)S(1)} %collective-permute-done.7.refs_4_), channel_id=1, source_target_pairs={{0,4},{4,0},{8,12},{12,8},{16,20},{20,16},{24,28},{28,24},{1,5},{5... | collective-permute-start | bytes 1179656 | tf_op jit(solution)/shard_map/ppermute | solution.py:454
